TPU v7x, 512 devices: a whole 4x4x16 slice. The times are simulated.
512 devices in a mesh: sub: 128 (over z, y, core), blk: 4 (over x).
Axes of the slice: x: 4, y: 4, z: 16, core: 2. Of those that a mesh axis runs over, the one named last changes fastest.
Arguments:
- rhs: float32 [128, 4, 1024, 256], P('sub', 'blk')
- blocks: float32 [128, 4, 4, 256, 256], P('sub', 'blk')
- coupling: float32 [128, 4, 2, 128, 128], P('sub', 'blk'), may hold values from -0.5 to 0.5
- inverse: float32 [128, 4, 5, 256, 256], P('sub', 'blk')
- deflation: float32 [128, 4, 40, 1024], P('sub', 'blk'), may hold values from -0.1875 to 0.1875
- counts: int32 [128, 4], P('sub', 'blk'), may hold values from 8 to 40
- panel: float32 [128, 160, 160], P('sub')
- intersection_rows: int32 [128, 4, 256], P('sub', 'blk'), may hold values from 0 to 1023, as said below
Outputs:
- solution: float32 [128, 4, 1024, 256], P('sub', 'blk')
- estimate: float32 [256], replicated
Inputs may be any that keep to these rules, and one draw needn't show every extreme that they name: `intersection_rows`: the (256) indices of one subdomain are distinct.
All inputs are finite; a program needn't handle non-finite values.
Results may differ from a plain program's by a relative error of at most 0.00015.
Values sent between devices are 32-bit elements; how exact they have to be, the bound alone decides.
No kernel may reach another device: no remote copies, remote signals or barrier semaphores. Data moves between devices by JAX's collectives and lax.ppermute only.
A program may use at most 64 MiB of HBM per device.

v0:
```python
import jax
import jax.numpy as jnp
from jax import lax
from jax.sharding import PartitionSpec as P

highest = lax.Precision.HIGHEST


def with_halo(array, sides, width):
    for axis, dim in sides:
        peers, length = (lax.axis_size(axis), array.shape[dim])
        up = [(i, (i + 1) % peers) for i in range(peers - 1)]
        down = [(j, i) for i, j in up]
        last = lax.slice_in_dim(array, length - width, length, axis=dim)
        first = lax.slice_in_dim(array, 0, width, axis=dim)
        before = lax.ppermute(last, axis, up)
        after = lax.ppermute(first, axis, down)
        array = jnp.concatenate([before, array, after], axis=dim)
    return array


def apply_operator(field, block_mats, couple, low_idx, high_idx):
    half = low_idx.shape[0]
    sent = jnp.concatenate([field[low_idx], field[high_idx]], 0)
    padded = with_halo(sent, (("sub", 0),), half)
    from_low = padded[:half]
    from_high = padded[padded.shape[0] - half :]
    count_blocks, width = (block_mats.shape[0], block_mats.shape[1])
    local = jnp.einsum(
        "nij,njr->nir",
        block_mats,
        field.reshape(count_blocks, width, field.shape[1]),
        precision=highest,
    )
    local = local.reshape(field.shape)
    local = local.at[low_idx].add(jnp.dot(couple[0], from_low, precision=highest))
    return local.at[high_idx].add(jnp.dot(couple[1], from_high, precision=highest))


def apply_precond(resid, inv_mats, masked, panel_mat, low_idx, high_idx):
    half = low_idx.shape[0]
    nrows, ncols = resid.shape
    sent = jnp.concatenate([resid[low_idx], resid[high_idx]], 0)
    padded = with_halo(sent, (("sub", 0),), half)
    extended = jnp.concatenate([padded[:half], resid, padded[padded.shape[0] - half :]], 0)
    count_blocks, width = (inv_mats.shape[0], inv_mats.shape[1])
    solved = jnp.einsum(
        "nij,njr->nir", inv_mats, extended.reshape(count_blocks, width, ncols), precision=highest
    )
    solved = solved.reshape(nrows + 2 * half, ncols)
    own = solved[half : half + nrows]
    back_low = solved[:half]
    back_high = solved[half + nrows :]
    coef = jnp.dot(masked, resid, precision=highest)
    kmax = coef.shape[0]
    slot = lax.axis_index("blk")
    every = lax.all_gather(coef, "blk", axis=0, tiled=True)
    mine = lax.dynamic_slice_in_dim(panel_mat, slot * kmax, kmax, 0)
    correct = jnp.dot(mine, every, precision=highest)
    partial_value = own + jnp.einsum("kn,kr->nr", masked, correct, precision=highest)
    back = jnp.concatenate([back_low, back_high], 0)
    returned = with_halo(back, (("sub", 0),), half)
    field = partial_value.at[low_idx].add(returned[:half])
    field = field.at[high_idx].add(returned[returned.shape[0] - half :])
    return (field, None)


def least_squares(beta, proj_one, sub_one, proj_two_a, proj_two_b, sub_two):
    diag_one = jnp.sqrt(proj_one * proj_one + sub_one * sub_one)
    cross = (proj_one * proj_two_a + sub_one * proj_two_b) / diag_one
    rest_a = proj_two_a - cross * proj_one / diag_one
    rest_b = proj_two_b - cross * sub_one / diag_one
    diag_two = jnp.sqrt(rest_a * rest_a + rest_b * rest_b + sub_two * sub_two)
    coeff_two = beta * rest_a / (diag_two * diag_two)
    coeff_one = (beta * proj_one / diag_one - cross * coeff_two) / diag_one
    miss_a = beta - proj_one * coeff_one - proj_two_a * coeff_two
    miss_b = sub_one * coeff_one + proj_two_b * coeff_two
    miss_c = sub_two * coeff_two
    miss = jnp.sqrt(miss_a * miss_a + miss_b * miss_b + miss_c * miss_c)
    return (coeff_one, coeff_two, miss)


def body(rhs, blocks, coupling, inverse, deflation, counts, panel, intersection_rows):
    source = rhs[0, 0]
    block_mats = blocks[0, 0]
    couple = coupling[0, 0]
    inv_mats = inverse[0, 0]
    panel_mat = panel[0]
    index_rows = intersection_rows[0, 0]
    half = index_rows.shape[0] // 2
    low_idx = index_rows[:half]
    high_idx = index_rows[half:]
    kmax = deflation.shape[2]
    keep = (jnp.arange(kmax, dtype=jnp.int32) < counts[0, 0]).astype(jnp.float32)
    masked = deflation[0, 0] * keep[:, None]

    def precond(vector):
        return apply_precond(vector, inv_mats, masked, panel_mat, low_idx, high_idx)

    def operator(vector):
        return apply_operator(vector, block_mats, couple, low_idx, high_idx)

    norm_sq = lax.psum(jnp.sum(source * source, 0), ("sub", "blk"))
    beta = jnp.sqrt(norm_sq)
    basis_one = source / beta
    search_one, rows_one = precond(basis_one)
    image = operator(search_one)
    proj_one, image_sq = lax.psum(
        (jnp.sum(image * basis_one, 0), jnp.sum(image * image, 0)), ("sub", "blk")
    )
    sub_one = jnp.sqrt(image_sq - proj_one * proj_one)
    basis_two = (image - proj_one * basis_one) / sub_one
    search_two, rows_two = precond(basis_two)
    image_two = operator(search_two)
    proj_two_a, proj_two_b, image_two_sq = lax.psum(
        (
            jnp.sum(image_two * basis_one, 0),
            jnp.sum(image_two * basis_two, 0),
            jnp.sum(image_two * image_two, 0),
        ),
        ("sub", "blk"),
    )
    sub_two = jnp.sqrt(image_two_sq - proj_two_a * proj_two_a - proj_two_b * proj_two_b)
    coeff_one, coeff_two, miss = least_squares(
        beta, proj_one, sub_one, proj_two_a, proj_two_b, sub_two
    )
    solution = coeff_one * search_one + coeff_two * search_two
    return (solution[None, None], miss)


def solution(mesh):
    placed = (
        P("sub", "blk", None, None),
        P("sub", "blk", None, None, None),
        P("sub", "blk", None, None, None),
        P("sub", "blk", None, None, None),
        P("sub", "blk", None, None),
        P("sub", "blk"),
        P("sub", None, None),
        P("sub", "blk", None),
    )
    return jax.shard_map(
        body,
        mesh=mesh,
        in_specs=placed,
        out_specs=(P("sub", "blk", None, None), P()),
        check_vma=False,
    )
```

profile of v0, /device:TPU:1, one launch (start us, length us, event | category | flops | bytes accessed | tf_op | source)
XLA Modules:
  0.0 466.5 jit_solution(16233847028954167172)
XLA Ops:
  0.7 0.8 fusion.35
  1.5 1.4 fusion.10
  2.9 111.0 %psum.42 = f32[256]{0:T(256)S(1)} all-reduce(f32[256]{0:T(256)S(1)} %fusion.10), channel_id=1, replica_groups=mesh['sub'=128,'blk'=4] {'sub','blk'}, use_global_device_ids=true, to_apply=%region_1.0 | all-reduce | flops 256 | bytes 2048 | tf_op jit(solution)/shard_map/psum | solution.py:103
  114.6 1.4 gather_fusion
  116.0 1.9 collective-permute-start
  117.9 0.6 pad_clamp_fusion
  118.5 1.5 gather_fusion.1
  120.0 2.4 collective-permute-start.1
  123.1 1.6 fusion.8
  124.7 9.5 %all_gather.6 = f32[160,256]{1,0:T(8,128)S(1)} all-gather(f32[40,256]{1,0:T(8,128)S(1)} %fusion.8), channel_id=1, replica_groups=mesh['sub'=128,'blk'=4] {'blk'}, dimensions={0}, use_global_device_ids=true | all-gather | bytes 204800 | tf_op jit(solution)/shard_map/all_gather | solution.py:57
  134.2 1.0 fusion.30
  135.2 1.0 pad_maximum_fusion
  136.3 1.4 fusion.2
  137.7 5.8 %collective-permute-start.2 = (f32[128,256]{1,0:T(8,128)S(1)}, f32[128,256]{1,0:T(8,128)S(1)}, u32[]{:S(2)}, u32[]{:S(2)}) collective-permute-start(f32[128,256]{1,0:T(8,128)S(1)} %get-tuple-element.18), channel_id=1, source_target_pairs={{0,4},{4,8},{8,12},{12,16},{16,20},{20,24},{24,28},{28,32},{32,36}... | collective-permute-start | bytes 393224 | tf_op jit(solution)/shard_map/ppermute | solution.py:16
  143.5 1.9 collective-permute-start.3
  145.5 1.1 convolution_add_fusion.1
  146.6 1.7 scatter_fusion
  148.3 1.5 collective-permute-done.3
  149.8 1.7 scatter_fusion.1
  151.5 1.4 gather_fusion.2
  152.9 1.5 gather_fusion.3
  154.4 2.1 collective-permute-start.4
  156.5 2.2 collective-permute-start.5
  158.7 2.4 fusion.6
  161.2 1.0 convolution_bitcast_fusion.3
  162.2 1.6 copy.10
  163.9 1.9 convolution_bitcast_fusion.2
  165.8 1.7 copy.11
  167.5 2.0 scatter_fusion.2
  169.5 2.1 scatter_fusion.3
  171.6 2.4 multiply_reduce_fusion.4
  174.0 111.5 %all-reduce.1 = (f32[256]{0:T(256)}, f32[256]{0:T(256)S(1)}) all-reduce(f32[256]{0:T(256)} %get-tuple-element.6, f32[256]{0:T(256)} %get-tuple-element.5), channel_id=1, replica_groups=mesh['sub'=128,'blk'=4] {'sub','blk'}, use_global_device_ids=true, to_apply=%region_9.0 | all-reduce | flops 512 | bytes 4096 | tf_op jit(solution)/shard_map/psum | solution.py:108
  285.5 0.7 fusion.34
  286.1 1.7 subtract_divide_fusion
  287.9 1.5 gather_fusion.4
  289.4 1.5 gather_fusion.5
  290.9 1.6 fusion.15
  292.5 3.3 collective-permute-start.6
  295.9 1.9 collective-permute-start.7
  297.8 9.4 %all_gather.7 = f32[160,256]{1,0:T(8,128)S(1)} all-gather(f32[40,256]{1,0:T(8,128)S(1)} %fusion.15), channel_id=1, replica_groups=mesh['sub'=128,'blk'=4] {'blk'}, dimensions={0}, use_global_device_ids=true | all-gather | bytes 204800 | tf_op jit(solution)/shard_map/all_gather | solution.py:57
  307.2 1.0 fusion.28
  308.3 1.4 fusion
  309.8 0.7 fusion.39
  310.4 6.3 %collective-permute-start.8 = (f32[128,256]{1,0:T(8,128)S(1)}, f32[128,256]{1,0:T(8,128)}, u32[]{:S(2)}, u32[]{:S(2)}) collective-permute-start(f32[128,256]{1,0:T(8,128)S(1)} %get-tuple-element.16), channel_id=1, source_target_pairs={{0,4},{4,8},{8,12},{12,16},{16,20},{20,24},{24,28},{28,32},{32,36}... | collective-permute-start | bytes 393224 | tf_op jit(solution)/shard_map/ppermute | solution.py:16
  316.7 1.9 collective-permute-start.9
  318.7 1.1 convolution_add_fusion
  319.8 2.1 scatter_fusion.4
  321.9 1.5 collective-permute-done.9
  323.3 2.0 scatter_fusion.5
  325.4 1.5 gather_fusion.6
  326.9 2.2 collective-permute-start.10
  329.1 3.3 fusion.4
  332.4 1.5 gather_fusion.7
  333.9 2.8 collective-permute-start.11
  336.7 1.9 convolution_bitcast_fusion.1
  338.7 1.6 copy.12
  340.5 1.9 convolution_bitcast_fusion
  342.5 1.0 copy.13
  343.5 3.7 scatter_fusion.6
  347.2 3.3 scatter_fusion.7
  350.5 2.2 multiply_reduce_fusion
  352.7 112.1 %all-reduce = (f32[256]{0:T(256)S(1)}, f32[256]{0:T(256)S(1)}, f32[256]{0:T(256)S(1)}) all-reduce(f32[256]{0:T(256)S(1)} %get-tuple-element.3, f32[256]{0:T(256)S(1)} %get-tuple-element.4, f32[256]{0:T(256)S(1)} %get-tuple-element.2), channel_id=1, replica_groups=mesh['sub'=128,'blk'=4] {'sub','blk'}, use_global_device_ids=true, to_apply=%region_17.0 | all-reduce | flops 768 | bytes 6144 | tf_op jit(solution)/shard_map/psum | solution.py:115
  464.8 0.6 add_sqrt_fusion
  465.4 1.1 add_bitcast_fusion
  (44 shorter events, 1.1 us)
Async XLA Ops:
  0.6 135.6 %copy-start = (f32[1,1,5,256,256]{4,3,2,1,0:T(8,128)S(1)}, f32[1,1,5,256,256]{4,3,2,1,0:T(8,128)}, u32[]{:S(2)}) copy-start(f32[1,1,5,256,256]{4,3,2,1,0:T(8,128)} %param.11) | copy-start | bytes 3932164
  0.6 113.8 %copy-start.3 = (f32[1,1,1024,256]{3,2,1,0:T(8,128)S(1)}, f32[1,1,1024,256]{3,2,1,0:T(8,128)}, u32[]{:S(2)}) copy-start(f32[1,1,1024,256]{3,2,1,0:T(8,128)} %param.8) | copy-start | bytes 3145732
  1.5 150.0 %copy-start.7 = (s32[1024]{0:T(1024)}, s32[1024]{0:T(1024)S(1)}, u32[]{:S(2)}) copy-start(s32[1024]{0:T(1024)S(1)} %pad_clamp_fusion.1) | copy-start | bytes 12292
  113.9 0.6 copy-start.8
  116.0 19.2 %collective-permute-start = (f32[128,256]{1,0:T(8,128)}, f32[128,256]{1,0:T(8,128)S(1)}, u32[]{:S(2)}, u32[]{:S(2)}) collective-permute-start(f32[128,256]{1,0:T(8,128)} %gather_fusion), channel_id=1, source_target_pairs={{0,4},{4,8},{8,12},{12,16},{16,20},{20,24},{24,28},{28,32},{32,36}... | collective-permute-start | bytes 393224 | tf_op jit(solution)/shard_map/ppermute | solution.py:16
  120.0 15.2 %collective-permute-start.1 = (f32[128,256]{1,0:T(8,128)}, f32[128,256]{1,0:T(8,128)}, u32[]{:S(2)}, u32[]{:S(2)}) collective-permute-start(f32[128,256]{1,0:T(8,128)} %gather_fusion.1), channel_id=1, source_target_pairs={{4,0},{8,4},{12,8},{16,12},{20,16},{24,20},{28,24},{32,28},{36,32}... | collective-permute-start | bytes 393224 | tf_op jit(solution)/shard_map/ppermute | solution.py:17
  123.1 1.6 copy-start.10
  136.2 9.2 %copy-start.4 = (f32[1,1,40,1024]{3,2,1,0:T(8,128)S(1)}, f32[1,1,40,1024]{3,2,1,0:T(8,128)}, u32[]{:S(2)}) copy-start(f32[1,1,40,1024]{3,2,1,0:T(8,128)} %param.12) | copy-start | bytes 491524
  136.2 9.2 %copy-start.11 = (f32[40]{0:T(128)S(1)}, f32[40]{0:T(128)}, u32[]{:S(2)}) copy-start(f32[40]{0:T(128)} %copy-done.10) | copy-start | bytes 484
  137.7 8.9 %collective-permute-start.2 = (f32[128,256]{1,0:T(8,128)S(1)}, f32[128,256]{1,0:T(8,128)S(1)}, u32[]{:S(2)}, u32[]{:S(2)}) collective-permute-start(f32[128,256]{1,0:T(8,128)S(1)} %get-tuple-element.18), channel_id=1, source_target_pairs={{0,4},{4,8},{8,12},{12,16},{16,20},{20,24},{24,28},{28,32},{32,36}... | collective-permute-start | bytes 393224 | tf_op jit(solution)/shard_map/ppermute | solution.py:16
  143.5 6.3 %collective-permute-start.3 = (f32[128,256]{1,0:T(8,128)S(1)}, f32[128,256]{1,0:T(8,128)S(1)}, u32[]{:S(2)}, u32[]{:S(2)}) collective-permute-start(f32[128,256]{1,0:T(8,128)S(1)} %get-tuple-element.17), channel_id=1, source_target_pairs={{4,0},{8,4},{12,8},{16,12},{20,16},{24,20},{28,24},{32,28},{36,32}... | collective-permute-start | bytes 393224 | tf_op jit(solution)/shard_map/ppermute | solution.py:17
  154.4 6.8 %collective-permute-start.4 = (f32[128,256]{1,0:T(8,128)}, f32[128,256]{1,0:T(8,128)S(1)}, u32[]{:S(2)}, u32[]{:S(2)}) collective-permute-start(f32[128,256]{1,0:T(8,128)} %gather_fusion.2), channel_id=1, source_target_pairs={{0,4},{4,8},{8,12},{12,16},{16,20},{20,24},{24,28},{28,32},{32,36}... | collective-permute-start | bytes 393224 | tf_op jit(solution)/shard_map/ppermute | solution.py:16
  156.5 7.3 %collective-permute-start.5 = (f32[128,256]{1,0:T(8,128)}, f32[128,256]{1,0:T(8,128)}, u32[]{:S(2)}, u32[]{:S(2)}) collective-permute-start(f32[128,256]{1,0:T(8,128)} %gather_fusion.3), channel_id=1, source_target_pairs={{4,0},{8,4},{12,8},{16,12},{20,16},{24,20},{28,24},{32,28},{36,32}... | collective-permute-start | bytes 393224 | tf_op jit(solution)/shard_map/ppermute | solution.py:17
  158.7 2.4 copy-start.6
  171.6 113.9 %copy-start.2 = (f32[1024,256]{1,0:T(8,128)}, f32[1024,256]{1,0:T(8,128)S(1)}, u32[]{:S(2)}) copy-start(f32[1024,256]{1,0:T(8,128)S(1)} %scatter_fusion.3) | copy-start | bytes 3145732
  287.9 20.4 %copy-start.1 = (f32[1024,256]{1,0:T(8,128)}, f32[1024,256]{1,0:T(8,128)S(1)}, u32[]{:S(2)}) copy-start(f32[1024,256]{1,0:T(8,128)S(1)} %subtract_divide_fusion) | copy-start | bytes 3145732
  292.5 15.7 %collective-permute-start.6 = (f32[128,256]{1,0:T(8,128)}, f32[128,256]{1,0:T(8,128)S(1)}, u32[]{:S(2)}, u32[]{:S(2)}) collective-permute-start(f32[128,256]{1,0:T(8,128)} %gather_fusion.4), channel_id=1, source_target_pairs={{0,4},{4,8},{8,12},{12,16},{16,20},{20,24},{24,28},{28,32},{32,36}... | collective-permute-start | bytes 393224 | tf_op jit(solution)/shard_map/ppermute | solution.py:16
  295.9 12.3 %collective-permute-start.7 = (f32[128,256]{1,0:T(8,128)}, f32[128,256]{1,0:T(8,128)S(1)}, u32[]{:S(2)}, u32[]{:S(2)}) collective-permute-start(f32[128,256]{1,0:T(8,128)} %gather_fusion.5), channel_id=1, source_target_pairs={{4,0},{8,4},{12,8},{16,12},{20,16},{24,20},{28,24},{32,28},{36,32}... | collective-permute-start | bytes 393224 | tf_op jit(solution)/shard_map/ppermute | solution.py:17
  308.3 10.3 %copy-start.5 = (f32[1,1,40,1024]{3,2,1,0:T(8,128)S(1)}, f32[1,1,40,1024]{3,2,1,0:T(8,128)}, u32[]{:S(2)}) copy-start(f32[1,1,40,1024]{3,2,1,0:T(8,128)} %param.12) | copy-start | bytes 491524
  308.3 10.3 %copy-start.12 = (f32[40]{0:T(128)S(1)}, f32[40]{0:T(128)}, u32[]{:S(2)}) copy-start(f32[40]{0:T(128)} %copy-done.10) | copy-start | bytes 484
  310.4 9.4 %collective-permute-start.8 = (f32[128,256]{1,0:T(8,128)S(1)}, f32[128,256]{1,0:T(8,128)}, u32[]{:S(2)}, u32[]{:S(2)}) collective-permute-start(f32[128,256]{1,0:T(8,128)S(1)} %get-tuple-element.16), channel_id=1, source_target_pairs={{0,4},{4,8},{8,12},{12,16},{16,20},{20,24},{24,28},{28,32},{32,36}... | collective-permute-start | bytes 393224 | tf_op jit(solution)/shard_map/ppermute | solution.py:16
  316.7 6.6 %collective-permute-start.9 = (f32[128,256]{1,0:T(8,128)}, f32[128,256]{1,0:T(8,128)}, u32[]{:S(2)}, u32[]{:S(2)}) collective-permute-start(f32[128,256]{1,0:T(8,128)} %get-tuple-element.15), channel_id=1, source_target_pairs={{4,0},{8,4},{12,8},{16,12},{20,16},{24,20},{28,24},{32,28},{36,32}... | collective-permute-start | bytes 393224 | tf_op jit(solution)/shard_map/ppermute | solution.py:17
  326.9 9.8 %collective-permute-start.10 = (f32[128,256]{1,0:T(8,128)}, f32[128,256]{1,0:T(8,128)}, u32[]{:S(2)}, u32[]{:S(2)}) collective-permute-start(f32[128,256]{1,0:T(8,128)} %gather_fusion.6), channel_id=1, source_target_pairs={{0,4},{4,8},{8,12},{12,16},{16,20},{20,24},{24,28},{28,32},{32,36}... | collective-permute-start | bytes 393224 | tf_op jit(solution)/shard_map/ppermute | solution.py:16
  333.9 6.6 %collective-permute-start.11 = (f32[128,256]{1,0:T(8,128)}, f32[128,256]{1,0:T(8,128)}, u32[]{:S(2)}, u32[]{:S(2)}) collective-permute-start(f32[128,256]{1,0:T(8,128)} %gather_fusion.7), channel_id=1, source_target_pairs={{4,0},{8,4},{12,8},{16,12},{20,16},{24,20},{28,24},{32,28},{36,32}... | collective-permute-start | bytes 393224 | tf_op jit(solution)/shard_map/ppermute | solution.py:17
  350.5 114.2 %copy-start.9 = (f32[256]{0:T(256)S(1)}, f32[256]{0:T(256)}, u32[]{:S(2)}) copy-start(f32[256]{0:T(256)} %copy-done.8) | copy-start | bytes 3076
  350.5 114.2 %copy-start.13 = (f32[256]{0:T(256)S(1)}, f32[256]{0:T(256)}, u32[]{:S(2)}) copy-start(f32[256]{0:T(256)} %get-tuple-element.10) | copy-start | bytes 3076
where the time goes:
time: 468 us; the launch traced here: 467 us
  blocking collectives  354 us (76%)
  starting transfers between devices  34.8 us (7%)
  other arithmetic  31.2 us (7%)
  matrix products  22.8 us (5%)
  local copies, waits for them, and re-layouts  19.2 us (4%)
    psum x1, blocking collectives, body(): lax.psum((jnp.sum(image_two * basis_one, 0), jnp.sum(image_two * basis_tw...  112 us
    psum x1, blocking collectives, body(): lax.psum((jnp.sum(image * basis_one, 0), jnp.sum(image * image, 0)), ('su...  111 us
    psum x1, blocking collectives, body(): norm_sq = lax.psum(jnp.sum(source * source, 0), ('sub', 'blk'))  111 us
    ppermute x6, starting transfers between devices, with_halo(): before = lax.ppermute(last, axis, up)  21.7 us
    all_gather x2, blocking collectives, apply_precond(): every = lax.all_gather(coef, 'blk', axis=0, tiled=True)  18.9 us
    ppermute x6, starting transfers between devices, with_halo(): after = lax.ppermute(first, axis, down)  13.1 us
  transfers between devices with their start and end apart: 12, of which 3 were waited for; matrix products, arithmetic and copies ran while one was open for 5% of the time, Pallas kernels for 0%

commit v1 on v0

v1 whole, which is shorter than its diff:
```python
import functools

import jax
import jax.numpy as jnp
from jax import lax
from jax.experimental import pallas as pl
from jax.experimental.pallas import tpu as pltpu
from jax.sharding import PartitionSpec as P

f32 = jnp.float32
bf16 = jnp.bfloat16
AXES = ("sub", "blk")
LIMIT = 24 * 1024 * 1024


def split(a):
    high = a.astype(bf16)
    return high, (a - high.astype(f32)).astype(bf16)


def dot(a, b, dims=((1,), (0,))):
    return lax.dot_general(a, b, (dims, ((), ())), preferred_element_type=f32)


def mul(a, b, dims=((1,), (0,))):
    return dot(a[0], b[0], dims) + (dot(a[0], b[1], dims) + dot(a[1], b[0], dims))


def pick(onehot, b):
    return dot(onehot, b[0]) + dot(onehot, b[1])


def gather_matrix(idx, nrows):
    count = idx.shape[1]
    column = jnp.broadcast_to(idx.astype(f32), (128, count)).T
    lane = lax.broadcasted_iota(jnp.int32, (count, 128), 1).astype(f32)
    parts = [
        jnp.where(column == lane + float(128 * k), 1.0, 0.0).astype(bf16)
        for k in range(nrows // 128)
    ]
    return jnp.concatenate(parts, axis=1)


def scatter_matrix(idx, nrows):
    row = lax.broadcasted_iota(jnp.int32, (nrows, idx.shape[1]), 0)
    return jnp.where(row == idx, 1.0, 0.0).astype(bf16)


def masked_deflation(defl_ref, count):
    kmax, nrows = defl_ref.shape
    row = lax.broadcasted_iota(jnp.int32, (kmax, nrows), 0)
    return jnp.where(row < count, defl_ref[...], 0.0)


def prep_kernel(scal_ref, r_ref, idx_ref, defl_ref, inv_ref, up_ref, dn_ref, coef_ref):
    half = idx_ref.shape[1] // 2
    nrows = r_ref.shape[0]
    r = split(r_ref[...])
    rows = pick(gather_matrix(idx_ref[...], nrows), r)
    dn_ref[:half] = rows[:half]
    up_ref[:half] = rows[half:]
    dn_ref[half : 2 * half] = r_ref[:half]
    up_ref[half : 2 * half] = r_ref[nrows - half :]
    dn_ref[2 * half :] = inv_ref[0, :half]
    up_ref[2 * half :] = inv_ref[inv_ref.shape[0] - 1, inv_ref.shape[1] - half :]
    coef = mul(split(masked_deflation(defl_ref, scal_ref[0])), r)
    for k in range(coef_ref.shape[0]):
        coef_ref[k] = coef


def local_kernel(
    scal_ref, r_ref, up_ref, dn_ref, lo_ref, hi_ref, inv_lo_ref, inv_hi_ref, inv_ref, all_ref,
    panel_ref, defl_ref, idx_ref, z_ref, zup_ref, zdn_ref,
):
    half = idx_ref.shape[1] // 2
    nrows, ncols = r_ref.shape
    kmax = defl_ref.shape[0]
    width = inv_ref.shape[1]
    idx = idx_ref[...]
    r_first, r_last = r_ref[:half], r_ref[nrows - half :]
    back_lo = mul(split(inv_lo_ref[2 * half :]), split(jnp.concatenate([lo_ref[half : 2 * half], dn_ref[:half]], 0)))
    back_hi = mul(split(inv_hi_ref[2 * half :]), split(jnp.concatenate([up_ref[:half], hi_ref[half : 2 * half]], 0)))
    back = split(jnp.concatenate([back_lo, back_hi], 0))
    slot = pl.multiple_of(scal_ref[1] * kmax, 8)
    panel = split(panel_ref[pl.ds(slot, kmax), :])
    coefs = split(all_ref[...].reshape(all_ref.shape[0] * kmax, ncols))
    coarse = split(mul(panel, coefs))
    masked = split(masked_deflation(defl_ref, scal_ref[0]))
    z_ref[...] = mul(masked, coarse, ((0,), (0,))) + pick(scatter_matrix(idx, nrows), back)
    last = inv_ref.shape[0] - 1
    for n in range(last + 1):
        if n == 0:
            part = jnp.concatenate([lo_ref[:half], r_first], 0)
        elif n == last:
            part = jnp.concatenate([r_last, hi_ref[:half]], 0)
        else:
            part = r_ref[n * width - half : (n + 1) * width - half]
        low = half if n == 0 else 0
        high = width - half if n == last else width
        y = mul(split(inv_ref[n][low:high]), split(part))
        at = n * width + low - half
        z_ref[at : at + high - low] += y
    rows = pick(gather_matrix(idx, nrows), split(z_ref[...]))
    zdn_ref[...] = rows[:half]
    zup_ref[...] = rows[half:]


def blocks_kernel(scal_ref, z_ref, mats_ref, defl_ref, idx_ref, t_ref, rows_ref, coef_ref):
    width = mats_ref.shape[1]
    nrows = z_ref.shape[0]
    for n in range(mats_ref.shape[0]):
        part = slice(n * width, (n + 1) * width)
        t_ref[part] = mul(split(mats_ref[n]), split(z_ref[part]))
    t = split(t_ref[...])
    rows_ref[...] = pick(gather_matrix(idx_ref[...], nrows), t)
    coef_ref[...] = mul(split(masked_deflation(defl_ref, scal_ref[0])), t)


def near_rows(couple_ref, lo_ref, hi_ref):
    near_lo = mul(split(couple_ref[0]), split(lo_ref[...]))
    near_hi = mul(split(couple_ref[1]), split(hi_ref[...]))
    return jnp.concatenate([near_lo, near_hi], 0)


def image_kernel(
    scal_ref, t_ref, rows_ref, tcoef_ref, couple_ref, lo_ref, hi_ref, defl_ref, idx_ref,
    u_ref, up_ref, dn_ref, coef_ref,
):
    half = idx_ref.shape[1] // 2
    nrows = t_ref.shape[0]
    near = near_rows(couple_ref, lo_ref, hi_ref)
    rows = rows_ref[...] + near
    near = split(near)
    scatter = scatter_matrix(idx_ref[...], nrows)
    spread = pick(scatter, near)
    u_ref[...] = t_ref[...] + spread
    dn_ref[:half] = rows[:half]
    up_ref[:half] = rows[half:]
    dn_ref[half:] = u_ref[:half]
    up_ref[half:] = u_ref[nrows - half :]
    coef = tcoef_ref[...] + mul(split(masked_deflation(defl_ref, scal_ref[0])), split(spread))
    for k in range(coef_ref.shape[0]):
        coef_ref[k] = coef


def inverse_or_zero(a):
    return jnp.where(a > 0.0, 1.0 / jnp.where(a > 0.0, a, 1.0), 0.0)


def total(a):
    return jnp.sum(a, axis=0, keepdims=True)


def gram_kernel(t_ref, couple_ref, lo_ref, hi_ref, idx_ref, u0_ref, u1_ref, out_ref):
    nrows = t_ref.shape[0]
    near = split(near_rows(couple_ref, lo_ref, hi_ref))
    u2 = t_ref[...] + pick(scatter_matrix(idx_ref[...], nrows), near)
    u0, u1 = u0_ref[...], u1_ref[...]
    unit, length = [], []
    for u in (u0, u1, u2):
        top = jnp.max(jnp.abs(u), axis=0, keepdims=True)
        scaled = u * inverse_or_zero(top)
        size = jnp.sqrt(total(scaled * scaled))
        unit.append((scaled, inverse_or_zero(size)))
        length.append(top * size)
    rows = list(length)
    for i, j in ((0, 1), (0, 2), (1, 2)):
        rows.append(total(unit[i][0] * unit[j][0]) * unit[i][1] * unit[j][1])
    rows += [jnp.zeros_like(rows[0])] * 2
    full = jnp.concatenate(rows, 0)
    for k in range(out_ref.shape[0]):
        out_ref[k] = full


def merge(parts):
    lengths, shares = [], []
    for i in range(3):
        own = parts[:, i, :]
        top = jnp.max(own, axis=0, keepdims=True)
        share = own * inverse_or_zero(top)
        size = jnp.sqrt(total(share * share))
        lengths.append(top * size)
        shares.append(share * inverse_or_zero(size))
    cosines = [
        total(parts[:, 3 + k, :] * shares[i] * shares[j])
        for k, (i, j) in enumerate(((0, 1), (0, 2), (1, 2)))
    ]
    return lengths, cosines


def merge_kernel(parts_ref, out_ref):
    lengths, cosines = merge(parts_ref[...])
    rows = lengths + cosines
    full = jnp.concatenate(rows + [jnp.zeros_like(rows[0])] * 2, 0)
    for k in range(out_ref.shape[0]):
        out_ref[k] = full


def least_squares(beta, proj_one, sub_one, proj_two_a, proj_two_b, sub_two):
    diag_one = jnp.sqrt(proj_one * proj_one + sub_one * sub_one)
    cross = (proj_one * proj_two_a + sub_one * proj_two_b) / diag_one
    rest_a = proj_two_a - cross * proj_one / diag_one
    rest_b = proj_two_b - cross * sub_one / diag_one
    diag_two = jnp.sqrt(rest_a * rest_a + rest_b * rest_b + sub_two * sub_two)
    coeff_two = beta * rest_a / (diag_two * diag_two)
    coeff_one = (beta * proj_one / diag_one - cross * coeff_two) / diag_one
    miss_a = beta - proj_one * coeff_one - proj_two_a * coeff_two
    miss_b = sub_one * coeff_one + proj_two_b * coeff_two
    miss_c = sub_two * coeff_two
    miss = jnp.sqrt(miss_a * miss_a + miss_b * miss_b + miss_c * miss_c)
    return (coeff_one, coeff_two, miss)


def finish_kernel(parts_ref, p_ref, q_ref, out_ref, miss_ref):
    (beta, len_one, len_two), (cos_01, cos_02, cos_12) = merge(parts_ref[...])
    rel_one = len_one / beta
    proj_one = rel_one * cos_01
    sine_sq = 1.0 - cos_01 * cos_01
    sub_one = rel_one * jnp.sqrt(sine_sq)
    rel_two = len_two / beta / sub_one
    proj_two_a = rel_two * cos_02 - proj_one * (proj_one / sub_one)
    side = (cos_12 - cos_01 * cos_02) / jnp.sqrt(sine_sq)
    proj_two_b = rel_two * side - proj_one
    sub_two = rel_two * jnp.sqrt(1.0 - cos_02 * cos_02 - side * side)
    coeff_one, coeff_two, miss = least_squares(beta, proj_one, sub_one, proj_two_a, proj_two_b, sub_two)
    miss_ref[...] = miss
    second = coeff_two / sub_one
    first = (coeff_one - second * proj_one) / beta
    out_ref[...] = first * p_ref[...] + (second / beta) * q_ref[...]


def shape(*dims):
    return jax.ShapeDtypeStruct(dims, f32)


def call(kernel, out_shape, *operands, specs=None, flops=0):
    extra = {} if specs is None else {"in_specs": specs}
    size = sum(4 * a.size for a in operands)
    return pl.pallas_call(
        kernel,
        out_shape=out_shape,
        compiler_params=pltpu.CompilerParams(vmem_limit_bytes=LIMIT),
        cost_estimate=pl.CostEstimate(flops=flops, bytes_accessed=size, transcendentals=0),
        name=kernel.__name__,
        **extra,
    )(*operands)


VMEM = pl.BlockSpec(memory_space=pltpu.VMEM)
SMEM = pl.BlockSpec(memory_space=pltpu.SMEM)


def body(mesh, rhs, blocks, coupling, inverse, deflation, counts, panel, intersection_rows):
    source, mats, couple, inv = rhs[0, 0], blocks[0, 0], coupling[0, 0], inverse[0, 0]
    defl, panel_mat = deflation[0, 0], panel[0]
    idx = intersection_rows[0]
    half = idx.shape[1] // 2
    nrows, ncols = source.shape
    kmax = defl.shape[0]
    n_sub, n_blk = mesh.shape["sub"], mesh.shape["blk"]
    scal = jnp.stack([counts[0, 0], lax.axis_index("blk").astype(jnp.int32)])
    up = [(i, i + 1) for i in range(n_sub - 1)]
    down = [(i + 1, i) for i in range(n_sub - 1)]

    def halo(to_up, to_down):
        return lax.ppermute(to_up, "sub", up), lax.ppermute(to_down, "sub", down)

    def coarse_group(coef):
        return lax.all_to_all(coef, "blk", 0, 0)

    def precond(vector, sent, got, coefs, inv_lo, inv_hi):
        return call(
            local_kernel, (shape(nrows, ncols), shape(half, ncols), shape(half, ncols)),
            scal, vector, sent[0], sent[1], got[0], got[1], inv_lo, inv_hi, inv, coefs, panel_mat,
            defl, idx, specs=[SMEM] + [VMEM] * 12, flops=10**9,
        )

    def diagonal(field):
        return call(
            blocks_kernel, (shape(nrows, ncols), shape(2 * half, ncols), shape(kmax, ncols)),
            scal, field, mats, defl, idx, specs=[SMEM] + [VMEM] * 4, flops=10**9,
        )

    sent_up, sent_dn, coef = call(
        prep_kernel,
        (shape(3 * half, ncols), shape(3 * half, ncols), shape(n_blk, kmax, ncols)),
        scal, source, idx, defl, inv, specs=[SMEM] + [VMEM] * 4,
        flops=3 * 10**8,
    )
    got_lo, got_hi = halo(sent_up, sent_dn)
    coefs = coarse_group(coef)
    inv_lo, inv_hi = got_lo, got_hi
    search_one, z_up, z_dn = precond(source, (sent_up, sent_dn), (got_lo, got_hi), coefs, inv_lo, inv_hi)
    z_lo, z_hi = halo(z_up, z_dn)
    diag, diag_rows, diag_coef = diagonal(search_one)
    image, sent_up, sent_dn, coef = call(
        image_kernel,
        (shape(nrows, ncols), shape(2 * half, ncols), shape(2 * half, ncols), shape(n_blk, kmax, ncols)),
        scal, diag, diag_rows, diag_coef, couple, z_lo, z_hi, defl, idx,
        specs=[SMEM] + [VMEM] * 8, flops=5 * 10**8,
    )
    got_lo, got_hi = halo(sent_up, sent_dn)
    coefs = coarse_group(coef)
    search_two, z_up, z_dn = precond(image, (sent_up, sent_dn), (got_lo, got_hi), coefs, inv_lo, inv_hi)
    z_lo, z_hi = halo(z_up, z_dn)
    diag, _, _ = diagonal(search_two)
    plane, depth = sum_groups(mesh)
    partial_sums = call(
        gram_kernel, shape(len(plane[0]), 8, ncols),
        diag, couple, z_lo, z_hi, idx, source, image, flops=5 * 10**8,
    )
    partial_sums = lax.all_to_all(partial_sums, AXES, 0, 0, axis_index_groups=plane)
    partial_sums = call(merge_kernel, shape(len(depth[0]), 8, ncols), partial_sums)
    partial_sums = lax.all_to_all(partial_sums, AXES, 0, 0, axis_index_groups=depth)
    answer, miss = call(
        finish_kernel, (shape(nrows, ncols), shape(1, ncols)), partial_sums, search_one, search_two
    )
    return (answer[None, None], miss[0])


def sum_groups(mesh):
    n_sub, n_blk = mesh.shape["sub"], mesh.shape["blk"]
    near = min(8, n_sub)
    size = near * n_blk
    count = n_sub // near
    plane = [[g * size + k for k in range(size)] for g in range(count)]
    depth = [[g * size + k for g in range(count)] for k in range(size)]
    return plane, depth


def solution(mesh):
    placed = (
        P("sub", "blk", None, None),
        P("sub", "blk", None, None, None),
        P("sub", "blk", None, None, None),
        P("sub", "blk", None, None, None),
        P("sub", "blk", None, None),
        P("sub", "blk"),
        P("sub", None, None),
        P("sub", "blk", None),
    )
    return jax.shard_map(
        functools.partial(body, mesh),
        mesh=mesh,
        in_specs=placed,
        out_specs=(P("sub", "blk", None, None), P()),
        check_vma=False,
    )
```

time: 468 us -> 121 us (0.26)
  blocking collectives: 354 us -> 68.7 us
  other arithmetic: 31.2 us -> 0.08 us
  matrix products: 22.8 us -> 0 us
  Pallas kernels: 0 us -> 16 us
  local copies, waits for them, and re-layouts: 19.2 us -> 4.18 us
  starting transfers between devices: 34.8 us -> 24.5 us
    psum x3 -> x0, blocking collectives: 335 us -> none  [the longest x1 112 us: body(): lax.psum((jnp.sum(image_two * basis_one, 0), jnp.sum(image_two * basis_tw...]
    all_to_all x0 -> x4, blocking collectives: none -> 68.7 us  [the longest x1 30.4 us: body(): lax.all_to_all(partial_sums, AXES, 0, 0, axis_index_groups=depth)]
    dot_general x14 -> x0, matrix products: 22.8 us -> none  [the longest x2 5.74 us: apply_operator(): jnp.einsum('nij,njr->nir', block_mats, field.reshape(count_blocks, width,...]
    all_gather x2 -> x0, blocking collectives: 18.9 us -> none  [apply_precond(): every = lax.all_gather(coef, 'blk', axis=0, tiled=True)]
    scatter-add x8 -> x0, other arithmetic: 18.6 us -> none  [the longest x2 5.76 us: apply_operator(): local.at[low_idx].add(jnp.dot(couple[0], from_low, precision=highest))]
    pallas_call x0 -> x9, Pallas kernels: none -> 16 us  [call(): pl.pallas_call(kernel, out_shape=out_shape, compiler_params=pltpu.Compile...]
    gather x8 -> x0, local copies, waits for them, and re-layouts: 11.9 us -> none  [the longest x4 5.96 us: apply_operator(): sent = jnp.concatenate([field[low_idx], field[high_idx]], 0)]
    ppermute x12 -> x8, starting transfers between devices: 34.8 us -> 24.5 us  [halo(): return (lax.ppermute(to_up, 'sub', up), lax.ppermute(to_down, 'sub', down))]
  transfers between devices with their start and end apart: 12 -> 8, of which waited for: 3 -> 2; matrix products, arithmetic and copies ran while one was open for 5% -> 0% of each run, Pallas kernels for 0% -> 4%
where the time goes in v1:
time: 121 us; the launch traced here: 119 us
  blocking collectives  68.7 us (57%)
  starting transfers between devices  24.5 us (20%)
  Pallas kernels  16 us (13%)
  local copies, waits for them, and re-layouts  4.18 us (3%)
  waiting for transfers between devices  4.1 us (3%)
  between operations  1.48 us (1%)
    all_to_all x1, blocking collectives, body(): lax.all_to_all(partial_sums, AXES, 0, 0, axis_index_groups=depth)  30.4 us
    ppermute x8, starting transfers between devices, halo(): return (lax.ppermute(to_up, 'sub', up), lax.ppermute(to_down, 'sub', down))  24.5 us
    all_to_all x1, blocking collectives, body(): lax.all_to_all(partial_sums, AXES, 0, 0, axis_index_groups=plane)  21.9 us
    all_to_all x2, blocking collectives, coarse_group(): return lax.all_to_all(coef, 'blk', 0, 0)  16.4 us
    pallas_call x9, Pallas kernels, call(): pl.pallas_call(kernel, out_shape=out_shape, compiler_params=pltpu.Compile...  16 us
    unnamed x22, local copies, waits for them, and re-layouts  4.18 us
    ppermute x8, waiting for transfers between devices, halo(): return (lax.ppermute(to_up, 'sub', up), lax.ppermute(to_down, 'sub', down))  4.1 us
  transfers between devices with their start and end apart: 8, of which 2 were waited for; matrix products, arithmetic and copies ran while one was open for 0% of the time, Pallas kernels for 4%

profile of v1, /device:TPU:1, one launch (start us, length us, event | category | flops | bytes accessed | tf_op | source)
XLA Modules:
  0.0 119.1 jit_solution(2759950092632139644)
XLA Ops:
  1.3 0.1 pad_add_fusion.scal_ref
  1.4 0.0 copy-start
  1.4 1.3 %copy-done = f32[1,1,5,256,256]{4,3,2,1,0:T(8,128)S(1)} copy-done((f32[1,1,5,256,256]{4,3,2,1,0:T(8,128)S(1)}, f32[1,1,5,256,256]{4,3,2,1,0:T(8,128)}, u32[]{:S(2)}) %copy-start) | copy-done | bytes 1310744
  2.7 0.0 copy-start.2
  2.7 1.2 %copy-done.2 = f32[1,1,1024,256]{3,2,1,0:T(8,128)S(1)} copy-done((f32[1,1,1024,256]{3,2,1,0:T(8,128)S(1)}, f32[1,1,1024,256]{3,2,1,0:T(8,128)}, u32[]{:S(2)}) %copy-start.2) | copy-done | bytes 1048600
  3.9 0.0 copy-start.4
  3.9 0.9 copy-done.4
  4.8 0.0 copy-start.8
  4.8 0.7 copy-done.8
  5.5 0.0 copy-start.6
  5.5 1.3 %prep_kernel.1 = (f32[384,256]{1,0:T(8,128)S(1)}, f32[384,256]{1,0:T(8,128)S(1)}, f32[4,40,256]{2,1,0:T(8,128)S(1)}) custom-call(s32[2]{0:T(128)S(1)} %pad_add_fusion.scal_ref, f32[1024,256]{1,0:T(8,128)S(1)} %bitcast.15, s32[1,256]{1,0:T(1,128)S(1)} %bitcast.28, f32[40,1024]{1,0:T(8,128)S(1)} %bitcast.18, f32[5,256,256]{2,1,0:T(8,128)S(1)} %bitcast.12), custom_call_target="tpu_custom_call" | custom-call | flops 300000000 | bytes 2524168 | tf_op jit(solution)/shard_map/prep_kernel/pallas_call | solution.py:239
  6.8 4.6 %collective-permute-start = (f32[384,256]{1,0:T(8,128)S(1)}, f32[384,256]{1,0:T(8,128)S(1)}, u32[]{:S(2)}, u32[]{:S(2)}) collective-permute-start(f32[384,256]{1,0:T(8,128)S(1)} %get-tuple-element.21.up_ref), channel_id=1, source_target_pairs={{0,4},{4,8},{8,12},{12,16},{16,20},{20,24},{24,28},{28,32},{32,36}... | collective-permute-start | bytes 1179656 | tf_op jit(solution)/shard_map/ppermute | solution.py:266
  11.4 5.5 %collective-permute-start.1 = (f32[384,256]{1,0:T(8,128)S(1)}, f32[384,256]{1,0:T(8,128)S(1)}, u32[]{:S(2)}, u32[]{:S(2)}) collective-permute-start(f32[384,256]{1,0:T(8,128)S(1)} %get-tuple-element.22.dn_ref), channel_id=1, source_target_pairs={{4,0},{8,4},{12,8},{16,12},{20,16},{24,20},{28,24},{32,28},{36,32}... | collective-permute-start | bytes 1179656 | tf_op jit(solution)/shard_map/ppermute | solution.py:266
  16.9 8.2 %all_to_all.20.all_ref = f32[4,40,256]{2,1,0:T(8,128)S(1)} all-to-all(f32[4,40,256]{2,1,0:T(8,128)S(1)} %get-tuple-element.23), channel_id=1, replica_groups=mesh['sub'=128,'blk'=4] {'blk'}, dimensions={0} | all-to-all | bytes 327680 | tf_op jit(solution)/shard_map/all_to_all | solution.py:269
  25.1 0.0 collective-permute-done.lo_ref.inv_lo_ref
  25.1 0.0 collective-permute-done.1.hi_ref.inv_hi_ref
  25.1 0.0 copy-done.6
  25.1 0.0 copy-start.5
  25.2 0.0 copy-start.9
  25.2 0.0 copy-start.10
  25.2 2.9 %local_kernel.2 = (f32[1024,256]{1,0:T(8,128)S(1)}, f32[128,256]{1,0:T(8,128)S(1)}, f32[128,256]{1,0:T(8,128)S(1)}) custom-call(s32[2]{0:T(128)S(1)} %pad_add_fusion.scal_ref, f32[1024,256]{1,0:T(8,128)S(1)} %bitcast.16, f32[384,256]{1,0:T(8,128)S(1)} %get-tuple-element.21.up_ref, f32[384,256]{1,0:T(8,128)S(1)} %get-tuple-element.22.dn_ref, ...), custom_call_target="tpu_custom_call" | custom-call | flops 1000000000 | bytes 5149704 | tf_op jit(solution)/shard_map/local_kernel/pallas_call | solution.py:239
  28.1 2.1 %collective-permute-start.2 = (f32[128,256]{1,0:T(8,128)S(1)}, f32[128,256]{1,0:T(8,128)S(1)}, u32[]{:S(2)}, u32[]{:S(2)}) collective-permute-start(f32[128,256]{1,0:T(8,128)S(1)} %get-tuple-element.28), channel_id=1, source_target_pairs={{0,4},{4,8},{8,12},{12,16},{16,20},{20,24},{24,28},{28,32},{32,36}... | collective-permute-start | bytes 393224 | tf_op jit(solution)/shard_map/ppermute | solution.py:266
  30.2 2.2 %collective-permute-start.3 = (f32[128,256]{1,0:T(8,128)S(1)}, f32[128,256]{1,0:T(8,128)S(1)}, u32[]{:S(2)}, u32[]{:S(2)}) collective-permute-start(f32[128,256]{1,0:T(8,128)S(1)} %get-tuple-element.29), channel_id=1, source_target_pairs={{4,0},{8,4},{12,8},{16,12},{20,16},{24,20},{28,24},{32,28},{36,32}... | collective-permute-start | bytes 393224 | tf_op jit(solution)/shard_map/ppermute | solution.py:266
  32.4 0.0 copy-done.5
  32.4 0.0 copy-done.9
  32.5 0.0 copy-done.10
  32.5 0.0 copy-start.7
  32.5 1.8 %blocks_kernel.2 = (f32[1024,256]{1,0:T(8,128)S(1)}, f32[256,256]{1,0:T(8,128)S(1)}, f32[40,256]{1,0:T(8,128)S(1)}) custom-call(s32[2]{0:T(128)S(1)} %pad_add_fusion.scal_ref, f32[1024,256]{1,0:T(8,128)S(1)} %get-tuple-element.24.z_ref.p_ref, f32[4,256,256]{2,1,0:T(8,128)S(1)} %bitcast.35, f32[40,1024]{1,0:T(8,128)S(1)} %bitcast.20, s32[1,256]{1,0:T(1,128)S(1)} %bitcast.30), custom_call_target="tpu_custom_call" | custom-call | flops 1000000000 | bytes 2262024 | tf_op jit(solution)/shard_map/blocks_kernel/pallas_call | solution.py:239
  34.2 0.0 copy-start.1
  34.2 0.0 collective-permute-done.2.lo_ref
  34.3 2.2 %collective-permute-done.3.hi_ref = f32[128,256]{1,0:T(8,128)S(1)} collective-permute-done((f32[128,256]{1,0:T(8,128)S(1)}, f32[128,256]{1,0:T(8,128)S(1)}, u32[]{:S(2)}, u32[]{:S(2)}) %collective-permute-start.3) | collective-permute-done | bytes 131104 | tf_op jit(solution)/shard_map/ppermute | solution.py:266
  36.5 0.0 copy-done.7
  36.5 1.8 %image_kernel.1 = (f32[1024,256]{1,0:T(8,128)S(1)}, f32[256,256]{1,0:T(8,128)S(1)}, f32[256,256]{1,0:T(8,128)S(1)}, f32[4,40,256]{2,1,0:T(8,128)S(1)}) custom-call(s32[2]{0:T(128)S(1)} %pad_add_fusion.scal_ref, f32[1024,256]{1,0:T(8,128)S(1)} %get-tuple-element.25.t_ref, f32[256,256]{1,0:T(8,128)S(1)} %get-tuple-element.26.rows_ref, ...), custom_call_target="tpu_custom_call" | custom-call | flops 500000000 | bytes 1909768 | tf_op jit(solution)/shard_map/image_kernel/pallas_call | solution.py:239
  38.3 1.9 %collective-permute-start.4 = (f32[256,256]{1,0:T(8,128)S(1)}, f32[256,256]{1,0:T(8,128)S(1)}, u32[]{:S(2)}, u32[]{:S(2)}) collective-permute-start(f32[256,256]{1,0:T(8,128)S(1)} %get-tuple-element.31.up_ref), channel_id=1, source_target_pairs={{0,4},{4,8},{8,12},{12,16},{16,20},{20,24},{24,28},{28,32},{32,36}... | collective-permute-start | bytes 786440 | tf_op jit(solution)/shard_map/ppermute | solution.py:266
  40.2 2.4 %collective-permute-start.5 = (f32[256,256]{1,0:T(8,128)S(1)}, f32[256,256]{1,0:T(8,128)S(1)}, u32[]{:S(2)}, u32[]{:S(2)}) collective-permute-start(f32[256,256]{1,0:T(8,128)S(1)} %get-tuple-element.32.dn_ref), channel_id=1, source_target_pairs={{4,0},{8,4},{12,8},{16,12},{20,16},{24,20},{28,24},{32,28},{36,32}... | collective-permute-start | bytes 786440 | tf_op jit(solution)/shard_map/ppermute | solution.py:266
  42.7 8.2 %all_to_all.21.all_ref = f32[4,40,256]{2,1,0:T(8,128)S(1)} all-to-all(f32[4,40,256]{2,1,0:T(8,128)S(1)} %get-tuple-element.33), channel_id=1, replica_groups=mesh['sub'=128,'blk'=4] {'blk'}, dimensions={0} | all-to-all | bytes 327680 | tf_op jit(solution)/shard_map/all_to_all | solution.py:269
  50.9 0.0 collective-permute-done.4.lo_ref
  50.9 0.0 collective-permute-done.5.hi_ref
  50.9 0.0 copy-done.1
  50.9 2.9 %local_kernel.3 = (f32[1024,256]{1,0:T(8,128)S(1)}, f32[128,256]{1,0:T(8,128)S(1)}, f32[128,256]{1,0:T(8,128)S(1)}) custom-call(s32[2]{0:T(128)S(1)} %pad_add_fusion.scal_ref, f32[1024,256]{1,0:T(8,128)S(1)} %get-tuple-element.30.r_ref.u1_ref, f32[256,256]{1,0:T(8,128)S(1)} %get-tuple-element.31.up_ref, f32[256,256]{1,0:T(8,128)S(1)} %get-tuple-element.32.dn_ref, ...), custom_call_target="tpu_custom_call" | custom-call | flops 1000000000 | bytes 4625416 | tf_op jit(solution)/shard_map/local_kernel/pallas_call | solution.py:239
  53.8 3.8 %collective-permute-start.6 = (f32[128,256]{1,0:T(8,128)S(1)}, f32[128,256]{1,0:T(8,128)S(1)}, u32[]{:S(2)}, u32[]{:S(2)}) collective-permute-start(f32[128,256]{1,0:T(8,128)S(1)} %get-tuple-element.36), channel_id=1, source_target_pairs={{0,4},{4,8},{8,12},{12,16},{16,20},{20,24},{24,28},{28,32},{32,36}... | collective-permute-start | bytes 393224 | tf_op jit(solution)/shard_map/ppermute | solution.py:266
  57.6 1.9 %collective-permute-start.7 = (f32[128,256]{1,0:T(8,128)S(1)}, f32[128,256]{1,0:T(8,128)S(1)}, u32[]{:S(2)}, u32[]{:S(2)}) collective-permute-start(f32[128,256]{1,0:T(8,128)S(1)} %get-tuple-element.37), channel_id=1, source_target_pairs={{4,0},{8,4},{12,8},{16,12},{20,16},{24,20},{28,24},{32,28},{36,32}... | collective-permute-start | bytes 393224 | tf_op jit(solution)/shard_map/ppermute | solution.py:266
  59.5 0.0 copy-start.3
  59.5 2.5 %blocks_kernel.3 = (f32[1024,256]{1,0:T(8,128)S(1)}, f32[256,256]{1,0:T(8,128)}, f32[40,256]{1,0:T(8,128)}) custom-call(s32[2]{0:T(128)S(1)} %pad_add_fusion.scal_ref, f32[1024,256]{1,0:T(8,128)S(1)} %get-tuple-element.34.z_ref.q_ref, f32[4,256,256]{2,1,0:T(8,128)S(1)} %bitcast.36, f32[40,1024]{1,0:T(8,128)S(1)} %bitcast.23, s32[1,256]{1,0:T(1,128)S(1)} %bitcast.33), custom_call_target="tpu_custom_call" | custom-call | flops 1000000000 | bytes 2262024 | tf_op jit(solution)/shard_map/blocks_kernel/pallas_call | solution.py:239
  62.0 0.0 collective-permute-done.6.lo_ref
  62.0 1.9 %collective-permute-done.7.hi_ref = f32[128,256]{1,0:T(8,128)S(1)} collective-permute-done((f32[128,256]{1,0:T(8,128)S(1)}, f32[128,256]{1,0:T(8,128)S(1)}, u32[]{:S(2)}, u32[]{:S(2)}) %collective-permute-start.7) | collective-permute-done | bytes 131104 | tf_op jit(solution)/shard_map/ppermute | solution.py:266
  63.9 0.0 copy-done.3
  63.9 1.5 %gram_kernel.1 = f32[32,8,256]{2,1,0:T(8,128)S(1)} custom-call(f32[1024,256]{1,0:T(8,128)S(1)} %get-tuple-element.35.t_ref, f32[2,128,128]{2,1,0:T(8,128)S(1)} %bitcast.27, f32[128,256]{1,0:T(8,128)S(1)} %collective-permute-done.6.lo_ref, f32[128,256]{1,0:T(8,128)S(1)} %collective-permute-done.7.hi_ref, s32[1,256]{1,0:T(1,128)S(1)} %bitcast.34, ...), custom_call_target="tpu_custom_call" | custom-call | flops 500000000 | bytes 3539968 | tf_op jit(solution)/shard_map/gram_kernel/pallas_call | solution.py:239
  65.3 21.9 %all_to_all.22.parts_ref = f32[32,8,256]{2,1,0:T(8,128)S(1)} all-to-all(f32[32,8,256]{2,1,0:T(8,128)S(1)} %gram_kernel.1), channel_id=1, replica_groups={{0,1,2,3,4,5,6,7,8,9,10,11,12,13,14,15,16,17,18,19,20,21,22,23,24,25,26..., dimensions={0} | all-to-all | bytes 524288 | tf_op jit(solution)/shard_map/all_to_all | solution.py:312
  87.3 0.2 merge_kernel.1
  87.5 30.4 %all_to_all.23.parts_ref = f32[16,8,256]{2,1,0:T(8,128)S(1)} all-to-all(f32[16,8,256]{2,1,0:T(8,128)S(1)} %merge_kernel.1), channel_id=1, replica_groups={{0,32,64,96,128,160,192,224,256,288,320,352,384,416,448,480},{1,33,65,9..., dimensions={0} | all-to-all | bytes 262144 | tf_op jit(solution)/shard_map/all_to_all | solution.py:314
  117.8 1.2 %finish_kernel.1 = (f32[1024,256]{1,0:T(8,128)}, f32[1,256]{1,0:T(1,128)}) custom-call(f32[16,8,256]{2,1,0:T(8,128)S(1)} %all_to_all.23.parts_ref, f32[1024,256]{1,0:T(8,128)S(1)} %get-tuple-element.24.z_ref.p_ref, f32[1024,256]{1,0:T(8,128)S(1)} %get-tuple-element.34.z_ref.q_ref), custom_call_target="tpu_custom_call" | custom-call | bytes 2228224 | tf_op jit(solution)/shard_map/finish_kernel/pallas_call | solution.py:239
Async XLA Ops:
  1.4 1.3 %copy-start = (f32[1,1,5,256,256]{4,3,2,1,0:T(8,128)S(1)}, f32[1,1,5,256,256]{4,3,2,1,0:T(8,128)}, u32[]{:S(2)}) copy-start(f32[1,1,5,256,256]{4,3,2,1,0:T(8,128)} %param.11) | copy-start | bytes 3932164
  2.7 1.2 %copy-start.2 = (f32[1,1,1024,256]{3,2,1,0:T(8,128)S(1)}, f32[1,1,1024,256]{3,2,1,0:T(8,128)}, u32[]{:S(2)}) copy-start(f32[1,1,1024,256]{3,2,1,0:T(8,128)} %param.8) | copy-start | bytes 3145732
  3.9 0.9 copy-start.4
  4.8 0.7 copy-start.8
  5.5 19.7 %copy-start.6 = (f32[1,160,160]{2,1,0:T(8,128)S(1)}, f32[1,160,160]{2,1,0:T(8,128)}, u32[]{:S(2)}) copy-start(f32[1,160,160]{2,1,0:T(8,128)} %param.14) | copy-start | bytes 307204
  6.8 18.3 %collective-permute-start = (f32[384,256]{1,0:T(8,128)S(1)}, f32[384,256]{1,0:T(8,128)S(1)}, u32[]{:S(2)}, u32[]{:S(2)}) collective-permute-start(f32[384,256]{1,0:T(8,128)S(1)} %get-tuple-element.21.up_ref), channel_id=1, source_target_pairs={{0,4},{4,8},{8,12},{12,16},{16,20},{20,24},{24,28},{28,32},{32,36}... | collective-permute-start | bytes 1179656 | tf_op jit(solution)/shard_map/ppermute | solution.py:266
  11.4 13.7 %collective-permute-start.1 = (f32[384,256]{1,0:T(8,128)S(1)}, f32[384,256]{1,0:T(8,128)S(1)}, u32[]{:S(2)}, u32[]{:S(2)}) collective-permute-start(f32[384,256]{1,0:T(8,128)S(1)} %get-tuple-element.22.dn_ref), channel_id=1, source_target_pairs={{4,0},{8,4},{12,8},{16,12},{20,16},{24,20},{28,24},{32,28},{36,32}... | collective-permute-start | bytes 1179656 | tf_op jit(solution)/shard_map/ppermute | solution.py:266
  25.1 7.3 %copy-start.5 = (f32[1,1,40,1024]{3,2,1,0:T(8,128)S(1)}, f32[1,1,40,1024]{3,2,1,0:T(8,128)}, u32[]{:S(2)}) copy-start(f32[1,1,40,1024]{3,2,1,0:T(8,128)} %param.12) | copy-start | bytes 491524
  25.2 7.3 %copy-start.9 = (s32[1,1,256]{2,1,0:T(1,128)S(1)}, s32[1,1,256]{2,1,0:T(1,128)}, u32[]{:S(2)}) copy-start(s32[1,1,256]{2,1,0:T(1,128)} %param.15) | copy-start | bytes 3076
  25.2 7.3 %copy-start.10 = (f32[1,1,4,256,256]{4,3,2,1,0:T(8,128)S(1)}, f32[1,1,4,256,256]{4,3,2,1,0:T(8,128)}, u32[]{:S(2)}) copy-start(f32[1,1,4,256,256]{4,3,2,1,0:T(8,128)} %param.9) | copy-start | bytes 3145732
  28.1 6.2 %collective-permute-start.2 = (f32[128,256]{1,0:T(8,128)S(1)}, f32[128,256]{1,0:T(8,128)S(1)}, u32[]{:S(2)}, u32[]{:S(2)}) collective-permute-start(f32[128,256]{1,0:T(8,128)S(1)} %get-tuple-element.28), channel_id=1, source_target_pairs={{0,4},{4,8},{8,12},{12,16},{16,20},{20,24},{24,28},{28,32},{32,36}... | collective-permute-start | bytes 393224 | tf_op jit(solution)/shard_map/ppermute | solution.py:266
  30.2 6.3 %collective-permute-start.3 = (f32[128,256]{1,0:T(8,128)S(1)}, f32[128,256]{1,0:T(8,128)S(1)}, u32[]{:S(2)}, u32[]{:S(2)}) collective-permute-start(f32[128,256]{1,0:T(8,128)S(1)} %get-tuple-element.29), channel_id=1, source_target_pairs={{4,0},{8,4},{12,8},{16,12},{20,16},{24,20},{28,24},{32,28},{36,32}... | collective-permute-start | bytes 393224 | tf_op jit(solution)/shard_map/ppermute | solution.py:266
  32.5 4.0 %copy-start.7 = (f32[1,1,2,128,128]{4,3,2,1,0:T(8,128)S(1)}, f32[1,1,2,128,128]{4,3,2,1,0:T(8,128)}, u32[]{:S(2)}) copy-start(f32[1,1,2,128,128]{4,3,2,1,0:T(8,128)} %param.10) | copy-start | bytes 393220
  34.2 16.6 %copy-start.1 = (f32[1,1,5,256,256]{4,3,2,1,0:T(8,128)S(1)}, f32[1,1,5,256,256]{4,3,2,1,0:T(8,128)}, u32[]{:S(2)}) copy-start(f32[1,1,5,256,256]{4,3,2,1,0:T(8,128)} %param.11) | copy-start | bytes 3932164
  38.3 12.6 %collective-permute-start.4 = (f32[256,256]{1,0:T(8,128)S(1)}, f32[256,256]{1,0:T(8,128)S(1)}, u32[]{:S(2)}, u32[]{:S(2)}) collective-permute-start(f32[256,256]{1,0:T(8,128)S(1)} %get-tuple-element.31.up_ref), channel_id=1, source_target_pairs={{0,4},{4,8},{8,12},{12,16},{16,20},{20,24},{24,28},{28,32},{32,36}... | collective-permute-start | bytes 786440 | tf_op jit(solution)/shard_map/ppermute | solution.py:266
  40.2 10.6 %collective-permute-start.5 = (f32[256,256]{1,0:T(8,128)S(1)}, f32[256,256]{1,0:T(8,128)S(1)}, u32[]{:S(2)}, u32[]{:S(2)}) collective-permute-start(f32[256,256]{1,0:T(8,128)S(1)} %get-tuple-element.32.dn_ref), channel_id=1, source_target_pairs={{4,0},{8,4},{12,8},{16,12},{20,16},{24,20},{28,24},{32,28},{36,32}... | collective-permute-start | bytes 786440 | tf_op jit(solution)/shard_map/ppermute | solution.py:266
  53.8 8.2 %collective-permute-start.6 = (f32[128,256]{1,0:T(8,128)S(1)}, f32[128,256]{1,0:T(8,128)S(1)}, u32[]{:S(2)}, u32[]{:S(2)}) collective-permute-start(f32[128,256]{1,0:T(8,128)S(1)} %get-tuple-element.36), channel_id=1, source_target_pairs={{0,4},{4,8},{8,12},{12,16},{16,20},{20,24},{24,28},{28,32},{32,36}... | collective-permute-start | bytes 393224 | tf_op jit(solution)/shard_map/ppermute | solution.py:266
  57.6 6.3 %collective-permute-start.7 = (f32[128,256]{1,0:T(8,128)S(1)}, f32[128,256]{1,0:T(8,128)S(1)}, u32[]{:S(2)}, u32[]{:S(2)}) collective-permute-start(f32[128,256]{1,0:T(8,128)S(1)} %get-tuple-element.37), channel_id=1, source_target_pairs={{4,0},{8,4},{12,8},{16,12},{20,16},{24,20},{28,24},{32,28},{36,32}... | collective-permute-start | bytes 393224 | tf_op jit(solution)/shard_map/ppermute | solution.py:266
  59.5 4.4 %copy-start.3 = (f32[1,1,1024,256]{3,2,1,0:T(8,128)S(1)}, f32[1,1,1024,256]{3,2,1,0:T(8,128)}, u32[]{:S(2)}) copy-start(f32[1,1,1024,256]{3,2,1,0:T(8,128)} %param.8) | copy-start | bytes 3145732

commit v2 on v1

v2 whole, which is shorter than its diff:
```python
import functools

import jax
import jax.numpy as jnp
from jax import lax
from jax.experimental import pallas as pl
from jax.experimental.pallas import tpu as pltpu
from jax.sharding import PartitionSpec as P

f32 = jnp.float32
bf16 = jnp.bfloat16
AXES = ("sub", "blk")
WIDE = 128
LIMIT = 24 * 1024 * 1024


def split(a):
    high = a.astype(bf16)
    return high, (a - high.astype(f32)).astype(bf16)


def dot(a, b, dims=((1,), (0,))):
    return lax.dot_general(a, b, (dims, ((), ())), preferred_element_type=f32)


def mul(a, b, dims=((1,), (0,))):
    return dot(a[0], b[0], dims) + (dot(a[0], b[1], dims) + dot(a[1], b[0], dims))


def pick(onehot, b):
    return dot(onehot, b[0]) + dot(onehot, b[1])


def gather_matrix(idx, nrows):
    count = idx.shape[1]
    column = jnp.broadcast_to(idx.astype(f32), (128, count)).T
    lane = lax.broadcasted_iota(jnp.int32, (count, 128), 1).astype(f32)
    parts = [
        jnp.where(column == lane + float(128 * k), 1.0, 0.0).astype(bf16)
        for k in range(nrows // 128)
    ]
    return jnp.concatenate(parts, axis=1)


def scatter_matrix(idx, nrows):
    row = lax.broadcasted_iota(jnp.int32, (nrows, idx.shape[1]), 0)
    return jnp.where(row == idx, 1.0, 0.0).astype(bf16)


def masked_deflation(defl, count):
    row = lax.broadcasted_iota(jnp.int32, defl.shape, 0)
    return jnp.where(row < count, defl, 0.0)


def edge_block(high, ref, width):
    start = pl.multiple_of(jnp.where(high, ref.shape[0] - width, 0), width)
    return ref[pl.ds(start, width)]


def padded(a, count):
    return jnp.concatenate([a, jnp.zeros((count - a.shape[0], a.shape[1]), a.dtype)], 0)


def tripled(high, low):
    return padded(jnp.concatenate([high, high, low], 0), WIDE).astype(bf16)


def gather_all(gather_ref, many, lines, a):
    high, low = split(a)
    top = dot(gather_ref[...], high)
    rest = dot(gather_ref[: many + lines], low)
    return top[:many] + rest[:many], top[many : many + lines] + (top[many + lines :] + rest[many:])


def prep_kernel(
    count_ref, odd_ref, slot_ref, r_hbm, idx_hbm, defl_hbm, inv_hbm,
    far_ref, near_ref, coef_ref, r_ref, inv_ref, gather_ref, scatter_ref, zrows_ref, lift_ref, off_ref,
    idx_ref, defl_ref, sems,
):
    many = idx_ref.shape[1]
    half = many // 2
    nrows, ncols = r_ref.shape
    kmax = defl_ref.shape[0]
    lines = zrows_ref.shape[0] // 2
    step = nrows // 4
    blocks, width = inv_ref.shape[0], inv_ref.shape[2]
    odd = odd_ref[0] == 1
    pieces = [(idx_hbm, idx_ref), (defl_hbm, defl_ref)]
    pieces += [(r_hbm.at[pl.ds(k * step, step)], r_ref.at[pl.ds(k * step, step)]) for k in range(4)]
    pieces += [(inv_hbm.at[k], inv_ref.at[k]) for k in (0, blocks - 1)]
    pieces += [(inv_hbm.at[pl.ds(1, blocks - 2)], inv_ref.at[pl.ds(1, blocks - 2)])]
    copies = [pltpu.make_async_copy(a, b, sems.at[k]) for k, (a, b) in enumerate(pieces)]
    for copy in copies[:8]:
        copy.start()
    copies[0].wait()
    low, high = idx_ref[:, :half], idx_ref[:, half:]
    idx = jnp.concatenate([jnp.where(odd, low, high), jnp.where(odd, high, low)], 1)
    gather = gather_matrix(idx, nrows)
    scatter = scatter_matrix(idx, nrows)
    gather_ref[:many] = gather
    scatter_ref[:, :many] = scatter
    off_ref[...] = 1.0 - dot(scatter, jnp.ones((many, off_ref.shape[1]), bf16))
    copies[1].wait()
    masked = masked_deflation(defl_ref[...], count_ref[0, 0])
    z_high = masked.astype(bf16).astype(f32)
    z_low = (masked - z_high).astype(bf16).astype(f32)
    z_pair = jnp.concatenate([padded(z_high, lines), padded(z_low, lines)], 0).astype(bf16)
    gather_ref[many:] = z_pair
    zrows_ref[...] = dot(z_pair, scatter).astype(bf16)
    lift = padded(jnp.concatenate([z_high, z_low, z_high], 0), WIDE).T.astype(bf16)
    scatter_ref[:, many:] = lift
    lift_ref[...] = dot(gather, lift).astype(bf16)
    for copy in copies[2:6]:
        copy.wait()
    copies[8].start()
    rows, coef = gather_all(gather_ref, many, lines, r_ref[...])
    for k in range(coef_ref.shape[0]):
        coef_ref[k] = coef[:kmax]
    copies[6].wait()
    copies[7].wait()
    for k, (ref, high) in enumerate(((near_ref, odd_ref[0] == 0), (far_ref, odd))):
        ref[:half] = rows[k * half : (k + 1) * half]
        ref[half : 2 * half] = edge_block(high, r_ref, half)
        first, last = inv_ref[0, :half], inv_ref[blocks - 1, width - half :]
        ref[2 * half :, :half] = jnp.where(high, last[:, half:], first[:, :half])
        ref[2 * half :, half:] = jnp.where(high, last[:, :half], first[:, half:])
    copies[8].wait()


def local_kernel(
    odd_ref, slot_ref, r_ref, far_ref, near_ref, gfar_ref, gnear_ref, inv_far_ref, inv_near_ref,
    inv_ref, all_ref, panel_ref, lift_ref, gather_ref, own_ref, back_ref, coarse_ref, zfar_ref, znear_ref,
):
    odd = odd_ref[0] == 1
    half = znear_ref.shape[0]
    nrows, ncols = r_ref.shape
    kmax = all_ref.shape[1]
    width = inv_ref.shape[1]
    last = inv_ref.shape[0] - 1
    slot = pl.multiple_of(slot_ref[0] * kmax, 8)
    panel = split(panel_ref[pl.ds(slot, kmax), :])
    coefs = split(all_ref[...].reshape(all_ref.shape[0] * kmax, ncols))
    coarse = mul(panel, coefs)
    high = coarse.astype(bf16).astype(f32)
    coarse = tripled(high, coarse - high)
    coarse_ref[...] = coarse
    rows = dot(lift_ref[...], coarse)
    got_lo = jnp.where(odd, gnear_ref[:half], gfar_ref[:half])
    got_hi = jnp.where(odd, gfar_ref[:half], gnear_ref[:half])
    for n in range(last + 1):
        low = half if n == 0 else 0
        high = width - half if n == last else width
        if n == 0:
            part = jnp.concatenate([got_lo, r_ref[:half]], 0)
        elif n == last:
            part = jnp.concatenate([r_ref[nrows - half :], got_hi], 0)
        else:
            part = r_ref[n * width - half : (n + 1) * width - half]
        at = slice(n * width + low - half, n * width + high - half)
        y = mul(split(inv_ref[n, low:high]), split(part))
        own_ref[at] = y
        rows = rows + pick(gather_ref[: 2 * half, at], split(y))
    back = [
        mul(split(inverse[2 * half :]), split(jnp.concatenate([own[:half], got[half : 2 * half]], 0)))
        for own, got, inverse in ((near_ref, gnear_ref, inv_near_ref), (far_ref, gfar_ref, inv_far_ref))
    ]
    back = jnp.concatenate(back, 0)
    back_ref[...] = back
    rows = rows + back
    znear_ref[...] = rows[:half]
    zfar_ref[...] = rows[half:]


def block_products(own_ref, back_ref, coarse_ref, mats_ref, scatter_ref, z_ref, t_ref):
    many = back_ref.shape[0]
    high, low = split(back_ref[...])
    width = mats_ref.shape[1]
    both = jnp.concatenate([high, coarse_ref[...]], 0)
    for n in range(mats_ref.shape[0]):
        part = slice(n * width, (n + 1) * width)
        z = own_ref[part] + (dot(scatter_ref[part], both) + dot(scatter_ref[part, :many], low))
        z_ref[part] = z
        t_ref[part] = mul(split(mats_ref[n]), split(z))


def blocks_kernel(
    own_ref, back_ref, coarse_ref, mats_ref, scatter_ref, gather_ref, z_ref, t_ref, rows_ref, coef_ref
):
    block_products(own_ref, back_ref, coarse_ref, mats_ref, scatter_ref, z_ref, t_ref)
    rows_ref[...], coef = gather_all(gather_ref, rows_ref.shape[0], coef_ref.shape[0], t_ref[...])
    coef_ref[...] = coef


def shared_rows(odd_ref, couple_ref, gfar_ref, gnear_ref):
    near = mul(split(couple_ref[1 - odd_ref[0]]), split(gnear_ref[...]))
    far = mul(split(couple_ref[odd_ref[0]]), split(gfar_ref[...]))
    return jnp.concatenate([near, far], 0)


def image_kernel(
    odd_ref, t_ref, rows_ref, tcoef_ref, zrows_ref, couple_ref, gfar_ref, gnear_ref, scatter_ref,
    u_ref, far_ref, near_ref, coef_ref, urows_ref,
):
    add = shared_rows(odd_ref, couple_ref, gfar_ref, gnear_ref)
    many = add.shape[0]
    half = many // 2
    lines = tcoef_ref.shape[0]
    rows = rows_ref[...] + add
    urows_ref[...] = rows
    high, low = split(add)
    u_ref[...] = t_ref[...] + (dot(scatter_ref[:, :many], high) + dot(scatter_ref[:, :many], low))
    near_ref[:half] = rows[:half]
    far_ref[:half] = rows[half:]
    near_ref[half:] = edge_block(odd_ref[0] == 0, u_ref, half)
    far_ref[half:] = edge_block(odd_ref[0] == 1, u_ref, half)
    coef = dot(zrows_ref[...], high)
    coef = tcoef_ref[...] + (coef[:lines] + (coef[lines:] + dot(zrows_ref[:lines], low)))
    for k in range(coef_ref.shape[0]):
        coef_ref[k] = coef[: coef_ref.shape[1]]


def inverse_or_zero(a):
    return jnp.where(a > 0.0, 1.0 / jnp.where(a > 0.0, a, 1.0), 0.0)


def total(a):
    return jnp.sum(a, axis=0, keepdims=True)


PAIRS = ((0, 1), (0, 2), (1, 2))


def stacked(rows):
    return jnp.concatenate(rows + [jnp.zeros_like(rows[0])] * (8 - len(rows)), 0)


def last_blocks_kernel(
    own_ref, back_ref, coarse_ref, mats_ref, scatter_ref, gather_ref, off_ref,
    u0_ref, u1_ref, far0_ref, near0_ref, rows1_ref,
    z_ref, rows_ref, unit0_ref, unit1_ref, sums_ref, t_ref,
):
    many, ncols = rows_ref.shape
    half = many // 2
    nrows = z_ref.shape[0]
    lanes = off_ref.shape[1]
    block_products(own_ref, back_ref, coarse_ref, mats_ref, scatter_ref, z_ref, t_ref)
    rows_ref[...] = pick(gather_ref[:many], split(t_ref[...]))
    for at in range(0, nrows, 8):
        keep = off_ref[at : at + 8]
        for col in range(0, ncols, lanes):
            t_ref[at : at + 8, col : col + lanes] *= keep
    tops, factors = [], []
    for ref in (u0_ref, u1_ref, t_ref):
        top = jnp.max(jnp.abs(ref[...]).reshape(nrows // 8, 8, ncols), axis=0)
        top = jnp.max(top, axis=0, keepdims=True)
        tops.append(top)
        factors.append(inverse_or_zero(top))
    pairs = ((0, 0), (1, 1), (0, 1), (2, 2), (0, 2), (1, 2))
    sums = [jnp.zeros((8, ncols), f32)] * len(pairs)
    for at in range(0, nrows, 8):
        now = [ref[at : at + 8] * factor for ref, factor in zip((u0_ref, u1_ref, t_ref), factors)]
        sums = [total_ + now[i] * now[j] for total_, (i, j) in zip(sums, pairs)]
    sum_00, sum_11, sum_01, sum_22, sum_02, sum_12 = (total(a) for a in sums)
    size0, size1 = jnp.sqrt(sum_00), jnp.sqrt(sum_11)
    shrink0, shrink1 = inverse_or_zero(size0), inverse_or_zero(size1)
    unit0_ref[:half] = near0_ref[:half] * factors[0] * shrink0
    unit0_ref[half:] = far0_ref[:half] * factors[0] * shrink0
    unit1_ref[...] = rows1_ref[...] * factors[1] * shrink1
    sums_ref[...] = stacked(
        [
            tops[0] * size0, tops[1] * size1, tops[2], sum_01 * shrink0 * shrink1,
            sum_22, sum_02 * shrink0, sum_12 * shrink1,
        ]
    )


def gram_kernel(odd_ref, rows_ref, couple_ref, gfar_ref, gnear_ref, unit0_ref, unit1_ref, sums_ref, out_ref):
    rows = rows_ref[...] + shared_rows(odd_ref, couple_ref, gfar_ref, gnear_ref)
    len0, len1, top_off, cos_01, sum_22, sum_02, sum_12 = (sums_ref[k : k + 1] for k in range(7))
    top = jnp.maximum(top_off, jnp.max(jnp.abs(rows), axis=0, keepdims=True))
    scale = inverse_or_zero(top)
    rows = rows * scale
    ratio = top_off * scale
    size = jnp.sqrt(sum_22 * (ratio * ratio) + total(rows * rows))
    shrink = inverse_or_zero(size)
    cos_02 = (sum_02 * ratio + total(unit0_ref[...] * rows)) * shrink
    cos_12 = (sum_12 * ratio + total(unit1_ref[...] * rows)) * shrink
    full = stacked([len0, len1, top * size, cos_01, cos_02, cos_12])
    for k in range(out_ref.shape[0]):
        out_ref[k] = full


def merge(parts):
    lengths, shares = [], []
    for i in range(3):
        own = parts[:, i, :]
        top = jnp.max(own, axis=0, keepdims=True)
        share = own * inverse_or_zero(top)
        size = jnp.sqrt(total(share * share))
        lengths.append(top * size)
        shares.append(share * inverse_or_zero(size))
    cosines = [
        total(parts[:, 3 + k, :] * shares[i] * shares[j])
        for k, (i, j) in enumerate(PAIRS)
    ]
    return lengths, cosines


def merge_kernel(parts_ref, out_ref):
    lengths, cosines = merge(parts_ref[...])
    full = stacked(lengths + cosines)
    for k in range(out_ref.shape[0]):
        out_ref[k] = full


def least_squares(beta, proj_one, sub_one, proj_two_a, proj_two_b, sub_two):
    diag_one = jnp.sqrt(proj_one * proj_one + sub_one * sub_one)
    cross = (proj_one * proj_two_a + sub_one * proj_two_b) / diag_one
    rest_a = proj_two_a - cross * proj_one / diag_one
    rest_b = proj_two_b - cross * sub_one / diag_one
    diag_two = jnp.sqrt(rest_a * rest_a + rest_b * rest_b + sub_two * sub_two)
    coeff_two = beta * rest_a / (diag_two * diag_two)
    coeff_one = (beta * proj_one / diag_one - cross * coeff_two) / diag_one
    miss_a = beta - proj_one * coeff_one - proj_two_a * coeff_two
    miss_b = sub_one * coeff_one + proj_two_b * coeff_two
    miss_c = sub_two * coeff_two
    miss = jnp.sqrt(miss_a * miss_a + miss_b * miss_b + miss_c * miss_c)
    return (coeff_one, coeff_two, miss)


def finish_kernel(parts_ref, p_ref, q_ref, out_ref, miss_ref):
    (beta, len_one, len_two), (cos_01, cos_02, cos_12) = merge(parts_ref[...])
    rel_one = len_one / beta
    proj_one = rel_one * cos_01
    sine_sq = 1.0 - cos_01 * cos_01
    sub_one = rel_one * jnp.sqrt(sine_sq)
    rel_two = len_two / beta / sub_one
    proj_two_a = rel_two * cos_02 - proj_one * (proj_one / sub_one)
    side = (cos_12 - cos_01 * cos_02) / jnp.sqrt(sine_sq)
    proj_two_b = rel_two * side - proj_one
    sub_two = rel_two * jnp.sqrt(1.0 - cos_02 * cos_02 - side * side)
    coeff_one, coeff_two, miss = least_squares(beta, proj_one, sub_one, proj_two_a, proj_two_b, sub_two)
    miss_ref[...] = miss
    second = coeff_two / sub_one
    first = (coeff_one - second * proj_one) / beta
    out_ref[...] = first * p_ref[...] + (second / beta) * q_ref[...]


def shape(*dims, kind=f32):
    return jax.ShapeDtypeStruct(dims, kind)


VMEM = pl.BlockSpec(memory_space=pltpu.VMEM)
SMEM = pl.BlockSpec(memory_space=pltpu.SMEM)
HBM = pl.BlockSpec(memory_space=pltpu.HBM)


def call(name, kernel, out_shape, scalars, operands, place=VMEM, flops=0, scratch=(), out_place=None):
    size = sum(4 * a.size for a in operands)
    return pl.pallas_call(
        kernel,
        out_shape=out_shape,
        in_specs=[SMEM] * len(scalars) + [place] * len(operands),
        scratch_shapes=scratch,
        **({} if out_place is None else {"out_specs": out_place}),
        compiler_params=pltpu.CompilerParams(vmem_limit_bytes=LIMIT),
        cost_estimate=pl.CostEstimate(flops=flops, bytes_accessed=size, transcendentals=0),
        name=name,
    )(*scalars, *operands)


def body(mesh, rhs, blocks, coupling, inverse, deflation, counts, panel, intersection_rows):
    source, mats, couple, inv = rhs[0, 0], blocks[0, 0], coupling[0, 0], inverse[0, 0]
    defl, panel_mat = deflation[0, 0], panel[0]
    idx = intersection_rows[0]
    many = idx.shape[1]
    half = many // 2
    nrows, ncols = source.shape
    kmax = defl.shape[0]
    n_sub, n_blk = mesh.shape["sub"], mesh.shape["blk"]
    odd = jnp.bitwise_and(lax.axis_index("sub").astype(jnp.int32), 1)[None]
    slot = lax.axis_index("blk").astype(jnp.int32)[None]
    near_pairs = [(i, i ^ 1) for i in range(n_sub) if i ^ 1 < n_sub]
    far_pairs = [(i, ((i + 1) ^ 1) - 1) for i in range(1, n_sub) if ((i + 1) ^ 1) - 1 < n_sub]

    def halo(far, near):
        far = lax.ppermute(far, "sub", far_pairs)
        return far, lax.ppermute(near, "sub", near_pairs)

    def precond(vector, sent, got, coef):
        coefs = lax.all_to_all(coef, "blk", 0, 0)
        *parts, far, near = call(
            "local_solve", local_kernel,
            (
                shape(nrows, ncols), shape(many, ncols), shape(WIDE, ncols, kind=bf16), shape(half, ncols),
                shape(half, ncols),
            ),
            (odd, slot), (vector, *sent, *got, *inv_halves, inv, coefs, panel_mat, lift, gather),
            flops=10**9,
        )
        return parts, (far, near)

    lines = -(-kmax // 16) * 16
    *sent, coef, source, inv, gather, scatter, zrows, lift, off = call(
        "first_rows", prep_kernel,
        (
            shape(3 * half, ncols), shape(3 * half, ncols), shape(n_blk, kmax, ncols), shape(nrows, ncols),
            shape(*inv.shape), shape(many + 2 * lines, nrows, kind=bf16), shape(nrows, many + WIDE, kind=bf16),
            shape(2 * lines, many, kind=bf16), shape(many, WIDE, kind=bf16), shape(nrows, 128),
        ),
        (counts, odd, slot), [pltpu.with_memory_space_constraint(a, pltpu.HBM) for a in (source, idx, defl, inv)],
        place=HBM, flops=3 * 10**8, out_place=[VMEM] * 10,
        scratch=(pltpu.VMEM(idx.shape, jnp.int32), pltpu.VMEM(defl.shape, f32), pltpu.SemaphoreType.DMA((9,))),
    )
    got = inv_halves = halo(*sent)
    parts, halves = precond(source, sent, got, coef)
    z_got = halo(*halves)
    search_one, diag, diag_rows, diag_coef = call(
        "block_product", blocks_kernel,
        (shape(nrows, ncols), shape(nrows, ncols), shape(many, ncols), shape(lines, ncols)),
        (), (*parts, mats, scatter, gather), flops=10**9,
    )
    image, *sent_two, coef, image_rows = call(
        "image", image_kernel,
        (
            shape(nrows, ncols), shape(many, ncols), shape(many, ncols), shape(n_blk, kmax, ncols),
            shape(many, ncols),
        ),
        (odd,), (diag, diag_rows, diag_coef, zrows, couple, *z_got, scatter), flops=5 * 10**8,
    )
    got = halo(*sent_two)
    parts, halves = precond(image, sent_two, got, coef)
    z_got = halo(*halves)
    search_two, diag_rows, unit_one, unit_two, sums = call(
        "last_block_product", last_blocks_kernel,
        (shape(nrows, ncols), shape(many, ncols), shape(many, ncols), shape(many, ncols), shape(8, ncols)),
        (), (*parts, mats, scatter, gather, off, source, image, *sent, image_rows), flops=10**9,
        scratch=(pltpu.VMEM(source.shape, f32),),
    )
    plane, depth = sum_groups(mesh)
    parts = call(
        "lengths_cosines", gram_kernel, shape(len(plane[0]), 8, ncols),
        (odd,), (diag_rows, couple, *z_got, unit_one, unit_two, sums), flops=2 * 10**8,
    )
    parts = lax.all_to_all(parts, AXES, 0, 0, axis_index_groups=plane)
    parts = call("merge_plane", merge_kernel, shape(len(depth[0]), 8, ncols), (), (parts,))
    parts = lax.all_to_all(parts, AXES, 0, 0, axis_index_groups=depth)
    answer, miss = call(
        "combine", finish_kernel, (shape(nrows, ncols), shape(1, ncols)), (), (parts, search_one, search_two),
    )
    return (answer[None, None], miss[0])


def sum_groups(mesh):
    n_sub, n_blk = mesh.shape["sub"], mesh.shape["blk"]
    near = min(8, n_sub)
    size = near * n_blk
    count = n_sub // near
    plane = [[g * size + k for k in range(size)] for g in range(count)]
    depth = [[g * size + k for g in range(count)] for k in range(size)]
    return plane, depth


def solution(mesh):
    placed = (
        P("sub", "blk", None, None),
        P("sub", "blk", None, None, None),
        P("sub", "blk", None, None, None),
        P("sub", "blk", None, None, None),
        P("sub", "blk", None, None),
        P("sub", "blk"),
        P("sub", None, None),
        P("sub", "blk", None),
    )
    return jax.shard_map(
        functools.partial(body, mesh),
        mesh=mesh,
        in_specs=placed,
        out_specs=(P("sub", "blk", None, None), P()),
        check_vma=False,
    )
```

time: 121 us -> 102 us (0.84)
  blocking collectives: 68.7 us -> 59.7 us
  local copies, waits for them, and re-layouts: 4.18 us -> 0.02 us
  waiting for transfers between devices: 4.1 us -> 0.02 us
  Pallas kernels: 16 us -> 13 us
  starting transfers between devices: 24.5 us -> 26 us
    all_to_all x4, blocking collectives: 68.7 us -> 59.7 us  [the longest x1 28.3 us: body(): parts = lax.all_to_all(parts, AXES, 0, 0, axis_index_groups=depth)]
    unnamed x22 -> x6, local copies, waits for them, and re-layouts: 4.18 us -> 0.02 us
    ppermute x8, waiting for transfers between devices: 4.1 us -> 0.02 us  [the longest x4 0.01 us: halo(): far = lax.ppermute(far, 'sub', far_pairs)]
    pallas_call x9, Pallas kernels: 16 us -> 13 us  [call(): pl.pallas_call(kernel, out_shape=out_shape, in_specs=[SMEM] * len(scalars...]
    ppermute x8, starting transfers between devices: 24.5 us -> 26 us  [the longest x4 15.4 us: halo(): far = lax.ppermute(far, 'sub', far_pairs)]
  transfers between devices with their start and end apart: 8 -> 8, of which waited for: 2 -> 0; matrix products, arithmetic and copies ran while one was open for 0% -> 0% of each run, Pallas kernels for 4% -> 4%
where the time goes in v2:
time: 102 us; the launch traced here: 100 us
  blocking collectives  59.7 us (59%)
  starting transfers between devices  26 us (25%)
  Pallas kernels  13 us (13%)
  between operations  1.47 us (1%)
    all_to_all x1, blocking collectives, body(): parts = lax.all_to_all(parts, AXES, 0, 0, axis_index_groups=depth)  28.3 us
    all_to_all x1, blocking collectives, body(): parts = lax.all_to_all(parts, AXES, 0, 0, axis_index_groups=plane)  15.9 us
    all_to_all x2, blocking collectives, precond(): coefs = lax.all_to_all(coef, 'blk', 0, 0)  15.5 us
    ppermute x4, starting transfers between devices, halo(): far = lax.ppermute(far, 'sub', far_pairs)  15.4 us
    pallas_call x9, Pallas kernels, call(): pl.pallas_call(kernel, out_shape=out_shape, in_specs=[SMEM] * len(scalars...  13 us
    ppermute x4, starting transfers between devices, halo(): return (far, lax.ppermute(near, 'sub', near_pairs))  10.6 us
  transfers between devices with their start and end apart: 8, of which 0 were waited for; matrix products, arithmetic and copies ran while one was open for 0% of the time, Pallas kernels for 4%

profile of v2, /device:TPU:1, one launch (start us, length us, event | category | flops | bytes accessed | tf_op | source)
XLA Modules:
  0.0 100.2 jit_solution(4876654811275319114)
XLA Ops:
  1.3 0.0 copy-start.1
  1.3 2.9 %first_rows.1 = (f32[384,256]{1,0:T(8,128)S(1)}, f32[384,256]{1,0:T(8,128)S(1)}, f32[4,40,256]{2,1,0:T(8,128)S(1)}, f32[1024,256]{1,0:T(8,128)S(1)}, f32[5,256,2...) custom-call(s32[1,1]{1,0:T(1,128)S(6)} %copy.10.count_ref, ...), custom_call_target="tpu_custom_call" | custom-call | flops 300000000 | bytes 2524160 | tf_op jit(solution)/shard_map/first_rows/pallas_call | solution.py:360
  4.2 4.6 %collective-permute-start = (f32[384,256]{1,0:T(8,128)S(1)}, f32[384,256]{1,0:T(8,128)S(1)}, u32[]{:S(2)}, u32[]{:S(2)}) collective-permute-start(f32[384,256]{1,0:T(8,128)S(1)} %get-tuple-element.39.far_ref.far0_ref), channel_id=1, source_target_pairs={{4,8},{8,4},{12,16},{16,12},{20,24},{24,20},{28,32},{32,28},{36,40... | collective-permute-start | bytes 1179656 | tf_op jit(solution)/shard_map/ppermute | solution.py:387
  8.8 4.9 %collective-permute-start.1 = (f32[384,256]{1,0:T(8,128)S(1)}, f32[384,256]{1,0:T(8,128)S(1)}, u32[]{:S(2)}, u32[]{:S(2)}) collective-permute-start(f32[384,256]{1,0:T(8,128)S(1)} %get-tuple-element.40.near_ref.near0_ref), channel_id=1, source_target_pairs={{0,4},{4,0},{8,12},{12,8},{16,20},{20,16},{24,28},{28,24},{32,36},... | collective-permute-start | bytes 1179656 | tf_op jit(solution)/shard_map/ppermute | solution.py:388
  13.7 8.1 %all_to_all.20.all_ref = f32[4,40,256]{2,1,0:T(8,128)S(1)} all-to-all(f32[4,40,256]{2,1,0:T(8,128)S(1)} %get-tuple-element.42), channel_id=1, replica_groups=mesh['sub'=128,'blk'=4] {'blk'}, dimensions={0} | all-to-all | bytes 327680 | tf_op jit(solution)/shard_map/all_to_all | solution.py:391
  21.9 0.0 collective-permute-done.gfar_ref.inv_far_ref
  21.9 0.0 collective-permute-done.1.gnear_ref.inv_near_ref
  21.9 0.0 copy-done.1
  21.9 0.0 copy-start
  21.9 1.5 %local_solve.2 = (f32[1024,256]{1,0:T(8,128)S(1)}, f32[256,256]{1,0:T(8,128)S(1)}, bf16[128,256]{1,0:T(8,128)(2,1)S(1)}, f32[128,256]{1,0:T(8,128)S(1)}, f32[128,256]{1,0:T(8,128)S(1)}) custom-call(s32[1]{0:T(128)} %bitcast.odd_ref, s32[1]{0:T(128)} %bitcast.1.slot_ref, f32[1024,256]{1,0:T(8,128)S(1)} %get-tuple-element.38.r_ref.u0_ref, ...), custom_call_target="tpu_custom_call" | custom-call | flops 1000000000 | bytes 6557696 | tf_op jit(solution)/shard_map/local_solve/pallas_call | solution.py:360
  23.4 2.7 %collective-permute-start.2 = (f32[128,256]{1,0:T(8,128)S(1)}, f32[128,256]{1,0:T(8,128)S(1)}, u32[]{:S(2)}, u32[]{:S(2)}) collective-permute-start(f32[128,256]{1,0:T(8,128)S(1)} %get-tuple-element.53), channel_id=1, source_target_pairs={{4,8},{8,4},{12,16},{16,12},{20,24},{24,20},{28,32},{32,28},{36,40... | collective-permute-start | bytes 393224 | tf_op jit(solution)/shard_map/ppermute | solution.py:387
  26.2 1.9 %collective-permute-start.3 = (f32[128,256]{1,0:T(8,128)S(1)}, f32[128,256]{1,0:T(8,128)S(1)}, u32[]{:S(2)}, u32[]{:S(2)}) collective-permute-start(f32[128,256]{1,0:T(8,128)S(1)} %get-tuple-element.54), channel_id=1, source_target_pairs={{0,4},{4,0},{8,12},{12,8},{16,20},{20,16},{24,28},{28,24},{32,36},... | collective-permute-start | bytes 393224 | tf_op jit(solution)/shard_map/ppermute | solution.py:388
  28.1 0.0 copy-done
  28.1 0.0 copy-start.2
  28.1 1.9 %block_product.1 = (f32[1024,256]{1,0:T(8,128)S(1)}, f32[1024,256]{1,0:T(8,128)S(1)}, f32[256,256]{1,0:T(8,128)S(1)}, f32[48,256]{1,0:T(8,128)S(1)}) custom-call(f32[1024,256]{1,0:T(8,128)S(1)} %get-tuple-element.45.own_ref, f32[256,256]{1,0:T(8,128)S(1)} %get-tuple-element.46.back_ref, bf16[128,256]{1,0:T(8,128)(2,1)S(1)} %get-tuple-element.47.coarse_ref, ...), custom_call_target="tpu_custom_call" | custom-call | flops 1000000000 | bytes 5505024 | tf_op jit(solution)/shard_map/block_product/pallas_call | solution.py:360
  30.0 0.0 collective-permute-done.2.gfar_ref
  30.0 0.0 collective-permute-done.3.gnear_ref
  30.0 0.0 copy-done.2
  30.1 0.8 image.1
  30.8 3.3 %collective-permute-start.4 = (f32[256,256]{1,0:T(8,128)S(1)}, f32[256,256]{1,0:T(8,128)S(1)}, u32[]{:S(2)}, u32[]{:S(2)}) collective-permute-start(f32[256,256]{1,0:T(8,128)S(1)} %get-tuple-element.56.far_ref), channel_id=1, source_target_pairs={{4,8},{8,4},{12,16},{16,12},{20,24},{24,20},{28,32},{32,28},{36,40... | collective-permute-start | bytes 786440 | tf_op jit(solution)/shard_map/ppermute | solution.py:387
  34.1 1.9 %collective-permute-start.5 = (f32[256,256]{1,0:T(8,128)S(1)}, f32[256,256]{1,0:T(8,128)S(1)}, u32[]{:S(2)}, u32[]{:S(2)}) collective-permute-start(f32[256,256]{1,0:T(8,128)S(1)} %get-tuple-element.57.near_ref), channel_id=1, source_target_pairs={{0,4},{4,0},{8,12},{12,8},{16,20},{20,16},{24,28},{28,24},{32,36},... | collective-permute-start | bytes 786440 | tf_op jit(solution)/shard_map/ppermute | solution.py:388
  36.1 7.4 %all_to_all.21.all_ref = f32[4,40,256]{2,1,0:T(8,128)S(1)} all-to-all(f32[4,40,256]{2,1,0:T(8,128)S(1)} %get-tuple-element.58), channel_id=1, replica_groups=mesh['sub'=128,'blk'=4] {'blk'}, dimensions={0} | all-to-all | bytes 327680 | tf_op jit(solution)/shard_map/all_to_all | solution.py:391
  43.4 0.0 collective-permute-done.4.gfar_ref
  43.4 0.0 collective-permute-done.5.gnear_ref
  43.4 1.5 %local_solve.3 = (f32[1024,256]{1,0:T(8,128)S(1)}, f32[256,256]{1,0:T(8,128)S(1)}, bf16[128,256]{1,0:T(8,128)(2,1)S(1)}, f32[128,256]{1,0:T(8,128)S(1)}, f32[128,256]{1,0:T(8,128)S(1)}) custom-call(s32[1]{0:T(128)} %bitcast.odd_ref, s32[1]{0:T(128)} %bitcast.1.slot_ref, f32[1024,256]{1,0:T(8,128)S(1)} %get-tuple-element.55.r_ref.u1_ref, ...), custom_call_target="tpu_custom_call" | custom-call | flops 1000000000 | bytes 6033408 | tf_op jit(solution)/shard_map/local_solve/pallas_call | solution.py:360
  45.0 4.7 %collective-permute-start.6 = (f32[128,256]{1,0:T(8,128)S(1)}, f32[128,256]{1,0:T(8,128)S(1)}, u32[]{:S(2)}, u32[]{:S(2)}) collective-permute-start(f32[128,256]{1,0:T(8,128)S(1)} %get-tuple-element.65), channel_id=1, source_target_pairs={{4,8},{8,4},{12,16},{16,12},{20,24},{24,20},{28,32},{32,28},{36,40... | collective-permute-start | bytes 393224 | tf_op jit(solution)/shard_map/ppermute | solution.py:387
  49.7 1.9 %collective-permute-start.7 = (f32[128,256]{1,0:T(8,128)S(1)}, f32[128,256]{1,0:T(8,128)S(1)}, u32[]{:S(2)}, u32[]{:S(2)}) collective-permute-start(f32[128,256]{1,0:T(8,128)S(1)} %get-tuple-element.66), channel_id=1, source_target_pairs={{0,4},{4,0},{8,12},{12,8},{16,20},{20,16},{24,28},{28,24},{32,36},... | collective-permute-start | bytes 393224 | tf_op jit(solution)/shard_map/ppermute | solution.py:388
  51.7 2.4 %last_block_product.1 = (f32[1024,256]{1,0:T(8,128)S(1)}, f32[256,256]{1,0:T(8,128)S(1)}, f32[256,256]{1,0:T(8,128)S(1)}, f32[256,256]{1,0:T(8,128)S(1)}, f32[8,256]{1,0:T(8,128)S(1)}) custom-call(f32[1024,256]{1,0:T(8,128)S(1)} %get-tuple-element.59.own_ref, f32[256,256]{1,0:T(8,128)S(1)} %get-tuple-element.60.back_ref, ...), custom_call_target="tpu_custom_call" | custom-call | flops 1000000000 | bytes 9175040 | tf_op jit(solution)/shard_map/last_block_product/pallas_call | solution.py:360
  54.1 0.0 collective-permute-done.6.gfar_ref
  54.1 0.0 collective-permute-done.7.gnear_ref
  54.1 0.4 lengths_cosines.1
  54.5 15.9 %all_to_all.22.parts_ref = f32[32,8,256]{2,1,0:T(8,128)S(1)} all-to-all(f32[32,8,256]{2,1,0:T(8,128)S(1)} %lengths_cosines.1), channel_id=1, replica_groups={{0,1,2,3,4,5,6,7,8,9,10,11,12,13,14,15,16,17,18,19,20,21,22,23,24,25,26..., dimensions={0} | all-to-all | bytes 524288 | tf_op jit(solution)/shard_map/all_to_all | solution.py:445
  70.4 0.2 merge_plane.1
  70.6 28.3 %all_to_all.23.parts_ref = f32[16,8,256]{2,1,0:T(8,128)S(1)} all-to-all(f32[16,8,256]{2,1,0:T(8,128)S(1)} %merge_plane.1), channel_id=1, replica_groups={{0,32,64,96,128,160,192,224,256,288,320,352,384,416,448,480},{1,33,65,9..., dimensions={0} | all-to-all | bytes 262144 | tf_op jit(solution)/shard_map/all_to_all | solution.py:447
  98.9 1.3 %combine.1 = (f32[1024,256]{1,0:T(8,128)}, f32[1,256]{1,0:T(1,128)}) custom-call(f32[16,8,256]{2,1,0:T(8,128)S(1)} %all_to_all.23.parts_ref, f32[1024,256]{1,0:T(8,128)S(1)} %get-tuple-element.70.p_ref, f32[1024,256]{1,0:T(8,128)S(1)} %get-tuple-element.71.q_ref), custom_call_target="tpu_custom_call" | custom-call | bytes 2228224 | tf_op jit(solution)/shard_map/combine/pallas_call | solution.py:360
Async XLA Ops:
  1.3 20.6 %copy-start.1 = (f32[1,160,160]{2,1,0:T(8,128)S(1)}, f32[1,160,160]{2,1,0:T(8,128)}, u32[]{:S(2)}) copy-start(f32[1,160,160]{2,1,0:T(8,128)} %param.14) | copy-start | bytes 307204
  4.2 17.6 %collective-permute-start = (f32[384,256]{1,0:T(8,128)S(1)}, f32[384,256]{1,0:T(8,128)S(1)}, u32[]{:S(2)}, u32[]{:S(2)}) collective-permute-start(f32[384,256]{1,0:T(8,128)S(1)} %get-tuple-element.39.far_ref.far0_ref), channel_id=1, source_target_pairs={{4,8},{8,4},{12,16},{16,12},{20,24},{24,20},{28,32},{32,28},{36,40... | collective-permute-start | bytes 1179656 | tf_op jit(solution)/shard_map/ppermute | solution.py:387
  8.8 13.0 %collective-permute-start.1 = (f32[384,256]{1,0:T(8,128)S(1)}, f32[384,256]{1,0:T(8,128)S(1)}, u32[]{:S(2)}, u32[]{:S(2)}) collective-permute-start(f32[384,256]{1,0:T(8,128)S(1)} %get-tuple-element.40.near_ref.near0_ref), channel_id=1, source_target_pairs={{0,4},{4,0},{8,12},{12,8},{16,20},{20,16},{24,28},{28,24},{32,36},... | collective-permute-start | bytes 1179656 | tf_op jit(solution)/shard_map/ppermute | solution.py:388
  21.9 6.3 %copy-start = (f32[1,1,4,256,256]{4,3,2,1,0:T(8,128)S(1)}, f32[1,1,4,256,256]{4,3,2,1,0:T(8,128)}, u32[]{:S(2)}) copy-start(f32[1,1,4,256,256]{4,3,2,1,0:T(8,128)} %param.9) | copy-start | bytes 3145732
  23.4 6.6 %collective-permute-start.2 = (f32[128,256]{1,0:T(8,128)S(1)}, f32[128,256]{1,0:T(8,128)S(1)}, u32[]{:S(2)}, u32[]{:S(2)}) collective-permute-start(f32[128,256]{1,0:T(8,128)S(1)} %get-tuple-element.53), channel_id=1, source_target_pairs={{4,8},{8,4},{12,16},{16,12},{20,24},{24,20},{28,32},{32,28},{36,40... | collective-permute-start | bytes 393224 | tf_op jit(solution)/shard_map/ppermute | solution.py:387
  26.2 3.8 %collective-permute-start.3 = (f32[128,256]{1,0:T(8,128)S(1)}, f32[128,256]{1,0:T(8,128)S(1)}, u32[]{:S(2)}, u32[]{:S(2)}) collective-permute-start(f32[128,256]{1,0:T(8,128)S(1)} %get-tuple-element.54), channel_id=1, source_target_pairs={{0,4},{4,0},{8,12},{12,8},{16,20},{20,16},{24,28},{28,24},{32,36},... | collective-permute-start | bytes 393224 | tf_op jit(solution)/shard_map/ppermute | solution.py:388
  28.1 1.9 %copy-start.2 = (f32[1,1,2,128,128]{4,3,2,1,0:T(8,128)S(1)}, f32[1,1,2,128,128]{4,3,2,1,0:T(8,128)}, u32[]{:S(2)}) copy-start(f32[1,1,2,128,128]{4,3,2,1,0:T(8,128)} %param.10) | copy-start | bytes 393220
  30.8 12.6 %collective-permute-start.4 = (f32[256,256]{1,0:T(8,128)S(1)}, f32[256,256]{1,0:T(8,128)S(1)}, u32[]{:S(2)}, u32[]{:S(2)}) collective-permute-start(f32[256,256]{1,0:T(8,128)S(1)} %get-tuple-element.56.far_ref), channel_id=1, source_target_pairs={{4,8},{8,4},{12,16},{16,12},{20,24},{24,20},{28,32},{32,28},{36,40... | collective-permute-start | bytes 786440 | tf_op jit(solution)/shard_map/ppermute | solution.py:387
  34.1 9.3 %collective-permute-start.5 = (f32[256,256]{1,0:T(8,128)S(1)}, f32[256,256]{1,0:T(8,128)S(1)}, u32[]{:S(2)}, u32[]{:S(2)}) collective-permute-start(f32[256,256]{1,0:T(8,128)S(1)} %get-tuple-element.57.near_ref), channel_id=1, source_target_pairs={{0,4},{4,0},{8,12},{12,8},{16,20},{20,16},{24,28},{28,24},{32,36},... | collective-permute-start | bytes 786440 | tf_op jit(solution)/shard_map/ppermute | solution.py:388
  45.0 9.1 %collective-permute-start.6 = (f32[128,256]{1,0:T(8,128)S(1)}, f32[128,256]{1,0:T(8,128)S(1)}, u32[]{:S(2)}, u32[]{:S(2)}) collective-permute-start(f32[128,256]{1,0:T(8,128)S(1)} %get-tuple-element.65), channel_id=1, source_target_pairs={{4,8},{8,4},{12,16},{16,12},{20,24},{24,20},{28,32},{32,28},{36,40... | collective-permute-start | bytes 393224 | tf_op jit(solution)/shard_map/ppermute | solution.py:387
  49.7 4.4 %collective-permute-start.7 = (f32[128,256]{1,0:T(8,128)S(1)}, f32[128,256]{1,0:T(8,128)S(1)}, u32[]{:S(2)}, u32[]{:S(2)}) collective-permute-start(f32[128,256]{1,0:T(8,128)S(1)} %get-tuple-element.66), channel_id=1, source_target_pairs={{0,4},{4,0},{8,12},{12,8},{16,20},{20,16},{24,28},{28,24},{32,36},... | collective-permute-start | bytes 393224 | tf_op jit(solution)/shard_map/ppermute | solution.py:388

commit v3 on v2

--- a/solution.py
+++ b/solution.py
@@ -90,7 +90,7 @@
     pieces += [(inv_hbm.at[k], inv_ref.at[k]) for k in (0, blocks - 1)]
     pieces += [(inv_hbm.at[pl.ds(1, blocks - 2)], inv_ref.at[pl.ds(1, blocks - 2)])]
     copies = [pltpu.make_async_copy(a, b, sems.at[k]) for k, (a, b) in enumerate(pieces)]
-    for copy in copies[:8]:
+    for copy in copies:
         copy.start()
     copies[0].wait()
     low, high = idx_ref[:, :half], idx_ref[:, half:]
@@ -112,7 +112,6 @@
     lift_ref[...] = dot(gather, lift).astype(bf16)
     for copy in copies[2:6]:
         copy.wait()
-    copies[8].start()
     rows, coef = gather_all(gather_ref, many, lines, r_ref[...])
     for k in range(coef_ref.shape[0]):
         coef_ref[k] = coef[:kmax]
@@ -285,32 +284,38 @@
     shrink = inverse_or_zero(size)
     cos_02 = (sum_02 * ratio + total(unit0_ref[...] * rows)) * shrink
     cos_12 = (sum_12 * ratio + total(unit1_ref[...] * rows)) * shrink
-    full = stacked([len0, len1, top * size, cos_01, cos_02, cos_12])
-    for k in range(out_ref.shape[0]):
-        out_ref[k] = full
+    send_packed([len0, len1, top * size, cos_01, cos_02, cos_12], out_ref)
 
 
 def merge(parts):
     lengths, shares = [], []
-    for i in range(3):
-        own = parts[:, i, :]
+    for own in parts[:3]:
         top = jnp.max(own, axis=0, keepdims=True)
         share = own * inverse_or_zero(top)
         size = jnp.sqrt(total(share * share))
         lengths.append(top * size)
         shares.append(share * inverse_or_zero(size))
     cosines = [
-        total(parts[:, 3 + k, :] * shares[i] * shares[j])
+        total(parts[3 + k] * shares[i] * shares[j])
         for k, (i, j) in enumerate(PAIRS)
     ]
     return lengths, cosines
 
 
+def unpacked(ref):
+    ncols = ref.shape[2] // 6
+    return [ref[:, 0, k * ncols : (k + 1) * ncols] for k in range(6)]
+
+
+def send_packed(rows, ref):
+    full = jnp.concatenate(rows, 1)
+    for k in range(ref.shape[0]):
+        ref[k] = full
+
+
 def merge_kernel(parts_ref, out_ref):
-    lengths, cosines = merge(parts_ref[...])
-    full = stacked(lengths + cosines)
-    for k in range(out_ref.shape[0]):
-        out_ref[k] = full
+    lengths, cosines = merge(unpacked(parts_ref))
+    send_packed(lengths + cosines, out_ref)
 
 
 def least_squares(beta, proj_one, sub_one, proj_two_a, proj_two_b, sub_two):
@@ -329,7 +334,7 @@
 
 
 def finish_kernel(parts_ref, p_ref, q_ref, out_ref, miss_ref):
-    (beta, len_one, len_two), (cos_01, cos_02, cos_12) = merge(parts_ref[...])
+    (beta, len_one, len_two), (cos_01, cos_02, cos_12) = merge(unpacked(parts_ref))
     rel_one = len_one / beta
     proj_one = rel_one * cos_01
     sine_sq = 1.0 - cos_01 * cos_01
@@ -439,11 +444,11 @@
     )
     plane, depth = sum_groups(mesh)
     parts = call(
-        "lengths_cosines", gram_kernel, shape(len(plane[0]), 8, ncols),
+        "lengths_cosines", gram_kernel, shape(len(plane[0]), 1, 6 * ncols),
         (odd,), (diag_rows, couple, *z_got, unit_one, unit_two, sums), flops=2 * 10**8,
     )
     parts = lax.all_to_all(parts, AXES, 0, 0, axis_index_groups=plane)
-    parts = call("merge_plane", merge_kernel, shape(len(depth[0]), 8, ncols), (), (parts,))
+    parts = call("merge_plane", merge_kernel, shape(len(depth[0]), 1, 6 * ncols), (), (parts,))
     parts = lax.all_to_all(parts, AXES, 0, 0, axis_index_groups=depth)
     answer, miss = call(
         "combine", finish_kernel, (shape(nrows, ncols), shape(1, ncols)), (), (parts, search_one, search_two),

time: 102 us -> 99.7 us (0.977)
  no operation moved by 1% of the time
where the time goes in v3:
time: 99.7 us; the launch traced here: 98.8 us
  blocking collectives  58.9 us (59%)
  starting transfers between devices  26 us (26%)
  Pallas kernels  12.4 us (12%)
  between operations  1.47 us (1%)
    all_to_all x1, blocking collectives, body(): parts = lax.all_to_all(parts, AXES, 0, 0, axis_index_groups=depth)  28.1 us
    all_to_all x2, blocking collectives, precond(): coefs = lax.all_to_all(coef, 'blk', 0, 0)  15.5 us
    ppermute x4, starting transfers between devices, halo(): far = lax.ppermute(far, 'sub', far_pairs)  15.4 us
    all_to_all x1, blocking collectives, body(): parts = lax.all_to_all(parts, AXES, 0, 0, axis_index_groups=plane)  15.2 us
    pallas_call x9, Pallas kernels, call(): pl.pallas_call(kernel, out_shape=out_shape, in_specs=[SMEM] * len(scalars...  12.4 us
    ppermute x4, starting transfers between devices, halo(): return (far, lax.ppermute(near, 'sub', near_pairs))  10.6 us
  transfers between devices with their start and end apart: 8, of which 0 were waited for; matrix products, arithmetic and copies ran while one was open for 0% of the time, Pallas kernels for 4%

profile of v3, /device:TPU:1, one launch (start us, length us, event | category | flops | bytes accessed | tf_op | source)
XLA Modules:
  0.0 98.8 jit_solution(2636192248348146487)
XLA Ops:
  1.3 0.0 copy-start.1
  1.3 2.4 %first_rows.1 = (f32[384,256]{1,0:T(8,128)S(1)}, f32[384,256]{1,0:T(8,128)S(1)}, f32[4,40,256]{2,1,0:T(8,128)S(1)}, f32[1024,256]{1,0:T(8,128)S(1)}, f32[5,256,2...) custom-call(s32[1,1]{1,0:T(1,128)S(6)} %copy.10.count_ref, ...), custom_call_target="tpu_custom_call" | custom-call | flops 300000000 | bytes 2524160 | tf_op jit(solution)/shard_map/first_rows/pallas_call | solution.py:365
  3.7 4.6 %collective-permute-start = (f32[384,256]{1,0:T(8,128)S(1)}, f32[384,256]{1,0:T(8,128)S(1)}, u32[]{:S(2)}, u32[]{:S(2)}) collective-permute-start(f32[384,256]{1,0:T(8,128)S(1)} %get-tuple-element.39.far_ref.far0_ref), channel_id=1, source_target_pairs={{4,8},{8,4},{12,16},{16,12},{20,24},{24,20},{28,32},{32,28},{36,40... | collective-permute-start | bytes 1179656 | tf_op jit(solution)/shard_map/ppermute | solution.py:392
  8.3 4.9 %collective-permute-start.1 = (f32[384,256]{1,0:T(8,128)S(1)}, f32[384,256]{1,0:T(8,128)S(1)}, u32[]{:S(2)}, u32[]{:S(2)}) collective-permute-start(f32[384,256]{1,0:T(8,128)S(1)} %get-tuple-element.40.near_ref.near0_ref), channel_id=1, source_target_pairs={{0,4},{4,0},{8,12},{12,8},{16,20},{20,16},{24,28},{28,24},{32,36},... | collective-permute-start | bytes 1179656 | tf_op jit(solution)/shard_map/ppermute | solution.py:393
  13.2 8.1 %all_to_all.20.all_ref = f32[4,40,256]{2,1,0:T(8,128)S(1)} all-to-all(f32[4,40,256]{2,1,0:T(8,128)S(1)} %get-tuple-element.42), channel_id=1, replica_groups=mesh['sub'=128,'blk'=4] {'blk'}, dimensions={0} | all-to-all | bytes 327680 | tf_op jit(solution)/shard_map/all_to_all | solution.py:396
  21.3 0.0 collective-permute-done.gfar_ref.inv_far_ref
  21.3 0.0 collective-permute-done.1.gnear_ref.inv_near_ref
  21.3 0.0 copy-done.1
  21.4 0.0 copy-start
  21.4 1.6 %local_solve.2 = (f32[1024,256]{1,0:T(8,128)S(1)}, f32[256,256]{1,0:T(8,128)S(1)}, bf16[128,256]{1,0:T(8,128)(2,1)S(1)}, f32[128,256]{1,0:T(8,128)S(1)}, f32[128,256]{1,0:T(8,128)S(1)}) custom-call(s32[1]{0:T(128)} %bitcast.odd_ref, s32[1]{0:T(128)} %bitcast.1.slot_ref, f32[1024,256]{1,0:T(8,128)S(1)} %get-tuple-element.38.r_ref.u0_ref, ...), custom_call_target="tpu_custom_call" | custom-call | flops 1000000000 | bytes 6557696 | tf_op jit(solution)/shard_map/local_solve/pallas_call | solution.py:365
  22.9 2.7 %collective-permute-start.2 = (f32[128,256]{1,0:T(8,128)S(1)}, f32[128,256]{1,0:T(8,128)S(1)}, u32[]{:S(2)}, u32[]{:S(2)}) collective-permute-start(f32[128,256]{1,0:T(8,128)S(1)} %get-tuple-element.53), channel_id=1, source_target_pairs={{4,8},{8,4},{12,16},{16,12},{20,24},{24,20},{28,32},{32,28},{36,40... | collective-permute-start | bytes 393224 | tf_op jit(solution)/shard_map/ppermute | solution.py:392
  25.7 1.9 %collective-permute-start.3 = (f32[128,256]{1,0:T(8,128)S(1)}, f32[128,256]{1,0:T(8,128)S(1)}, u32[]{:S(2)}, u32[]{:S(2)}) collective-permute-start(f32[128,256]{1,0:T(8,128)S(1)} %get-tuple-element.54), channel_id=1, source_target_pairs={{0,4},{4,0},{8,12},{12,8},{16,20},{20,16},{24,28},{28,24},{32,36},... | collective-permute-start | bytes 393224 | tf_op jit(solution)/shard_map/ppermute | solution.py:393
  27.6 0.0 copy-done
  27.6 0.0 copy-start.2
  27.6 1.9 %block_product.1 = (f32[1024,256]{1,0:T(8,128)S(1)}, f32[1024,256]{1,0:T(8,128)S(1)}, f32[256,256]{1,0:T(8,128)S(1)}, f32[48,256]{1,0:T(8,128)S(1)}) custom-call(f32[1024,256]{1,0:T(8,128)S(1)} %get-tuple-element.45.own_ref, f32[256,256]{1,0:T(8,128)S(1)} %get-tuple-element.46.back_ref, bf16[128,256]{1,0:T(8,128)(2,1)S(1)} %get-tuple-element.47.coarse_ref, ...), custom_call_target="tpu_custom_call" | custom-call | flops 1000000000 | bytes 5505024 | tf_op jit(solution)/shard_map/block_product/pallas_call | solution.py:365
  29.5 0.0 collective-permute-done.2.gfar_ref
  29.5 0.0 collective-permute-done.3.gnear_ref
  29.5 0.0 copy-done.2
  29.5 0.8 image.1
  30.3 3.3 %collective-permute-start.4 = (f32[256,256]{1,0:T(8,128)S(1)}, f32[256,256]{1,0:T(8,128)S(1)}, u32[]{:S(2)}, u32[]{:S(2)}) collective-permute-start(f32[256,256]{1,0:T(8,128)S(1)} %get-tuple-element.56.far_ref), channel_id=1, source_target_pairs={{4,8},{8,4},{12,16},{16,12},{20,24},{24,20},{28,32},{32,28},{36,40... | collective-permute-start | bytes 786440 | tf_op jit(solution)/shard_map/ppermute | solution.py:392
  33.6 1.9 %collective-permute-start.5 = (f32[256,256]{1,0:T(8,128)S(1)}, f32[256,256]{1,0:T(8,128)S(1)}, u32[]{:S(2)}, u32[]{:S(2)}) collective-permute-start(f32[256,256]{1,0:T(8,128)S(1)} %get-tuple-element.57.near_ref), channel_id=1, source_target_pairs={{0,4},{4,0},{8,12},{12,8},{16,20},{20,16},{24,28},{28,24},{32,36},... | collective-permute-start | bytes 786440 | tf_op jit(solution)/shard_map/ppermute | solution.py:393
  35.5 7.4 %all_to_all.21.all_ref = f32[4,40,256]{2,1,0:T(8,128)S(1)} all-to-all(f32[4,40,256]{2,1,0:T(8,128)S(1)} %get-tuple-element.58), channel_id=1, replica_groups=mesh['sub'=128,'blk'=4] {'blk'}, dimensions={0} | all-to-all | bytes 327680 | tf_op jit(solution)/shard_map/all_to_all | solution.py:396
  42.9 0.0 collective-permute-done.4.gfar_ref
  42.9 0.0 collective-permute-done.5.gnear_ref
  42.9 1.5 %local_solve.3 = (f32[1024,256]{1,0:T(8,128)S(1)}, f32[256,256]{1,0:T(8,128)S(1)}, bf16[128,256]{1,0:T(8,128)(2,1)S(1)}, f32[128,256]{1,0:T(8,128)S(1)}, f32[128,256]{1,0:T(8,128)S(1)}) custom-call(s32[1]{0:T(128)} %bitcast.odd_ref, s32[1]{0:T(128)} %bitcast.1.slot_ref, f32[1024,256]{1,0:T(8,128)S(1)} %get-tuple-element.55.r_ref.u1_ref, ...), custom_call_target="tpu_custom_call" | custom-call | flops 1000000000 | bytes 6033408 | tf_op jit(solution)/shard_map/local_solve/pallas_call | solution.py:365
  44.5 4.7 %collective-permute-start.6 = (f32[128,256]{1,0:T(8,128)S(1)}, f32[128,256]{1,0:T(8,128)S(1)}, u32[]{:S(2)}, u32[]{:S(2)}) collective-permute-start(f32[128,256]{1,0:T(8,128)S(1)} %get-tuple-element.65), channel_id=1, source_target_pairs={{4,8},{8,4},{12,16},{16,12},{20,24},{24,20},{28,32},{32,28},{36,40... | collective-permute-start | bytes 393224 | tf_op jit(solution)/shard_map/ppermute | solution.py:392
  49.2 1.9 %collective-permute-start.7 = (f32[128,256]{1,0:T(8,128)S(1)}, f32[128,256]{1,0:T(8,128)S(1)}, u32[]{:S(2)}, u32[]{:S(2)}) collective-permute-start(f32[128,256]{1,0:T(8,128)S(1)} %get-tuple-element.66), channel_id=1, source_target_pairs={{0,4},{4,0},{8,12},{12,8},{16,20},{20,16},{24,28},{28,24},{32,36},... | collective-permute-start | bytes 393224 | tf_op jit(solution)/shard_map/ppermute | solution.py:393
  51.1 2.4 %last_block_product.1 = (f32[1024,256]{1,0:T(8,128)S(1)}, f32[256,256]{1,0:T(8,128)S(1)}, f32[256,256]{1,0:T(8,128)S(1)}, f32[256,256]{1,0:T(8,128)S(1)}, f32[8,256]{1,0:T(8,128)S(1)}) custom-call(f32[1024,256]{1,0:T(8,128)S(1)} %get-tuple-element.59.own_ref, f32[256,256]{1,0:T(8,128)S(1)} %get-tuple-element.60.back_ref, ...), custom_call_target="tpu_custom_call" | custom-call | flops 1000000000 | bytes 9175040 | tf_op jit(solution)/shard_map/last_block_product/pallas_call | solution.py:365
  53.6 0.0 collective-permute-done.6.gfar_ref
  53.6 0.0 collective-permute-done.7.gnear_ref
  53.6 0.4 lengths_cosines.1
  54.0 15.2 %all_to_all.22.parts_ref = f32[32,1,1536]{2,1,0:T(1,128)S(1)} all-to-all(f32[32,1,1536]{2,1,0:T(1,128)S(1)} %lengths_cosines.1), channel_id=1, replica_groups={{0,1,2,3,4,5,6,7,8,9,10,11,12,13,14,15,16,17,18,19,20,21,22,23,24,25,26..., dimensions={0} | all-to-all | bytes 393216 | tf_op jit(solution)/shard_map/all_to_all | solution.py:450
  69.2 0.2 merge_plane.1
  69.4 28.1 %all_to_all.23.parts_ref = f32[16,1,1536]{2,1,0:T(1,128)S(1)} all-to-all(f32[16,1,1536]{2,1,0:T(1,128)S(1)} %merge_plane.1), channel_id=1, replica_groups={{0,32,64,96,128,160,192,224,256,288,320,352,384,416,448,480},{1,33,65,9..., dimensions={0} | all-to-all | bytes 196608 | tf_op jit(solution)/shard_map/all_to_all | solution.py:452
  97.5 1.3 %combine.1 = (f32[1024,256]{1,0:T(8,128)}, f32[1,256]{1,0:T(1,128)}) custom-call(f32[16,1,1536]{2,1,0:T(1,128)S(1)} %all_to_all.23.parts_ref, f32[1024,256]{1,0:T(8,128)S(1)} %get-tuple-element.70.p_ref, f32[1024,256]{1,0:T(8,128)S(1)} %get-tuple-element.71.q_ref), custom_call_target="tpu_custom_call" | custom-call | bytes 2195456 | tf_op jit(solution)/shard_map/combine/pallas_call | solution.py:365
Async XLA Ops:
  1.3 20.1 %copy-start.1 = (f32[1,160,160]{2,1,0:T(8,128)S(1)}, f32[1,160,160]{2,1,0:T(8,128)}, u32[]{:S(2)}) copy-start(f32[1,160,160]{2,1,0:T(8,128)} %param.14) | copy-start | bytes 307204
  3.7 17.6 %collective-permute-start = (f32[384,256]{1,0:T(8,128)S(1)}, f32[384,256]{1,0:T(8,128)S(1)}, u32[]{:S(2)}, u32[]{:S(2)}) collective-permute-start(f32[384,256]{1,0:T(8,128)S(1)} %get-tuple-element.39.far_ref.far0_ref), channel_id=1, source_target_pairs={{4,8},{8,4},{12,16},{16,12},{20,24},{24,20},{28,32},{32,28},{36,40... | collective-permute-start | bytes 1179656 | tf_op jit(solution)/shard_map/ppermute | solution.py:392
  8.3 13.0 %collective-permute-start.1 = (f32[384,256]{1,0:T(8,128)S(1)}, f32[384,256]{1,0:T(8,128)S(1)}, u32[]{:S(2)}, u32[]{:S(2)}) collective-permute-start(f32[384,256]{1,0:T(8,128)S(1)} %get-tuple-element.40.near_ref.near0_ref), channel_id=1, source_target_pairs={{0,4},{4,0},{8,12},{12,8},{16,20},{20,16},{24,28},{28,24},{32,36},... | collective-permute-start | bytes 1179656 | tf_op jit(solution)/shard_map/ppermute | solution.py:393
  21.4 6.3 %copy-start = (f32[1,1,4,256,256]{4,3,2,1,0:T(8,128)S(1)}, f32[1,1,4,256,256]{4,3,2,1,0:T(8,128)}, u32[]{:S(2)}) copy-start(f32[1,1,4,256,256]{4,3,2,1,0:T(8,128)} %param.9) | copy-start | bytes 3145732
  22.9 6.6 %collective-permute-start.2 = (f32[128,256]{1,0:T(8,128)S(1)}, f32[128,256]{1,0:T(8,128)S(1)}, u32[]{:S(2)}, u32[]{:S(2)}) collective-permute-start(f32[128,256]{1,0:T(8,128)S(1)} %get-tuple-element.53), channel_id=1, source_target_pairs={{4,8},{8,4},{12,16},{16,12},{20,24},{24,20},{28,32},{32,28},{36,40... | collective-permute-start | bytes 393224 | tf_op jit(solution)/shard_map/ppermute | solution.py:392
  25.7 3.8 %collective-permute-start.3 = (f32[128,256]{1,0:T(8,128)S(1)}, f32[128,256]{1,0:T(8,128)S(1)}, u32[]{:S(2)}, u32[]{:S(2)}) collective-permute-start(f32[128,256]{1,0:T(8,128)S(1)} %get-tuple-element.54), channel_id=1, source_target_pairs={{0,4},{4,0},{8,12},{12,8},{16,20},{20,16},{24,28},{28,24},{32,36},... | collective-permute-start | bytes 393224 | tf_op jit(solution)/shard_map/ppermute | solution.py:393
  27.6 1.9 %copy-start.2 = (f32[1,1,2,128,128]{4,3,2,1,0:T(8,128)S(1)}, f32[1,1,2,128,128]{4,3,2,1,0:T(8,128)}, u32[]{:S(2)}) copy-start(f32[1,1,2,128,128]{4,3,2,1,0:T(8,128)} %param.10) | copy-start | bytes 393220
  30.3 12.6 %collective-permute-start.4 = (f32[256,256]{1,0:T(8,128)S(1)}, f32[256,256]{1,0:T(8,128)S(1)}, u32[]{:S(2)}, u32[]{:S(2)}) collective-permute-start(f32[256,256]{1,0:T(8,128)S(1)} %get-tuple-element.56.far_ref), channel_id=1, source_target_pairs={{4,8},{8,4},{12,16},{16,12},{20,24},{24,20},{28,32},{32,28},{36,40... | collective-permute-start | bytes 786440 | tf_op jit(solution)/shard_map/ppermute | solution.py:392
  33.6 9.3 %collective-permute-start.5 = (f32[256,256]{1,0:T(8,128)S(1)}, f32[256,256]{1,0:T(8,128)S(1)}, u32[]{:S(2)}, u32[]{:S(2)}) collective-permute-start(f32[256,256]{1,0:T(8,128)S(1)} %get-tuple-element.57.near_ref), channel_id=1, source_target_pairs={{0,4},{4,0},{8,12},{12,8},{16,20},{20,16},{24,28},{28,24},{32,36},... | collective-permute-start | bytes 786440 | tf_op jit(solution)/shard_map/ppermute | solution.py:393
  44.5 9.1 %collective-permute-start.6 = (f32[128,256]{1,0:T(8,128)S(1)}, f32[128,256]{1,0:T(8,128)S(1)}, u32[]{:S(2)}, u32[]{:S(2)}) collective-permute-start(f32[128,256]{1,0:T(8,128)S(1)} %get-tuple-element.65), channel_id=1, source_target_pairs={{4,8},{8,4},{12,16},{16,12},{20,24},{24,20},{28,32},{32,28},{36,40... | collective-permute-start | bytes 393224 | tf_op jit(solution)/shard_map/ppermute | solution.py:392
  49.2 4.4 %collective-permute-start.7 = (f32[128,256]{1,0:T(8,128)S(1)}, f32[128,256]{1,0:T(8,128)S(1)}, u32[]{:S(2)}, u32[]{:S(2)}) collective-permute-start(f32[128,256]{1,0:T(8,128)S(1)} %get-tuple-element.66), channel_id=1, source_target_pairs={{0,4},{4,0},{8,12},{12,8},{16,20},{20,16},{24,28},{28,24},{32,36},... | collective-permute-start | bytes 393224 | tf_op jit(solution)/shard_map/ppermute | solution.py:393

commit v4 on v3

--- a/solution.py
+++ b/solution.py
@@ -11,6 +11,7 @@
 bf16 = jnp.bfloat16
 AXES = ("sub", "blk")
 WIDE = 128
+LEAST, MOST = 1e-12, 1e24
 LIMIT = 24 * 1024 * 1024
 
 
@@ -218,6 +219,116 @@
         coef_ref[k] = coef[: coef_ref.shape[1]]
 
 
+highest = lax.Precision.HIGHEST
+
+
+def with_halo(array, sides, width):
+    for axis, dim in sides:
+        peers, length = (lax.axis_size(axis), array.shape[dim])
+        up = [(i, (i + 1) % peers) for i in range(peers - 1)]
+        down = [(j, i) for i, j in up]
+        last = lax.slice_in_dim(array, length - width, length, axis=dim)
+        first = lax.slice_in_dim(array, 0, width, axis=dim)
+        before = lax.ppermute(last, axis, up)
+        after = lax.ppermute(first, axis, down)
+        array = jnp.concatenate([before, array, after], axis=dim)
+    return array
+
+
+def apply_operator(field, block_mats, couple, low_idx, high_idx):
+    half = low_idx.shape[0]
+    sent = jnp.concatenate([field[low_idx], field[high_idx]], 0)
+    padded = with_halo(sent, (("sub", 0),), half)
+    from_low = padded[:half]
+    from_high = padded[padded.shape[0] - half :]
+    count_blocks, width = (block_mats.shape[0], block_mats.shape[1])
+    local = jnp.einsum(
+        "nij,njr->nir",
+        block_mats,
+        field.reshape(count_blocks, width, field.shape[1]),
+        precision=highest,
+    )
+    local = local.reshape(field.shape)
+    local = local.at[low_idx].add(jnp.dot(couple[0], from_low, precision=highest))
+    return local.at[high_idx].add(jnp.dot(couple[1], from_high, precision=highest))
+
+
+def apply_precond(resid, inv_mats, masked, panel_mat, low_idx, high_idx):
+    half = low_idx.shape[0]
+    nrows, ncols = resid.shape
+    sent = jnp.concatenate([resid[low_idx], resid[high_idx]], 0)
+    padded = with_halo(sent, (("sub", 0),), half)
+    extended = jnp.concatenate([padded[:half], resid, padded[padded.shape[0] - half :]], 0)
+    count_blocks, width = (inv_mats.shape[0], inv_mats.shape[1])
+    solved = jnp.einsum(
+        "nij,njr->nir", inv_mats, extended.reshape(count_blocks, width, ncols), precision=highest
+    )
+    solved = solved.reshape(nrows + 2 * half, ncols)
+    own = solved[half : half + nrows]
+    back_low = solved[:half]
+    back_high = solved[half + nrows :]
+    coef = jnp.dot(masked, resid, precision=highest)
+    kmax = coef.shape[0]
+    slot = lax.axis_index("blk")
+    every = lax.all_gather(coef, "blk", axis=0, tiled=True)
+    mine = lax.dynamic_slice_in_dim(panel_mat, slot * kmax, kmax, 0)
+    correct = jnp.dot(mine, every, precision=highest)
+    partial_value = own + jnp.einsum("kn,kr->nr", masked, correct, precision=highest)
+    back = jnp.concatenate([back_low, back_high], 0)
+    returned = with_halo(back, (("sub", 0),), half)
+    field = partial_value.at[low_idx].add(returned[:half])
+    field = field.at[high_idx].add(returned[returned.shape[0] - half :])
+    return (field, None)
+
+
+def normalised_solve(rhs, blocks, coupling, inverse, deflation, counts, panel, intersection_rows):
+    source = rhs[0, 0]
+    block_mats = blocks[0, 0]
+    couple = coupling[0, 0]
+    inv_mats = inverse[0, 0]
+    panel_mat = panel[0]
+    index_rows = intersection_rows[0, 0]
+    half = index_rows.shape[0] // 2
+    low_idx = index_rows[:half]
+    high_idx = index_rows[half:]
+    kmax = deflation.shape[2]
+    keep = (jnp.arange(kmax, dtype=jnp.int32) < counts[0, 0]).astype(jnp.float32)
+    masked = deflation[0, 0] * keep[:, None]
+
+    def precond(vector):
+        return apply_precond(vector, inv_mats, masked, panel_mat, low_idx, high_idx)
+
+    def operator(vector):
+        return apply_operator(vector, block_mats, couple, low_idx, high_idx)
+
+    norm_sq = lax.psum(jnp.sum(source * source, 0), ("sub", "blk"))
+    beta = jnp.sqrt(norm_sq)
+    basis_one = source / beta
+    search_one, rows_one = precond(basis_one)
+    image = operator(search_one)
+    proj_one, image_sq = lax.psum(
+        (jnp.sum(image * basis_one, 0), jnp.sum(image * image, 0)), ("sub", "blk")
+    )
+    sub_one = jnp.sqrt(image_sq - proj_one * proj_one)
+    basis_two = (image - proj_one * basis_one) / sub_one
+    search_two, rows_two = precond(basis_two)
+    image_two = operator(search_two)
+    proj_two_a, proj_two_b, image_two_sq = lax.psum(
+        (
+            jnp.sum(image_two * basis_one, 0),
+            jnp.sum(image_two * basis_two, 0),
+            jnp.sum(image_two * image_two, 0),
+        ),
+        ("sub", "blk"),
+    )
+    sub_two = jnp.sqrt(image_two_sq - proj_two_a * proj_two_a - proj_two_b * proj_two_b)
+    coeff_one, coeff_two, miss = least_squares(
+        beta, proj_one, sub_one, proj_two_a, proj_two_b, sub_two
+    )
+    solution = coeff_one * search_one + coeff_two * search_two
+    return (solution, miss)
+
+
 def inverse_or_zero(a):
     return jnp.where(a > 0.0, 1.0 / jnp.where(a > 0.0, a, 1.0), 0.0)
 
@@ -333,7 +444,7 @@
     return (coeff_one, coeff_two, miss)
 
 
-def finish_kernel(parts_ref, p_ref, q_ref, out_ref, miss_ref):
+def judge_kernel(parts_ref, rows_ref, ok_ref):
     (beta, len_one, len_two), (cos_01, cos_02, cos_12) = merge(unpacked(parts_ref))
     rel_one = len_one / beta
     proj_one = rel_one * cos_01
@@ -345,10 +456,17 @@
     proj_two_b = rel_two * side - proj_one
     sub_two = rel_two * jnp.sqrt(1.0 - cos_02 * cos_02 - side * side)
     coeff_one, coeff_two, miss = least_squares(beta, proj_one, sub_one, proj_two_a, proj_two_b, sub_two)
-    miss_ref[...] = miss
     second = coeff_two / sub_one
     first = (coeff_one - second * proj_one) / beta
-    out_ref[...] = first * p_ref[...] + (second / beta) * q_ref[...]
+    rows_ref[...] = stacked([first, second / beta, miss])
+    good = jnp.where(first * 0.0 + second * 0.0 + miss * 0.0 == 0.0, 1.0, 0.0)
+    for a in (beta, len_one, len_two):
+        good = jnp.where((a > LEAST) & (a < MOST), good, 0.0)
+    ok_ref[0, 0] = jnp.where(jnp.min(good) > 0.0, 1, 0)
+
+
+def combine_kernel(rows_ref, p_ref, q_ref, out_ref):
+    out_ref[...] = rows_ref[0:1] * p_ref[...] + rows_ref[1:2] * q_ref[...]
 
 
 def shape(*dims, kind=f32):
@@ -450,10 +568,21 @@
     parts = lax.all_to_all(parts, AXES, 0, 0, axis_index_groups=plane)
     parts = call("merge_plane", merge_kernel, shape(len(depth[0]), 1, 6 * ncols), (), (parts,))
     parts = lax.all_to_all(parts, AXES, 0, 0, axis_index_groups=depth)
-    answer, miss = call(
-        "combine", finish_kernel, (shape(nrows, ncols), shape(1, ncols)), (), (parts, search_one, search_two),
-    )
-    return (answer[None, None], miss[0])
+    rows, ok = call(
+        "judge", judge_kernel, (shape(8, ncols), shape(1, 1, kind=jnp.int32)), (), (parts,), out_place=(VMEM, SMEM)
+    )
+
+    def combined(rows, p, q, *_):
+        return call("combine", combine_kernel, shape(nrows, ncols), (), (rows, p, q)), rows[2]
+
+    def normalised(rows, p, q, *args):
+        return normalised_solve(*args)
+
+    answer, miss = lax.cond(
+        ok[0, 0] == 1, combined, normalised, rows, search_one, search_two, rhs, blocks, coupling, inverse,
+        deflation, counts, panel, intersection_rows,
+    )
+    return (answer[None, None], miss)
 
 
 def sum_groups(mesh):

time: 99.7 us -> 105 us (1.053)
  blocking collectives: 58.9 us -> 30.9 us
  starting transfers between devices: 26 us -> 42 us
  waiting for transfers between devices: 0.02 us -> 12 us
  Pallas kernels: 12.4 us -> 14.7 us
  local copies, waits for them, and re-layouts: 0.02 us -> 1.7 us
    all_to_all x1 -> x0, blocking collectives: 28.1 us -> none  [body(): parts = lax.all_to_all(parts, AXES, 0, 0, axis_index_groups=depth)]
    all_to_all x0 -> x1, starting transfers between devices: none -> 16 us  [body(): parts = lax.all_to_all(parts, AXES, 0, 0, axis_index_groups=depth)]
    all_to_all x0 -> x1, waiting for transfers between devices: none -> 12 us  [body(): parts = lax.all_to_all(parts, AXES, 0, 0, axis_index_groups=depth)]
    pallas_call x9 -> x10, Pallas kernels: 12.4 us -> 14.7 us  [call(): pl.pallas_call(kernel, out_shape=out_shape, in_specs=[SMEM] * len(scalars...]
  transfers between devices with their start and end apart: 8 -> 9, of which waited for: 0 -> 1; matrix products, arithmetic and copies ran while one was open for 0% -> 0% of each run, Pallas kernels for 4% -> 5%
where the time goes in v4:
time: 105 us; the launch traced here: 104 us
  starting transfers between devices  42 us (40%)
  blocking collectives  30.9 us (29%)
  Pallas kernels  14.7 us (14%)
  waiting for transfers between devices  12 us (11%)
  between operations  2.13 us (2%)
  local copies, waits for them, and re-layouts  1.7 us (2%)
    all_to_all x1, starting transfers between devices, body(): parts = lax.all_to_all(parts, AXES, 0, 0, axis_index_groups=depth)  16 us
    all_to_all x2, blocking collectives, precond(): coefs = lax.all_to_all(coef, 'blk', 0, 0)  15.5 us
    all_to_all x1, blocking collectives, body(): parts = lax.all_to_all(parts, AXES, 0, 0, axis_index_groups=plane)  15.4 us
    ppermute x4, starting transfers between devices, halo(): far = lax.ppermute(far, 'sub', far_pairs)  15.4 us
    pallas_call x10, Pallas kernels, call(): pl.pallas_call(kernel, out_shape=out_shape, in_specs=[SMEM] * len(scalars...  14.7 us
    all_to_all x1, waiting for transfers between devices, body(): parts = lax.all_to_all(parts, AXES, 0, 0, axis_index_groups=depth)  12 us
    ppermute x4, starting transfers between devices, halo(): return (far, lax.ppermute(near, 'sub', near_pairs))  10.6 us
  transfers between devices with their start and end apart: 9, of which 1 were waited for; matrix products, arithmetic and copies ran while one was open for 0% of the time, Pallas kernels for 5%

profile of v4, /device:TPU:1, one launch (start us, length us, event | category | flops | bytes accessed | tf_op | source)
XLA Modules:
  0.0 103.7 jit_solution(8811875781212207079)
XLA Ops:
  1.3 0.0 copy-start.11
  1.3 2.4 %first_rows.1 = (f32[384,256]{1,0:T(8,128)S(1)}, f32[384,256]{1,0:T(8,128)S(1)}, f32[4,40,256]{2,1,0:T(8,128)S(1)}, f32[1024,256]{1,0:T(8,128)S(1)}, f32[5,256,2...) custom-call(s32[1,1]{1,0:T(1,128)S(6)} %copy.26.count_ref, ...), custom_call_target="tpu_custom_call" | custom-call | flops 300000000 | bytes 2524160 | tf_op jit(solution)/shard_map/first_rows/pallas_call | solution.py:483
  3.7 4.6 %collective-permute-start.12 = (f32[384,256]{1,0:T(8,128)S(1)}, f32[384,256]{1,0:T(8,128)S(1)}, u32[]{:S(2)}, u32[]{:S(2)}) collective-permute-start(f32[384,256]{1,0:T(8,128)S(1)} %get-tuple-element.75.far_ref.far0_ref), channel_id=1, source_target_pairs={{4,8},{8,4},{12,16},{16,12},{20,24},{24,20},{28,32},{32,28},{36,40... | collective-permute-start | bytes 1179656 | tf_op jit(solution)/shard_map/ppermute | solution.py:510
  8.3 4.9 %collective-permute-start.13 = (f32[384,256]{1,0:T(8,128)S(1)}, f32[384,256]{1,0:T(8,128)S(1)}, u32[]{:S(2)}, u32[]{:S(2)}) collective-permute-start(f32[384,256]{1,0:T(8,128)S(1)} %get-tuple-element.76.near_ref.near0_ref), channel_id=1, source_target_pairs={{0,4},{4,0},{8,12},{12,8},{16,20},{20,16},{24,28},{28,24},{32,36},... | collective-permute-start | bytes 1179656 | tf_op jit(solution)/shard_map/ppermute | solution.py:511
  13.2 8.1 %all_to_all.20.all_ref = f32[4,40,256]{2,1,0:T(8,128)S(1)} all-to-all(f32[4,40,256]{2,1,0:T(8,128)S(1)} %get-tuple-element.78), channel_id=1, replica_groups=mesh['sub'=128,'blk'=4] {'blk'}, dimensions={0} | all-to-all | bytes 327680 | tf_op jit(solution)/shard_map/all_to_all | solution.py:514
  21.3 0.0 collective-permute-done.12.gfar_ref.inv_far_ref
  21.3 0.0 collective-permute-done.13.gnear_ref.inv_near_ref
  21.3 0.0 copy-done.11
  21.3 0.0 copy-start.3
  21.3 1.5 %local_solve.2 = (f32[1024,256]{1,0:T(8,128)S(1)}, f32[256,256]{1,0:T(8,128)S(1)}, bf16[128,256]{1,0:T(8,128)(2,1)S(1)}, f32[128,256]{1,0:T(8,128)S(1)}, f32[128,256]{1,0:T(8,128)S(1)}) custom-call(s32[1]{0:T(128)} %bitcast.35.odd_ref, s32[1]{0:T(128)} %bitcast.36.slot_ref, f32[1024,256]{1,0:T(8,128)S(1)} %get-tuple-element.74.r_ref.u0_ref, ...), custom_call_target="tpu_custom_call" | custom-call | flops 1000000000 | bytes 6557696 | tf_op jit(solution)/shard_map/local_solve/pallas_call | solution.py:483
  22.9 2.7 %collective-permute-start.14 = (f32[128,256]{1,0:T(8,128)S(1)}, f32[128,256]{1,0:T(8,128)S(1)}, u32[]{:S(2)}, u32[]{:S(2)}) collective-permute-start(f32[128,256]{1,0:T(8,128)S(1)} %get-tuple-element.89), channel_id=1, source_target_pairs={{4,8},{8,4},{12,16},{16,12},{20,24},{24,20},{28,32},{32,28},{36,40... | collective-permute-start | bytes 393224 | tf_op jit(solution)/shard_map/ppermute | solution.py:510
  25.6 1.9 %collective-permute-start.15 = (f32[128,256]{1,0:T(8,128)S(1)}, f32[128,256]{1,0:T(8,128)S(1)}, u32[]{:S(2)}, u32[]{:S(2)}) collective-permute-start(f32[128,256]{1,0:T(8,128)S(1)} %get-tuple-element.90), channel_id=1, source_target_pairs={{0,4},{4,0},{8,12},{12,8},{16,20},{20,16},{24,28},{28,24},{32,36},... | collective-permute-start | bytes 393224 | tf_op jit(solution)/shard_map/ppermute | solution.py:511
  27.5 0.0 copy-done.3
  27.6 0.0 copy-start.9
  27.6 2.0 %block_product.1 = (f32[1024,256]{1,0:T(8,128)}, f32[1024,256]{1,0:T(8,128)S(1)}, f32[256,256]{1,0:T(8,128)S(1)}, f32[48,256]{1,0:T(8,128)S(1)}) custom-call(f32[1024,256]{1,0:T(8,128)S(1)} %get-tuple-element.81.own_ref, f32[256,256]{1,0:T(8,128)S(1)} %get-tuple-element.82.back_ref, bf16[128,256]{1,0:T(8,128)(2,1)S(1)} %get-tuple-element.83.coarse_ref, ...), custom_call_target="tpu_custom_call" | custom-call | flops 1000000000 | bytes 5505024 | tf_op jit(solution)/shard_map/block_product/pallas_call | solution.py:483
  29.5 0.0 collective-permute-done.14.gfar_ref
  29.5 0.0 collective-permute-done.15.gnear_ref
  29.5 0.0 copy-done.9
  29.5 0.8 image.1
  30.3 3.3 %collective-permute-start.16 = (f32[256,256]{1,0:T(8,128)S(1)}, f32[256,256]{1,0:T(8,128)S(1)}, u32[]{:S(2)}, u32[]{:S(2)}) collective-permute-start(f32[256,256]{1,0:T(8,128)S(1)} %get-tuple-element.92.far_ref), channel_id=1, source_target_pairs={{4,8},{8,4},{12,16},{16,12},{20,24},{24,20},{28,32},{32,28},{36,40... | collective-permute-start | bytes 786440 | tf_op jit(solution)/shard_map/ppermute | solution.py:510
  33.6 1.9 %collective-permute-start.17 = (f32[256,256]{1,0:T(8,128)S(1)}, f32[256,256]{1,0:T(8,128)S(1)}, u32[]{:S(2)}, u32[]{:S(2)}) collective-permute-start(f32[256,256]{1,0:T(8,128)S(1)} %get-tuple-element.93.near_ref), channel_id=1, source_target_pairs={{0,4},{4,0},{8,12},{12,8},{16,20},{20,16},{24,28},{28,24},{32,36},... | collective-permute-start | bytes 786440 | tf_op jit(solution)/shard_map/ppermute | solution.py:511
  35.5 7.4 %all_to_all.21.all_ref = f32[4,40,256]{2,1,0:T(8,128)S(1)} all-to-all(f32[4,40,256]{2,1,0:T(8,128)S(1)} %get-tuple-element.94), channel_id=1, replica_groups=mesh['sub'=128,'blk'=4] {'blk'}, dimensions={0} | all-to-all | bytes 327680 | tf_op jit(solution)/shard_map/all_to_all | solution.py:514
  42.9 0.0 collective-permute-done.16.gfar_ref
  42.9 0.0 collective-permute-done.17.gnear_ref
  42.9 1.5 %local_solve.3 = (f32[1024,256]{1,0:T(8,128)S(1)}, f32[256,256]{1,0:T(8,128)S(1)}, bf16[128,256]{1,0:T(8,128)(2,1)S(1)}, f32[128,256]{1,0:T(8,128)S(1)}, f32[128,256]{1,0:T(8,128)S(1)}) custom-call(s32[1]{0:T(128)} %bitcast.35.odd_ref, s32[1]{0:T(128)} %bitcast.36.slot_ref, f32[1024,256]{1,0:T(8,128)S(1)} %get-tuple-element.91.r_ref.u1_ref, ...), custom_call_target="tpu_custom_call" | custom-call | flops 1000000000 | bytes 6033408 | tf_op jit(solution)/shard_map/local_solve/pallas_call | solution.py:483
  44.4 4.7 %collective-permute-start.18 = (f32[128,256]{1,0:T(8,128)S(1)}, f32[128,256]{1,0:T(8,128)S(1)}, u32[]{:S(2)}, u32[]{:S(2)}) collective-permute-start(f32[128,256]{1,0:T(8,128)S(1)} %get-tuple-element.101), channel_id=1, source_target_pairs={{4,8},{8,4},{12,16},{16,12},{20,24},{24,20},{28,32},{32,28},{36,40... | collective-permute-start | bytes 393224 | tf_op jit(solution)/shard_map/ppermute | solution.py:510
  49.1 1.9 %collective-permute-start.19 = (f32[128,256]{1,0:T(8,128)S(1)}, f32[128,256]{1,0:T(8,128)S(1)}, u32[]{:S(2)}, u32[]{:S(2)}) collective-permute-start(f32[128,256]{1,0:T(8,128)S(1)} %get-tuple-element.102), channel_id=1, source_target_pairs={{0,4},{4,0},{8,12},{12,8},{16,20},{20,16},{24,28},{28,24},{32,36},... | collective-permute-start | bytes 393224 | tf_op jit(solution)/shard_map/ppermute | solution.py:511
  51.1 3.0 %last_block_product.1 = (f32[1024,256]{1,0:T(8,128)}, f32[256,256]{1,0:T(8,128)S(1)}, f32[256,256]{1,0:T(8,128)S(1)}, f32[256,256]{1,0:T(8,128)S(1)}, f32[8,256]{1,0:T(8,128)S(1)}) custom-call(f32[1024,256]{1,0:T(8,128)S(1)} %get-tuple-element.95.own_ref, f32[256,256]{1,0:T(8,128)S(1)} %get-tuple-element.96.back_ref, ...), custom_call_target="tpu_custom_call" | custom-call | flops 1000000000 | bytes 9175040 | tf_op jit(solution)/shard_map/last_block_product/pallas_call | solution.py:483
  54.0 0.0 copy-start
  54.0 0.0 copy-start.4
  54.0 0.0 copy-start.18
  54.0 0.0 collective-permute-done.18.gfar_ref
  54.0 0.0 collective-permute-done.19.gnear_ref
  54.1 0.4 lengths_cosines.1
  54.5 15.4 %all_to_all.22.parts_ref = f32[32,1,1536]{2,1,0:T(1,128)S(1)} all-to-all(f32[32,1,1536]{2,1,0:T(1,128)S(1)} %lengths_cosines.1), channel_id=1, replica_groups={{0,1,2,3,4,5,6,7,8,9,10,11,12,13,14,15,16,17,18,19,20,21,22,23,24,25,26..., dimensions={0} | all-to-all | bytes 393216 | tf_op jit(solution)/shard_map/all_to_all | solution.py:568
  69.8 0.8 merge_plane.1
  70.6 16.0 %all-to-all-start.3 = ((f32[16,1,1536]{2,1,0:T(1,128)}), f32[16,1,1536]{2,1,0:T(1,128)S(1)}, u32[]{:S(2)}, u32[]{:S(2)}) async-start(f32[16,1,1536]{2,1,0:T(1,128)} %merge_plane.1), calls=%async_computation.3 | async-start | bytes 196608 | tf_op jit(solution)/shard_map/all_to_all | solution.py:570
  86.6 12.0 %all-to-all-done.3.parts_ref = f32[16,1,1536]{2,1,0:T(1,128)S(1)} async-done(((f32[16,1,1536]{2,1,0:T(1,128)}), f32[16,1,1536]{2,1,0:T(1,128)S(1)}, u32[]{:S(2)}, u32[]{:S(2)}) %all-to-all-start.3) | async-done | bytes 98336 | tf_op jit(solution)/shard_map/all_to_all | solution.py:570
  98.6 0.8 judge.1
  100.1 0.0 copy-done
  100.1 0.0 copy-done.4
  100.1 0.0 copy-done.18
  100.1 2.6 %conditional.1 = (f32[256]{0:T(256)S(1)}, f32[1,1,1024,256]{3,2,1,0:T(8,128)S(1)}) conditional(s32[]{:T(128)} %bitcast.44, (f32[1,1,1024,256]{3,2,1,0:T(8,128)S(1)}, s32[1,1,256]{2,1,0:T(1,128)S(1)}, f32[1,1,5,256,256]{4,3,2,1,0:T(8,128)S(1)}, f32[1,1,40,1024]{3,2,1,0:T(8,128)}, s32[1,1]{1,0:T(1,128)}, /*index=5*/f32[1,160,160]{2,1,0:T(8,128)}, ...), branch_computations={%region_0.0_spmd, %region_21.0_spmd} | conditional | flops 4376148992 | bytes 77315704 | solution.py:581
  100.3 1.7 %combine.1 = f32[1024,256]{1,0:T(8,128)S(1)} custom-call(f32[8,256]{1,0:T(8,128)} %get-tuple-element.31.rows_ref, f32[1024,256]{1,0:T(8,128)} %get-tuple-element.32.p_ref, f32[1024,256]{1,0:T(8,128)} %get-tuple-element.33.q_ref), custom_call_target="tpu_custom_call" | custom-call | bytes 2105344 | tf_op jit(solution)/shard_map/cond/branch_1_fun/combine/pallas_call | solution.py:483
  102.0 0.7 slice.42
  102.7 0.0 copy-start.10
  102.7 0.0 copy-start.21
  102.7 1.0 copy-done.10
  103.7 0.0 copy-done.21
Async XLA Ops:
  1.3 20.0 %copy-start.11 = (f32[1,160,160]{2,1,0:T(8,128)S(1)}, f32[1,160,160]{2,1,0:T(8,128)}, u32[]{:S(2)}) copy-start(f32[1,160,160]{2,1,0:T(8,128)} %param.16) | copy-start | bytes 307204
  3.7 17.6 %collective-permute-start.12 = (f32[384,256]{1,0:T(8,128)S(1)}, f32[384,256]{1,0:T(8,128)S(1)}, u32[]{:S(2)}, u32[]{:S(2)}) collective-permute-start(f32[384,256]{1,0:T(8,128)S(1)} %get-tuple-element.75.far_ref.far0_ref), channel_id=1, source_target_pairs={{4,8},{8,4},{12,16},{16,12},{20,24},{24,20},{28,32},{32,28},{36,40... | collective-permute-start | bytes 1179656 | tf_op jit(solution)/shard_map/ppermute | solution.py:510
  8.3 13.0 %collective-permute-start.13 = (f32[384,256]{1,0:T(8,128)S(1)}, f32[384,256]{1,0:T(8,128)S(1)}, u32[]{:S(2)}, u32[]{:S(2)}) collective-permute-start(f32[384,256]{1,0:T(8,128)S(1)} %get-tuple-element.76.near_ref.near0_ref), channel_id=1, source_target_pairs={{0,4},{4,0},{8,12},{12,8},{16,20},{20,16},{24,28},{28,24},{32,36},... | collective-permute-start | bytes 1179656 | tf_op jit(solution)/shard_map/ppermute | solution.py:511
  21.3 6.2 %copy-start.3 = (f32[1,1,4,256,256]{4,3,2,1,0:T(8,128)S(1)}, f32[1,1,4,256,256]{4,3,2,1,0:T(8,128)}, u32[]{:S(2)}) copy-start(f32[1,1,4,256,256]{4,3,2,1,0:T(8,128)} %param.11) | copy-start | bytes 3145732
  22.9 6.7 %collective-permute-start.14 = (f32[128,256]{1,0:T(8,128)S(1)}, f32[128,256]{1,0:T(8,128)S(1)}, u32[]{:S(2)}, u32[]{:S(2)}) collective-permute-start(f32[128,256]{1,0:T(8,128)S(1)} %get-tuple-element.89), channel_id=1, source_target_pairs={{4,8},{8,4},{12,16},{16,12},{20,24},{24,20},{28,32},{32,28},{36,40... | collective-permute-start | bytes 393224 | tf_op jit(solution)/shard_map/ppermute | solution.py:510
  25.6 3.9 %collective-permute-start.15 = (f32[128,256]{1,0:T(8,128)S(1)}, f32[128,256]{1,0:T(8,128)S(1)}, u32[]{:S(2)}, u32[]{:S(2)}) collective-permute-start(f32[128,256]{1,0:T(8,128)S(1)} %get-tuple-element.90), channel_id=1, source_target_pairs={{0,4},{4,0},{8,12},{12,8},{16,20},{20,16},{24,28},{28,24},{32,36},... | collective-permute-start | bytes 393224 | tf_op jit(solution)/shard_map/ppermute | solution.py:511
  27.6 2.0 %copy-start.9 = (f32[1,1,2,128,128]{4,3,2,1,0:T(8,128)S(1)}, f32[1,1,2,128,128]{4,3,2,1,0:T(8,128)}, u32[]{:S(2)}) copy-start(f32[1,1,2,128,128]{4,3,2,1,0:T(8,128)} %param.12) | copy-start | bytes 393220
  30.3 12.6 %collective-permute-start.16 = (f32[256,256]{1,0:T(8,128)S(1)}, f32[256,256]{1,0:T(8,128)S(1)}, u32[]{:S(2)}, u32[]{:S(2)}) collective-permute-start(f32[256,256]{1,0:T(8,128)S(1)} %get-tuple-element.92.far_ref), channel_id=1, source_target_pairs={{4,8},{8,4},{12,16},{16,12},{20,24},{24,20},{28,32},{32,28},{36,40... | collective-permute-start | bytes 786440 | tf_op jit(solution)/shard_map/ppermute | solution.py:510
  33.6 9.3 %collective-permute-start.17 = (f32[256,256]{1,0:T(8,128)S(1)}, f32[256,256]{1,0:T(8,128)S(1)}, u32[]{:S(2)}, u32[]{:S(2)}) collective-permute-start(f32[256,256]{1,0:T(8,128)S(1)} %get-tuple-element.93.near_ref), channel_id=1, source_target_pairs={{0,4},{4,0},{8,12},{12,8},{16,20},{20,16},{24,28},{28,24},{32,36},... | collective-permute-start | bytes 786440 | tf_op jit(solution)/shard_map/ppermute | solution.py:511
  44.4 9.6 %collective-permute-start.18 = (f32[128,256]{1,0:T(8,128)S(1)}, f32[128,256]{1,0:T(8,128)S(1)}, u32[]{:S(2)}, u32[]{:S(2)}) collective-permute-start(f32[128,256]{1,0:T(8,128)S(1)} %get-tuple-element.101), channel_id=1, source_target_pairs={{4,8},{8,4},{12,16},{16,12},{20,24},{24,20},{28,32},{32,28},{36,40... | collective-permute-start | bytes 393224 | tf_op jit(solution)/shard_map/ppermute | solution.py:510
  49.1 4.9 %collective-permute-start.19 = (f32[128,256]{1,0:T(8,128)S(1)}, f32[128,256]{1,0:T(8,128)S(1)}, u32[]{:S(2)}, u32[]{:S(2)}) collective-permute-start(f32[128,256]{1,0:T(8,128)S(1)} %get-tuple-element.102), channel_id=1, source_target_pairs={{0,4},{4,0},{8,12},{12,8},{16,20},{20,16},{24,28},{28,24},{32,36},... | collective-permute-start | bytes 393224 | tf_op jit(solution)/shard_map/ppermute | solution.py:511
  54.0 46.0 %copy-start = (f32[1,1,1024,256]{3,2,1,0:T(8,128)S(1)}, f32[1,1,1024,256]{3,2,1,0:T(8,128)}, u32[]{:S(2)}) copy-start(f32[1,1,1024,256]{3,2,1,0:T(8,128)} %param.10) | copy-start | bytes 3145732
  54.0 46.0 %copy-start.4 = (f32[1,1,5,256,256]{4,3,2,1,0:T(8,128)S(1)}, f32[1,1,5,256,256]{4,3,2,1,0:T(8,128)}, u32[]{:S(2)}) copy-start(f32[1,1,5,256,256]{4,3,2,1,0:T(8,128)} %param.13) | copy-start | bytes 3932164
  54.0 46.0 %copy-start.18 = (s32[1,1,256]{2,1,0:T(1,128)S(1)}, s32[1,1,256]{2,1,0:T(1,128)}, u32[]{:S(2)}) copy-start(s32[1,1,256]{2,1,0:T(1,128)} %param.17) | copy-start | bytes 3076
  70.6 28.0 %all-to-all-start.3 = ((f32[16,1,1536]{2,1,0:T(1,128)}), f32[16,1,1536]{2,1,0:T(1,128)S(1)}, u32[]{:S(2)}, u32[]{:S(2)}) async-start(f32[16,1,1536]{2,1,0:T(1,128)} %merge_plane.1), calls=%async_computation.3 | async-start | bytes 196608 | tf_op jit(solution)/shard_map/all_to_all | solution.py:570
  102.7 1.0 copy-start.10
  102.7 1.0 copy-start.21

commit v5 on v4

--- a/solution.py
+++ b/solution.py
@@ -326,7 +326,7 @@
         beta, proj_one, sub_one, proj_two_a, proj_two_b, sub_two
     )
     solution = coeff_one * search_one + coeff_two * search_two
-    return (solution, miss)
+    return (solution, miss[None])
 
 
 def inverse_or_zero(a):
@@ -465,7 +465,8 @@
     ok_ref[0, 0] = jnp.where(jnp.min(good) > 0.0, 1, 0)
 
 
-def combine_kernel(rows_ref, p_ref, q_ref, out_ref):
+def combine_kernel(rows_ref, p_ref, q_ref, out_ref, miss_ref):
+    miss_ref[...] = rows_ref[2:3]
     out_ref[...] = rows_ref[0:1] * p_ref[...] + rows_ref[1:2] * q_ref[...]
 
 
@@ -573,7 +574,7 @@
     )
 
     def combined(rows, p, q, *_):
-        return call("combine", combine_kernel, shape(nrows, ncols), (), (rows, p, q)), rows[2]
+        return call("combine", combine_kernel, (shape(nrows, ncols), shape(1, ncols)), (), (rows, p, q))
 
     def normalised(rows, p, q, *args):
         return normalised_solve(*args)
@@ -582,7 +583,7 @@
         ok[0, 0] == 1, combined, normalised, rows, search_one, search_two, rhs, blocks, coupling, inverse,
         deflation, counts, panel, intersection_rows,
     )
-    return (answer[None, None], miss)
+    return (answer[None, None], miss[0])
 
 
 def sum_groups(mesh):

time: 105 us -> 104 us (level)
  local copies, waits for them, and re-layouts: 1.7 us -> 0.03 us
where the time goes in v5:
time: 104 us; the launch traced here: 103 us
  starting transfers between devices  42 us (40%)
  blocking collectives  30.9 us (30%)
  Pallas kernels  15.7 us (15%)
  waiting for transfers between devices  12 us (12%)
  between operations  2.12 us (2%)
    all_to_all x1, starting transfers between devices, body(): parts = lax.all_to_all(parts, AXES, 0, 0, axis_index_groups=depth)  16 us
    pallas_call x10, Pallas kernels, call(): pl.pallas_call(kernel, out_shape=out_shape, in_specs=[SMEM] * len(scalars...  15.7 us
    all_to_all x2, blocking collectives, precond(): coefs = lax.all_to_all(coef, 'blk', 0, 0)  15.5 us
    all_to_all x1, blocking collectives, body(): parts = lax.all_to_all(parts, AXES, 0, 0, axis_index_groups=plane)  15.4 us
    ppermute x4, starting transfers between devices, halo(): far = lax.ppermute(far, 'sub', far_pairs)  15.4 us
    all_to_all x1, waiting for transfers between devices, body(): parts = lax.all_to_all(parts, AXES, 0, 0, axis_index_groups=depth)  12 us
    ppermute x4, starting transfers between devices, halo(): return (far, lax.ppermute(near, 'sub', near_pairs))  10.6 us
  transfers between devices with their start and end apart: 9, of which 1 were waited for; matrix products, arithmetic and copies ran while one was open for 0% of the time, Pallas kernels for 5%

profile of v5, /device:TPU:1, one launch (start us, length us, event | category | flops | bytes accessed | tf_op | source)
XLA Modules:
  0.0 103.0 jit_solution(7231088279454766688)
XLA Ops:
  1.3 0.0 copy-start.10
  1.3 2.4 %first_rows.1 = (f32[384,256]{1,0:T(8,128)S(1)}, f32[384,256]{1,0:T(8,128)S(1)}, f32[4,40,256]{2,1,0:T(8,128)S(1)}, f32[1024,256]{1,0:T(8,128)S(1)}, f32[5,256,2...) custom-call(s32[1,1]{1,0:T(1,128)S(6)} %copy.30.count_ref, ...), custom_call_target="tpu_custom_call" | custom-call | flops 300000000 | bytes 2524160 | tf_op jit(solution)/shard_map/first_rows/pallas_call | solution.py:484
  3.7 4.6 %collective-permute-start.12 = (f32[384,256]{1,0:T(8,128)S(1)}, f32[384,256]{1,0:T(8,128)S(1)}, u32[]{:S(2)}, u32[]{:S(2)}) collective-permute-start(f32[384,256]{1,0:T(8,128)S(1)} %get-tuple-element.78.far_ref.far0_ref), channel_id=1, source_target_pairs={{4,8},{8,4},{12,16},{16,12},{20,24},{24,20},{28,32},{32,28},{36,40... | collective-permute-start | bytes 1179656 | tf_op jit(solution)/shard_map/ppermute | solution.py:511
  8.3 4.9 %collective-permute-start.13 = (f32[384,256]{1,0:T(8,128)S(1)}, f32[384,256]{1,0:T(8,128)S(1)}, u32[]{:S(2)}, u32[]{:S(2)}) collective-permute-start(f32[384,256]{1,0:T(8,128)S(1)} %get-tuple-element.79.near_ref.near0_ref), channel_id=1, source_target_pairs={{0,4},{4,0},{8,12},{12,8},{16,20},{20,16},{24,28},{28,24},{32,36},... | collective-permute-start | bytes 1179656 | tf_op jit(solution)/shard_map/ppermute | solution.py:512
  13.2 8.1 %all_to_all.20.all_ref = f32[4,40,256]{2,1,0:T(8,128)S(1)} all-to-all(f32[4,40,256]{2,1,0:T(8,128)S(1)} %get-tuple-element.81), channel_id=1, replica_groups=mesh['sub'=128,'blk'=4] {'blk'}, dimensions={0} | all-to-all | bytes 327680 | tf_op jit(solution)/shard_map/all_to_all | solution.py:515
  21.3 0.0 collective-permute-done.12.gfar_ref.inv_far_ref
  21.3 0.0 collective-permute-done.13.gnear_ref.inv_near_ref
  21.3 0.0 copy-done.10
  21.3 0.0 copy-start.3
  21.3 1.5 %local_solve.2 = (f32[1024,256]{1,0:T(8,128)S(1)}, f32[256,256]{1,0:T(8,128)S(1)}, bf16[128,256]{1,0:T(8,128)(2,1)S(1)}, f32[128,256]{1,0:T(8,128)S(1)}, f32[128,256]{1,0:T(8,128)S(1)}) custom-call(s32[1]{0:T(128)} %bitcast.35.odd_ref, s32[1]{0:T(128)} %bitcast.36.slot_ref, f32[1024,256]{1,0:T(8,128)S(1)} %get-tuple-element.77.r_ref.u0_ref, ...), custom_call_target="tpu_custom_call" | custom-call | flops 1000000000 | bytes 6557696 | tf_op jit(solution)/shard_map/local_solve/pallas_call | solution.py:484
  22.9 2.7 %collective-permute-start.14 = (f32[128,256]{1,0:T(8,128)S(1)}, f32[128,256]{1,0:T(8,128)S(1)}, u32[]{:S(2)}, u32[]{:S(2)}) collective-permute-start(f32[128,256]{1,0:T(8,128)S(1)} %get-tuple-element.92), channel_id=1, source_target_pairs={{4,8},{8,4},{12,16},{16,12},{20,24},{24,20},{28,32},{32,28},{36,40... | collective-permute-start | bytes 393224 | tf_op jit(solution)/shard_map/ppermute | solution.py:511
  25.6 1.9 %collective-permute-start.15 = (f32[128,256]{1,0:T(8,128)S(1)}, f32[128,256]{1,0:T(8,128)S(1)}, u32[]{:S(2)}, u32[]{:S(2)}) collective-permute-start(f32[128,256]{1,0:T(8,128)S(1)} %get-tuple-element.93), channel_id=1, source_target_pairs={{0,4},{4,0},{8,12},{12,8},{16,20},{20,16},{24,28},{28,24},{32,36},... | collective-permute-start | bytes 393224 | tf_op jit(solution)/shard_map/ppermute | solution.py:512
  27.5 0.0 copy-done.3
  27.6 0.0 copy-start.9
  27.6 1.9 %block_product.1 = (f32[1024,256]{1,0:T(8,128)}, f32[1024,256]{1,0:T(8,128)S(1)}, f32[256,256]{1,0:T(8,128)S(1)}, f32[48,256]{1,0:T(8,128)S(1)}) custom-call(f32[1024,256]{1,0:T(8,128)S(1)} %get-tuple-element.84.own_ref, f32[256,256]{1,0:T(8,128)S(1)} %get-tuple-element.85.back_ref, bf16[128,256]{1,0:T(8,128)(2,1)S(1)} %get-tuple-element.86.coarse_ref, ...), custom_call_target="tpu_custom_call" | custom-call | flops 1000000000 | bytes 5505024 | tf_op jit(solution)/shard_map/block_product/pallas_call | solution.py:484
  29.5 0.0 collective-permute-done.14.gfar_ref
  29.5 0.0 collective-permute-done.15.gnear_ref
  29.5 0.0 copy-done.9
  29.5 0.8 image.1
  30.3 3.3 %collective-permute-start.16 = (f32[256,256]{1,0:T(8,128)S(1)}, f32[256,256]{1,0:T(8,128)S(1)}, u32[]{:S(2)}, u32[]{:S(2)}) collective-permute-start(f32[256,256]{1,0:T(8,128)S(1)} %get-tuple-element.95.far_ref), channel_id=1, source_target_pairs={{4,8},{8,4},{12,16},{16,12},{20,24},{24,20},{28,32},{32,28},{36,40... | collective-permute-start | bytes 786440 | tf_op jit(solution)/shard_map/ppermute | solution.py:511
  33.6 1.9 %collective-permute-start.17 = (f32[256,256]{1,0:T(8,128)S(1)}, f32[256,256]{1,0:T(8,128)S(1)}, u32[]{:S(2)}, u32[]{:S(2)}) collective-permute-start(f32[256,256]{1,0:T(8,128)S(1)} %get-tuple-element.96.near_ref), channel_id=1, source_target_pairs={{0,4},{4,0},{8,12},{12,8},{16,20},{20,16},{24,28},{28,24},{32,36},... | collective-permute-start | bytes 786440 | tf_op jit(solution)/shard_map/ppermute | solution.py:512
  35.5 7.4 %all_to_all.21.all_ref = f32[4,40,256]{2,1,0:T(8,128)S(1)} all-to-all(f32[4,40,256]{2,1,0:T(8,128)S(1)} %get-tuple-element.97), channel_id=1, replica_groups=mesh['sub'=128,'blk'=4] {'blk'}, dimensions={0} | all-to-all | bytes 327680 | tf_op jit(solution)/shard_map/all_to_all | solution.py:515
  42.9 0.0 collective-permute-done.16.gfar_ref
  42.9 0.0 collective-permute-done.17.gnear_ref
  42.9 1.5 %local_solve.3 = (f32[1024,256]{1,0:T(8,128)S(1)}, f32[256,256]{1,0:T(8,128)S(1)}, bf16[128,256]{1,0:T(8,128)(2,1)S(1)}, f32[128,256]{1,0:T(8,128)S(1)}, f32[128,256]{1,0:T(8,128)S(1)}) custom-call(s32[1]{0:T(128)} %bitcast.35.odd_ref, s32[1]{0:T(128)} %bitcast.36.slot_ref, f32[1024,256]{1,0:T(8,128)S(1)} %get-tuple-element.94.r_ref.u1_ref, ...), custom_call_target="tpu_custom_call" | custom-call | flops 1000000000 | bytes 6033408 | tf_op jit(solution)/shard_map/local_solve/pallas_call | solution.py:484
  44.4 4.7 %collective-permute-start.18 = (f32[128,256]{1,0:T(8,128)S(1)}, f32[128,256]{1,0:T(8,128)S(1)}, u32[]{:S(2)}, u32[]{:S(2)}) collective-permute-start(f32[128,256]{1,0:T(8,128)S(1)} %get-tuple-element.104), channel_id=1, source_target_pairs={{4,8},{8,4},{12,16},{16,12},{20,24},{24,20},{28,32},{32,28},{36,40... | collective-permute-start | bytes 393224 | tf_op jit(solution)/shard_map/ppermute | solution.py:511
  49.1 1.9 %collective-permute-start.19 = (f32[128,256]{1,0:T(8,128)S(1)}, f32[128,256]{1,0:T(8,128)S(1)}, u32[]{:S(2)}, u32[]{:S(2)}) collective-permute-start(f32[128,256]{1,0:T(8,128)S(1)} %get-tuple-element.105), channel_id=1, source_target_pairs={{0,4},{4,0},{8,12},{12,8},{16,20},{20,16},{24,28},{28,24},{32,36},... | collective-permute-start | bytes 393224 | tf_op jit(solution)/shard_map/ppermute | solution.py:512
  51.1 3.0 %last_block_product.1 = (f32[1024,256]{1,0:T(8,128)}, f32[256,256]{1,0:T(8,128)S(1)}, f32[256,256]{1,0:T(8,128)S(1)}, f32[256,256]{1,0:T(8,128)S(1)}, f32[8,256]{1,0:T(8,128)S(1)}) custom-call(f32[1024,256]{1,0:T(8,128)S(1)} %get-tuple-element.98.own_ref, f32[256,256]{1,0:T(8,128)S(1)} %get-tuple-element.99.back_ref, ...), custom_call_target="tpu_custom_call" | custom-call | flops 1000000000 | bytes 9175040 | tf_op jit(solution)/shard_map/last_block_product/pallas_call | solution.py:484
  54.1 0.0 copy-start
  54.1 0.0 copy-start.4
  54.1 0.0 copy-start.17
  54.1 0.0 collective-permute-done.18.gfar_ref
  54.1 0.0 collective-permute-done.19.gnear_ref
  54.1 0.4 lengths_cosines.1
  54.5 15.4 %all_to_all.22.parts_ref = f32[32,1,1536]{2,1,0:T(1,128)S(1)} all-to-all(f32[32,1,1536]{2,1,0:T(1,128)S(1)} %lengths_cosines.1), channel_id=1, replica_groups={{0,1,2,3,4,5,6,7,8,9,10,11,12,13,14,15,16,17,18,19,20,21,22,23,24,25,26..., dimensions={0} | all-to-all | bytes 393216 | tf_op jit(solution)/shard_map/all_to_all | solution.py:569
  69.9 0.8 merge_plane.1
  70.7 16.0 %all-to-all-start.3 = ((f32[16,1,1536]{2,1,0:T(1,128)}), f32[16,1,1536]{2,1,0:T(1,128)S(1)}, u32[]{:S(2)}, u32[]{:S(2)}) async-start(f32[16,1,1536]{2,1,0:T(1,128)} %merge_plane.1), calls=%async_computation.3 | async-start | bytes 196608 | tf_op jit(solution)/shard_map/all_to_all | solution.py:571
  86.7 12.0 %all-to-all-done.3.parts_ref = f32[16,1,1536]{2,1,0:T(1,128)S(1)} async-done(((f32[16,1,1536]{2,1,0:T(1,128)}), f32[16,1,1536]{2,1,0:T(1,128)S(1)}, u32[]{:S(2)}, u32[]{:S(2)}) %all-to-all-start.3) | async-done | bytes 98336 | tf_op jit(solution)/shard_map/all_to_all | solution.py:571
  98.7 0.8 judge.1
  100.1 0.0 copy-done
  100.1 0.0 copy-done.4
  100.1 0.0 copy-done.17
  100.1 2.9 %conditional.1 = (f32[1,1,1024,256]{3,2,1,0:T(8,128)}, f32[256]{0:T(256)}) conditional(s32[]{:T(128)} %bitcast.44, (f32[1,1,1024,256]{3,2,1,0:T(8,128)S(1)}, s32[1,1,256]{2,1,0:T(1,128)S(1)}, f32[1,1,5,256,256]{4,3,2,1,0:T(8,128)S(1)}, f32[1,1,40,1024]{3,2,1,0:T(8,128)}, s32[1,1]{1,0:T(1,128)}, /*index=5*/f32[1,160,160]{2,1,0:T(8,128)}, ...), branch_computations={%region_0.0_spmd, %region_21.0_spmd} | conditional | flops 4376148992 | bytes 77315704 | solution.py:582
  100.4 2.6 %combine.1 = (f32[1024,256]{1,0:T(8,128)}, f32[1,256]{1,0:T(1,128)}) custom-call(f32[8,256]{1,0:T(8,128)} %get-tuple-element.34.rows_ref, f32[1024,256]{1,0:T(8,128)} %get-tuple-element.35.p_ref, f32[1024,256]{1,0:T(8,128)} %get-tuple-element.36.q_ref), custom_call_target="tpu_custom_call" | custom-call | bytes 2105344 | tf_op jit(solution)/shard_map/cond/branch_1_fun/combine/pallas_call | solution.py:484
Async XLA Ops:
  1.3 20.0 %copy-start.10 = (f32[1,160,160]{2,1,0:T(8,128)S(1)}, f32[1,160,160]{2,1,0:T(8,128)}, u32[]{:S(2)}) copy-start(f32[1,160,160]{2,1,0:T(8,128)} %param.16) | copy-start | bytes 307204
  3.7 17.6 %collective-permute-start.12 = (f32[384,256]{1,0:T(8,128)S(1)}, f32[384,256]{1,0:T(8,128)S(1)}, u32[]{:S(2)}, u32[]{:S(2)}) collective-permute-start(f32[384,256]{1,0:T(8,128)S(1)} %get-tuple-element.78.far_ref.far0_ref), channel_id=1, source_target_pairs={{4,8},{8,4},{12,16},{16,12},{20,24},{24,20},{28,32},{32,28},{36,40... | collective-permute-start | bytes 1179656 | tf_op jit(solution)/shard_map/ppermute | solution.py:511
  8.3 13.0 %collective-permute-start.13 = (f32[384,256]{1,0:T(8,128)S(1)}, f32[384,256]{1,0:T(8,128)S(1)}, u32[]{:S(2)}, u32[]{:S(2)}) collective-permute-start(f32[384,256]{1,0:T(8,128)S(1)} %get-tuple-element.79.near_ref.near0_ref), channel_id=1, source_target_pairs={{0,4},{4,0},{8,12},{12,8},{16,20},{20,16},{24,28},{28,24},{32,36},... | collective-permute-start | bytes 1179656 | tf_op jit(solution)/shard_map/ppermute | solution.py:512
  21.3 6.2 %copy-start.3 = (f32[1,1,4,256,256]{4,3,2,1,0:T(8,128)S(1)}, f32[1,1,4,256,256]{4,3,2,1,0:T(8,128)}, u32[]{:S(2)}) copy-start(f32[1,1,4,256,256]{4,3,2,1,0:T(8,128)} %param.11) | copy-start | bytes 3145732
  22.9 6.7 %collective-permute-start.14 = (f32[128,256]{1,0:T(8,128)S(1)}, f32[128,256]{1,0:T(8,128)S(1)}, u32[]{:S(2)}, u32[]{:S(2)}) collective-permute-start(f32[128,256]{1,0:T(8,128)S(1)} %get-tuple-element.92), channel_id=1, source_target_pairs={{4,8},{8,4},{12,16},{16,12},{20,24},{24,20},{28,32},{32,28},{36,40... | collective-permute-start | bytes 393224 | tf_op jit(solution)/shard_map/ppermute | solution.py:511
  25.6 3.9 %collective-permute-start.15 = (f32[128,256]{1,0:T(8,128)S(1)}, f32[128,256]{1,0:T(8,128)S(1)}, u32[]{:S(2)}, u32[]{:S(2)}) collective-permute-start(f32[128,256]{1,0:T(8,128)S(1)} %get-tuple-element.93), channel_id=1, source_target_pairs={{0,4},{4,0},{8,12},{12,8},{16,20},{20,16},{24,28},{28,24},{32,36},... | collective-permute-start | bytes 393224 | tf_op jit(solution)/shard_map/ppermute | solution.py:512
  27.6 2.0 %copy-start.9 = (f32[1,1,2,128,128]{4,3,2,1,0:T(8,128)S(1)}, f32[1,1,2,128,128]{4,3,2,1,0:T(8,128)}, u32[]{:S(2)}) copy-start(f32[1,1,2,128,128]{4,3,2,1,0:T(8,128)} %param.12) | copy-start | bytes 393220
  30.3 12.6 %collective-permute-start.16 = (f32[256,256]{1,0:T(8,128)S(1)}, f32[256,256]{1,0:T(8,128)S(1)}, u32[]{:S(2)}, u32[]{:S(2)}) collective-permute-start(f32[256,256]{1,0:T(8,128)S(1)} %get-tuple-element.95.far_ref), channel_id=1, source_target_pairs={{4,8},{8,4},{12,16},{16,12},{20,24},{24,20},{28,32},{32,28},{36,40... | collective-permute-start | bytes 786440 | tf_op jit(solution)/shard_map/ppermute | solution.py:511
  33.6 9.3 %collective-permute-start.17 = (f32[256,256]{1,0:T(8,128)S(1)}, f32[256,256]{1,0:T(8,128)S(1)}, u32[]{:S(2)}, u32[]{:S(2)}) collective-permute-start(f32[256,256]{1,0:T(8,128)S(1)} %get-tuple-element.96.near_ref), channel_id=1, source_target_pairs={{0,4},{4,0},{8,12},{12,8},{16,20},{20,16},{24,28},{28,24},{32,36},... | collective-permute-start | bytes 786440 | tf_op jit(solution)/shard_map/ppermute | solution.py:512
  44.4 9.7 %collective-permute-start.18 = (f32[128,256]{1,0:T(8,128)S(1)}, f32[128,256]{1,0:T(8,128)S(1)}, u32[]{:S(2)}, u32[]{:S(2)}) collective-permute-start(f32[128,256]{1,0:T(8,128)S(1)} %get-tuple-element.104), channel_id=1, source_target_pairs={{4,8},{8,4},{12,16},{16,12},{20,24},{24,20},{28,32},{32,28},{36,40... | collective-permute-start | bytes 393224 | tf_op jit(solution)/shard_map/ppermute | solution.py:511
  49.1 4.9 %collective-permute-start.19 = (f32[128,256]{1,0:T(8,128)S(1)}, f32[128,256]{1,0:T(8,128)S(1)}, u32[]{:S(2)}, u32[]{:S(2)}) collective-permute-start(f32[128,256]{1,0:T(8,128)S(1)} %get-tuple-element.105), channel_id=1, source_target_pairs={{0,4},{4,0},{8,12},{12,8},{16,20},{20,16},{24,28},{28,24},{32,36},... | collective-permute-start | bytes 393224 | tf_op jit(solution)/shard_map/ppermute | solution.py:512
  54.1 46.0 %copy-start = (f32[1,1,1024,256]{3,2,1,0:T(8,128)S(1)}, f32[1,1,1024,256]{3,2,1,0:T(8,128)}, u32[]{:S(2)}) copy-start(f32[1,1,1024,256]{3,2,1,0:T(8,128)} %param.10) | copy-start | bytes 3145732
  54.1 46.1 %copy-start.4 = (f32[1,1,5,256,256]{4,3,2,1,0:T(8,128)S(1)}, f32[1,1,5,256,256]{4,3,2,1,0:T(8,128)}, u32[]{:S(2)}) copy-start(f32[1,1,5,256,256]{4,3,2,1,0:T(8,128)} %param.13) | copy-start | bytes 3932164
  54.1 46.1 %copy-start.17 = (s32[1,1,256]{2,1,0:T(1,128)S(1)}, s32[1,1,256]{2,1,0:T(1,128)}, u32[]{:S(2)}) copy-start(s32[1,1,256]{2,1,0:T(1,128)} %param.17) | copy-start | bytes 3076
  70.7 28.0 %all-to-all-start.3 = ((f32[16,1,1536]{2,1,0:T(1,128)}), f32[16,1,1536]{2,1,0:T(1,128)S(1)}, u32[]{:S(2)}, u32[]{:S(2)}) async-start(f32[16,1,1536]{2,1,0:T(1,128)} %merge_plane.1), calls=%async_computation.3 | async-start | bytes 196608 | tf_op jit(solution)/shard_map/all_to_all | solution.py:571

commit v6 on v5

--- a/solution.py
+++ b/solution.py
@@ -444,7 +444,7 @@
     return (coeff_one, coeff_two, miss)
 
 
-def judge_kernel(parts_ref, rows_ref, ok_ref):
+def judge_kernel(parts_ref, p_ref, q_ref, out_ref, miss_ref, ok_ref):
     (beta, len_one, len_two), (cos_01, cos_02, cos_12) = merge(unpacked(parts_ref))
     rel_one = len_one / beta
     proj_one = rel_one * cos_01
@@ -458,16 +458,12 @@
     coeff_one, coeff_two, miss = least_squares(beta, proj_one, sub_one, proj_two_a, proj_two_b, sub_two)
     second = coeff_two / sub_one
     first = (coeff_one - second * proj_one) / beta
-    rows_ref[...] = stacked([first, second / beta, miss])
+    miss_ref[...] = miss
+    out_ref[...] = first * p_ref[...] + (second / beta) * q_ref[...]
     good = jnp.where(first * 0.0 + second * 0.0 + miss * 0.0 == 0.0, 1.0, 0.0)
     for a in (beta, len_one, len_two):
         good = jnp.where((a > LEAST) & (a < MOST), good, 0.0)
     ok_ref[0, 0] = jnp.where(jnp.min(good) > 0.0, 1, 0)
-
-
-def combine_kernel(rows_ref, p_ref, q_ref, out_ref, miss_ref):
-    miss_ref[...] = rows_ref[2:3]
-    out_ref[...] = rows_ref[0:1] * p_ref[...] + rows_ref[1:2] * q_ref[...]
 
 
 def shape(*dims, kind=f32):
@@ -569,19 +565,20 @@
     parts = lax.all_to_all(parts, AXES, 0, 0, axis_index_groups=plane)
     parts = call("merge_plane", merge_kernel, shape(len(depth[0]), 1, 6 * ncols), (), (parts,))
     parts = lax.all_to_all(parts, AXES, 0, 0, axis_index_groups=depth)
-    rows, ok = call(
-        "judge", judge_kernel, (shape(8, ncols), shape(1, 1, kind=jnp.int32)), (), (parts,), out_place=(VMEM, SMEM)
-    )
-
-    def combined(rows, p, q, *_):
-        return call("combine", combine_kernel, (shape(nrows, ncols), shape(1, ncols)), (), (rows, p, q))
-
-    def normalised(rows, p, q, *args):
+    answer, miss, ok = call(
+        "judge", judge_kernel, (shape(nrows, ncols), shape(1, ncols), shape(1, 1, kind=jnp.int32)), (),
+        (parts, search_one, search_two), out_place=(VMEM, VMEM, SMEM),
+    )
+
+    def kept(answer, miss, *_):
+        return answer, miss
+
+    def normalised(answer, miss, *args):
         return normalised_solve(*args)
 
     answer, miss = lax.cond(
-        ok[0, 0] == 1, combined, normalised, rows, search_one, search_two, rhs, blocks, coupling, inverse,
-        deflation, counts, panel, intersection_rows,
+        ok[0, 0] == 1, kept, normalised, answer, miss, rhs, blocks, coupling, inverse, deflation, counts, panel,
+        intersection_rows,
     )
     return (answer[None, None], miss[0])
 

time: 104 us -> 102 us (0.981)
  Pallas kernels: 15.7 us -> 13.1 us
    pallas_call x10 -> x9, Pallas kernels: 15.7 us -> 13.1 us  [call(): pl.pallas_call(kernel, out_shape=out_shape, in_specs=[SMEM] * len(scalars...]
  transfers between devices with their start and end apart: 9 -> 9, of which waited for: 1 -> 1; matrix products, arithmetic and copies ran while one was open for 0% -> 0% of each run, Pallas kernels for 5% -> 4%
where the time goes in v6:
time: 102 us; the launch traced here: 101 us
  starting transfers between devices  42.3 us (41%)
  blocking collectives  30.7 us (30%)
  Pallas kernels  13.1 us (13%)
  waiting for transfers between devices  12 us (12%)
  between operations  2.38 us (2%)
    all_to_all x1, starting transfers between devices, body(): parts = lax.all_to_all(parts, AXES, 0, 0, axis_index_groups=depth)  16.3 us
    all_to_all x2, blocking collectives, precond(): coefs = lax.all_to_all(coef, 'blk', 0, 0)  15.5 us
    ppermute x4, starting transfers between devices, halo(): far = lax.ppermute(far, 'sub', far_pairs)  15.4 us
    all_to_all x1, blocking collectives, body(): parts = lax.all_to_all(parts, AXES, 0, 0, axis_index_groups=plane)  15.2 us
    pallas_call x9, Pallas kernels, call(): pl.pallas_call(kernel, out_shape=out_shape, in_specs=[SMEM] * len(scalars...  13.1 us
    all_to_all x1, waiting for transfers between devices, body(): parts = lax.all_to_all(parts, AXES, 0, 0, axis_index_groups=depth)  12 us
    ppermute x4, starting transfers between devices, halo(): return (far, lax.ppermute(near, 'sub', near_pairs))  10.6 us
  transfers between devices with their start and end apart: 9, of which 1 were waited for; matrix products, arithmetic and copies ran while one was open for 0% of the time, Pallas kernels for 4%

profile of v6, /device:TPU:1, one launch (start us, length us, event | category | flops | bytes accessed | tf_op | source)
XLA Modules:
  0.0 100.9 jit_solution(15278161805148657822)
XLA Ops:
  1.3 0.0 copy-start.8
  1.3 2.4 %first_rows.1 = (f32[384,256]{1,0:T(8,128)S(1)}, f32[384,256]{1,0:T(8,128)S(1)}, f32[4,40,256]{2,1,0:T(8,128)S(1)}, f32[1024,256]{1,0:T(8,128)S(1)}, f32[5,256,2...) custom-call(s32[1,1]{1,0:T(1,128)S(6)} %copy.32.count_ref, ...), custom_call_target="tpu_custom_call" | custom-call | flops 300000000 | bytes 2524160 | tf_op jit(solution)/shard_map/first_rows/pallas_call | solution.py:480
  3.7 4.6 %collective-permute-start.12 = (f32[384,256]{1,0:T(8,128)S(1)}, f32[384,256]{1,0:T(8,128)S(1)}, u32[]{:S(2)}, u32[]{:S(2)}) collective-permute-start(f32[384,256]{1,0:T(8,128)S(1)} %get-tuple-element.74.far_ref.far0_ref), channel_id=1, source_target_pairs={{4,8},{8,4},{12,16},{16,12},{20,24},{24,20},{28,32},{32,28},{36,40... | collective-permute-start | bytes 1179656 | tf_op jit(solution)/shard_map/ppermute | solution.py:507
  8.3 4.9 %collective-permute-start.13 = (f32[384,256]{1,0:T(8,128)S(1)}, f32[384,256]{1,0:T(8,128)S(1)}, u32[]{:S(2)}, u32[]{:S(2)}) collective-permute-start(f32[384,256]{1,0:T(8,128)S(1)} %get-tuple-element.75.near_ref.near0_ref), channel_id=1, source_target_pairs={{0,4},{4,0},{8,12},{12,8},{16,20},{20,16},{24,28},{28,24},{32,36},... | collective-permute-start | bytes 1179656 | tf_op jit(solution)/shard_map/ppermute | solution.py:508
  13.2 8.1 %all_to_all.20.all_ref = f32[4,40,256]{2,1,0:T(8,128)S(1)} all-to-all(f32[4,40,256]{2,1,0:T(8,128)S(1)} %get-tuple-element.77), channel_id=1, replica_groups=mesh['sub'=128,'blk'=4] {'blk'}, dimensions={0} | all-to-all | bytes 327680 | tf_op jit(solution)/shard_map/all_to_all | solution.py:511
  21.3 0.0 collective-permute-done.12.gfar_ref.inv_far_ref
  21.3 0.0 collective-permute-done.13.gnear_ref.inv_near_ref
  21.3 0.0 copy-done.8
  21.4 0.0 copy-start.3
  21.4 1.5 %local_solve.2 = (f32[1024,256]{1,0:T(8,128)S(1)}, f32[256,256]{1,0:T(8,128)S(1)}, bf16[128,256]{1,0:T(8,128)(2,1)S(1)}, f32[128,256]{1,0:T(8,128)S(1)}, f32[128,256]{1,0:T(8,128)S(1)}) custom-call(s32[1]{0:T(128)} %bitcast.35.odd_ref, s32[1]{0:T(128)} %bitcast.36.slot_ref, f32[1024,256]{1,0:T(8,128)S(1)} %get-tuple-element.73.r_ref.u0_ref, ...), custom_call_target="tpu_custom_call" | custom-call | flops 1000000000 | bytes 6557696 | tf_op jit(solution)/shard_map/local_solve/pallas_call | solution.py:480
  22.9 2.7 %collective-permute-start.14 = (f32[128,256]{1,0:T(8,128)S(1)}, f32[128,256]{1,0:T(8,128)S(1)}, u32[]{:S(2)}, u32[]{:S(2)}) collective-permute-start(f32[128,256]{1,0:T(8,128)S(1)} %get-tuple-element.88), channel_id=1, source_target_pairs={{4,8},{8,4},{12,16},{16,12},{20,24},{24,20},{28,32},{32,28},{36,40... | collective-permute-start | bytes 393224 | tf_op jit(solution)/shard_map/ppermute | solution.py:507
  25.7 1.9 %collective-permute-start.15 = (f32[128,256]{1,0:T(8,128)S(1)}, f32[128,256]{1,0:T(8,128)S(1)}, u32[]{:S(2)}, u32[]{:S(2)}) collective-permute-start(f32[128,256]{1,0:T(8,128)S(1)} %get-tuple-element.89), channel_id=1, source_target_pairs={{0,4},{4,0},{8,12},{12,8},{16,20},{20,16},{24,28},{28,24},{32,36},... | collective-permute-start | bytes 393224 | tf_op jit(solution)/shard_map/ppermute | solution.py:508
  27.6 0.0 copy-done.3
  27.6 0.0 copy-start.7
  27.6 1.9 %block_product.1 = (f32[1024,256]{1,0:T(8,128)S(1)}, f32[1024,256]{1,0:T(8,128)S(1)}, f32[256,256]{1,0:T(8,128)S(1)}, f32[48,256]{1,0:T(8,128)S(1)}) custom-call(f32[1024,256]{1,0:T(8,128)S(1)} %get-tuple-element.80.own_ref, f32[256,256]{1,0:T(8,128)S(1)} %get-tuple-element.81.back_ref, bf16[128,256]{1,0:T(8,128)(2,1)S(1)} %get-tuple-element.82.coarse_ref, ...), custom_call_target="tpu_custom_call" | custom-call | flops 1000000000 | bytes 5505024 | tf_op jit(solution)/shard_map/block_product/pallas_call | solution.py:480
  29.5 0.0 collective-permute-done.14.gfar_ref
  29.5 0.0 collective-permute-done.15.gnear_ref
  29.5 0.0 copy-done.7
  29.5 0.8 image.1
  30.3 3.3 %collective-permute-start.16 = (f32[256,256]{1,0:T(8,128)S(1)}, f32[256,256]{1,0:T(8,128)S(1)}, u32[]{:S(2)}, u32[]{:S(2)}) collective-permute-start(f32[256,256]{1,0:T(8,128)S(1)} %get-tuple-element.91.far_ref), channel_id=1, source_target_pairs={{4,8},{8,4},{12,16},{16,12},{20,24},{24,20},{28,32},{32,28},{36,40... | collective-permute-start | bytes 786440 | tf_op jit(solution)/shard_map/ppermute | solution.py:507
  33.6 1.9 %collective-permute-start.17 = (f32[256,256]{1,0:T(8,128)S(1)}, f32[256,256]{1,0:T(8,128)S(1)}, u32[]{:S(2)}, u32[]{:S(2)}) collective-permute-start(f32[256,256]{1,0:T(8,128)S(1)} %get-tuple-element.92.near_ref), channel_id=1, source_target_pairs={{0,4},{4,0},{8,12},{12,8},{16,20},{20,16},{24,28},{28,24},{32,36},... | collective-permute-start | bytes 786440 | tf_op jit(solution)/shard_map/ppermute | solution.py:508
  35.6 7.4 %all_to_all.21.all_ref = f32[4,40,256]{2,1,0:T(8,128)S(1)} all-to-all(f32[4,40,256]{2,1,0:T(8,128)S(1)} %get-tuple-element.93), channel_id=1, replica_groups=mesh['sub'=128,'blk'=4] {'blk'}, dimensions={0} | all-to-all | bytes 327680 | tf_op jit(solution)/shard_map/all_to_all | solution.py:511
  42.9 0.0 collective-permute-done.16.gfar_ref
  42.9 0.0 collective-permute-done.17.gnear_ref
  42.9 1.5 %local_solve.3 = (f32[1024,256]{1,0:T(8,128)S(1)}, f32[256,256]{1,0:T(8,128)S(1)}, bf16[128,256]{1,0:T(8,128)(2,1)S(1)}, f32[128,256]{1,0:T(8,128)S(1)}, f32[128,256]{1,0:T(8,128)S(1)}) custom-call(s32[1]{0:T(128)} %bitcast.35.odd_ref, s32[1]{0:T(128)} %bitcast.36.slot_ref, f32[1024,256]{1,0:T(8,128)S(1)} %get-tuple-element.90.r_ref.u1_ref, ...), custom_call_target="tpu_custom_call" | custom-call | flops 1000000000 | bytes 6033408 | tf_op jit(solution)/shard_map/local_solve/pallas_call | solution.py:480
  44.5 4.7 %collective-permute-start.18 = (f32[128,256]{1,0:T(8,128)S(1)}, f32[128,256]{1,0:T(8,128)S(1)}, u32[]{:S(2)}, u32[]{:S(2)}) collective-permute-start(f32[128,256]{1,0:T(8,128)S(1)} %get-tuple-element.100), channel_id=1, source_target_pairs={{4,8},{8,4},{12,16},{16,12},{20,24},{24,20},{28,32},{32,28},{36,40... | collective-permute-start | bytes 393224 | tf_op jit(solution)/shard_map/ppermute | solution.py:507
  49.2 1.9 %collective-permute-start.19 = (f32[128,256]{1,0:T(8,128)S(1)}, f32[128,256]{1,0:T(8,128)S(1)}, u32[]{:S(2)}, u32[]{:S(2)}) collective-permute-start(f32[128,256]{1,0:T(8,128)S(1)} %get-tuple-element.101), channel_id=1, source_target_pairs={{0,4},{4,0},{8,12},{12,8},{16,20},{20,16},{24,28},{28,24},{32,36},... | collective-permute-start | bytes 393224 | tf_op jit(solution)/shard_map/ppermute | solution.py:508
  51.1 2.4 %last_block_product.1 = (f32[1024,256]{1,0:T(8,128)S(1)}, f32[256,256]{1,0:T(8,128)S(1)}, f32[256,256]{1,0:T(8,128)S(1)}, f32[256,256]{1,0:T(8,128)S(1)}, f32[8,256]{1,0:T(8,128)S(1)}) custom-call(f32[1024,256]{1,0:T(8,128)S(1)} %get-tuple-element.94.own_ref, f32[256,256]{1,0:T(8,128)S(1)} %get-tuple-element.95.back_ref, ...), custom_call_target="tpu_custom_call" | custom-call | flops 1000000000 | bytes 9175040 | tf_op jit(solution)/shard_map/last_block_product/pallas_call | solution.py:480
  53.6 0.0 collective-permute-done.18.gfar_ref
  53.6 0.0 collective-permute-done.19.gnear_ref
  53.6 0.4 lengths_cosines.1
  54.0 15.2 %all_to_all.22.parts_ref = f32[32,1,1536]{2,1,0:T(1,128)S(1)} all-to-all(f32[32,1,1536]{2,1,0:T(1,128)S(1)} %lengths_cosines.1), channel_id=1, replica_groups={{0,1,2,3,4,5,6,7,8,9,10,11,12,13,14,15,16,17,18,19,20,21,22,23,24,25,26..., dimensions={0} | all-to-all | bytes 393216 | tf_op jit(solution)/shard_map/all_to_all | solution.py:565
  69.3 0.0 copy-start
  69.3 0.0 copy-start.6
  69.3 0.0 copy-start.9
  69.3 0.8 merge_plane.1
  70.1 16.3 %all-to-all-start.3 = ((f32[16,1,1536]{2,1,0:T(1,128)}), f32[16,1,1536]{2,1,0:T(1,128)S(1)}, u32[]{:S(2)}, u32[]{:S(2)}) async-start(f32[16,1,1536]{2,1,0:T(1,128)} %merge_plane.1), calls=%async_computation.3 | async-start | bytes 196608 | tf_op jit(solution)/shard_map/all_to_all | solution.py:567
  86.4 12.0 %all-to-all-done.3.parts_ref = f32[16,1,1536]{2,1,0:T(1,128)S(1)} async-done(((f32[16,1,1536]{2,1,0:T(1,128)}), f32[16,1,1536]{2,1,0:T(1,128)S(1)}, u32[]{:S(2)}, u32[]{:S(2)}) %all-to-all-start.3) | async-done | bytes 98336 | tf_op jit(solution)/shard_map/all_to_all | solution.py:567
  98.4 1.3 %judge.1 = (f32[1024,256]{1,0:T(8,128)}, f32[1,256]{1,0:T(1,128)}, s32[1,1]{1,0:T(1,128)}) custom-call(f32[16,1,1536]{2,1,0:T(1,128)S(1)} %all-to-all-done.3.parts_ref, f32[1024,256]{1,0:T(8,128)S(1)} %get-tuple-element.105.p_ref, f32[1024,256]{1,0:T(8,128)S(1)} %get-tuple-element.106.q_ref), custom_call_target="tpu_custom_call" | custom-call | bytes 2195456 | tf_op jit(solution)/shard_map/judge/pallas_call | solution.py:480
  100.4 0.0 copy-done
  100.4 0.0 copy-done.6
  100.4 0.0 copy-done.9
  100.5 0.2 conditional.1
Async XLA Ops:
  1.3 20.1 %copy-start.8 = (f32[1,160,160]{2,1,0:T(8,128)S(1)}, f32[1,160,160]{2,1,0:T(8,128)}, u32[]{:S(2)}) copy-start(f32[1,160,160]{2,1,0:T(8,128)} %param.16) | copy-start | bytes 307204
  3.7 17.6 %collective-permute-start.12 = (f32[384,256]{1,0:T(8,128)S(1)}, f32[384,256]{1,0:T(8,128)S(1)}, u32[]{:S(2)}, u32[]{:S(2)}) collective-permute-start(f32[384,256]{1,0:T(8,128)S(1)} %get-tuple-element.74.far_ref.far0_ref), channel_id=1, source_target_pairs={{4,8},{8,4},{12,16},{16,12},{20,24},{24,20},{28,32},{32,28},{36,40... | collective-permute-start | bytes 1179656 | tf_op jit(solution)/shard_map/ppermute | solution.py:507
  8.3 13.0 %collective-permute-start.13 = (f32[384,256]{1,0:T(8,128)S(1)}, f32[384,256]{1,0:T(8,128)S(1)}, u32[]{:S(2)}, u32[]{:S(2)}) collective-permute-start(f32[384,256]{1,0:T(8,128)S(1)} %get-tuple-element.75.near_ref.near0_ref), channel_id=1, source_target_pairs={{0,4},{4,0},{8,12},{12,8},{16,20},{20,16},{24,28},{28,24},{32,36},... | collective-permute-start | bytes 1179656 | tf_op jit(solution)/shard_map/ppermute | solution.py:508
  21.4 6.3 %copy-start.3 = (f32[1,1,4,256,256]{4,3,2,1,0:T(8,128)S(1)}, f32[1,1,4,256,256]{4,3,2,1,0:T(8,128)}, u32[]{:S(2)}) copy-start(f32[1,1,4,256,256]{4,3,2,1,0:T(8,128)} %param.11) | copy-start | bytes 3145732
  22.9 6.6 %collective-permute-start.14 = (f32[128,256]{1,0:T(8,128)S(1)}, f32[128,256]{1,0:T(8,128)S(1)}, u32[]{:S(2)}, u32[]{:S(2)}) collective-permute-start(f32[128,256]{1,0:T(8,128)S(1)} %get-tuple-element.88), channel_id=1, source_target_pairs={{4,8},{8,4},{12,16},{16,12},{20,24},{24,20},{28,32},{32,28},{36,40... | collective-permute-start | bytes 393224 | tf_op jit(solution)/shard_map/ppermute | solution.py:507
  25.7 3.9 %collective-permute-start.15 = (f32[128,256]{1,0:T(8,128)S(1)}, f32[128,256]{1,0:T(8,128)S(1)}, u32[]{:S(2)}, u32[]{:S(2)}) collective-permute-start(f32[128,256]{1,0:T(8,128)S(1)} %get-tuple-element.89), channel_id=1, source_target_pairs={{0,4},{4,0},{8,12},{12,8},{16,20},{20,16},{24,28},{28,24},{32,36},... | collective-permute-start | bytes 393224 | tf_op jit(solution)/shard_map/ppermute | solution.py:508
  27.6 1.9 %copy-start.7 = (f32[1,1,2,128,128]{4,3,2,1,0:T(8,128)S(1)}, f32[1,1,2,128,128]{4,3,2,1,0:T(8,128)}, u32[]{:S(2)}) copy-start(f32[1,1,2,128,128]{4,3,2,1,0:T(8,128)} %param.12) | copy-start | bytes 393220
  30.3 12.6 %collective-permute-start.16 = (f32[256,256]{1,0:T(8,128)S(1)}, f32[256,256]{1,0:T(8,128)S(1)}, u32[]{:S(2)}, u32[]{:S(2)}) collective-permute-start(f32[256,256]{1,0:T(8,128)S(1)} %get-tuple-element.91.far_ref), channel_id=1, source_target_pairs={{4,8},{8,4},{12,16},{16,12},{20,24},{24,20},{28,32},{32,28},{36,40... | collective-permute-start | bytes 786440 | tf_op jit(solution)/shard_map/ppermute | solution.py:507
  33.6 9.3 %collective-permute-start.17 = (f32[256,256]{1,0:T(8,128)S(1)}, f32[256,256]{1,0:T(8,128)S(1)}, u32[]{:S(2)}, u32[]{:S(2)}) collective-permute-start(f32[256,256]{1,0:T(8,128)S(1)} %get-tuple-element.92.near_ref), channel_id=1, source_target_pairs={{0,4},{4,0},{8,12},{12,8},{16,20},{20,16},{24,28},{28,24},{32,36},... | collective-permute-start | bytes 786440 | tf_op jit(solution)/shard_map/ppermute | solution.py:508
  44.5 9.1 %collective-permute-start.18 = (f32[128,256]{1,0:T(8,128)S(1)}, f32[128,256]{1,0:T(8,128)S(1)}, u32[]{:S(2)}, u32[]{:S(2)}) collective-permute-start(f32[128,256]{1,0:T(8,128)S(1)} %get-tuple-element.100), channel_id=1, source_target_pairs={{4,8},{8,4},{12,16},{16,12},{20,24},{24,20},{28,32},{32,28},{36,40... | collective-permute-start | bytes 393224 | tf_op jit(solution)/shard_map/ppermute | solution.py:507
  49.2 4.4 %collective-permute-start.19 = (f32[128,256]{1,0:T(8,128)S(1)}, f32[128,256]{1,0:T(8,128)S(1)}, u32[]{:S(2)}, u32[]{:S(2)}) collective-permute-start(f32[128,256]{1,0:T(8,128)S(1)} %get-tuple-element.101), channel_id=1, source_target_pairs={{0,4},{4,0},{8,12},{12,8},{16,20},{20,16},{24,28},{28,24},{32,36},... | collective-permute-start | bytes 393224 | tf_op jit(solution)/shard_map/ppermute | solution.py:508
  69.3 31.2 %copy-start = (f32[1,1,1024,256]{3,2,1,0:T(8,128)S(1)}, f32[1,1,1024,256]{3,2,1,0:T(8,128)}, u32[]{:S(2)}) copy-start(f32[1,1,1024,256]{3,2,1,0:T(8,128)} %param.10) | copy-start | bytes 3145732
  69.3 31.2 %copy-start.6 = (f32[1,1,40,1024]{3,2,1,0:T(8,128)S(1)}, f32[1,1,40,1024]{3,2,1,0:T(8,128)}, u32[]{:S(2)}) copy-start(f32[1,1,40,1024]{3,2,1,0:T(8,128)} %param.14) | copy-start | bytes 491524
  69.3 31.2 %copy-start.9 = (s32[1,1,256]{2,1,0:T(1,128)S(1)}, s32[1,1,256]{2,1,0:T(1,128)}, u32[]{:S(2)}) copy-start(s32[1,1,256]{2,1,0:T(1,128)} %param.17) | copy-start | bytes 3076
  70.1 28.3 %all-to-all-start.3 = ((f32[16,1,1536]{2,1,0:T(1,128)}), f32[16,1,1536]{2,1,0:T(1,128)S(1)}, u32[]{:S(2)}, u32[]{:S(2)}) async-start(f32[16,1,1536]{2,1,0:T(1,128)} %merge_plane.1), calls=%async_computation.3 | async-start | bytes 196608 | tf_op jit(solution)/shard_map/all_to_all | solution.py:567
